TPU v7x, 256 devices: a whole 4x4x8 slice. The times are simulated.
256 devices in a mesh: dp: 64 (over x, z_lo, y, core), mp: 4 (over z_hi).
Axes of the slice: x: 4, y: 4, z: 8 (z_hi: 4, z_lo: 2; z = z_hi * 2 + z_lo), core: 2. Of those that a mesh axis runs over, the one named last changes fastest.
Arguments:
- query: bfloat16 [16384, 2560], P('dp', 'mp'), may hold values from -6 to 6
- key: bfloat16 [16384, 2560], P('dp', 'mp'), may hold values from -6 to 6
- value: bfloat16 [16384, 2560], P('dp', 'mp'), may hold values from -6 to 6
- residual: bfloat16 [16384, 5120], P(('dp', 'mp')), may hold values from -6 to 6
- cotangent: bfloat16 [16384, 5120], P(('dp', 'mp')), may hold values from -48 to 48
- out_weight: bfloat16 [5120, 2560], P('dp', 'mp'), may hold values from -1 to 1
- norm_gain: float32 [5120], replicated, may hold values from 0.1 to 1.9
- doc_ids: int32 [16384], P('dp'), may hold values from 0 to 1, as said below
Outputs:
- grad_query: bfloat16 [16384, 2560], P('dp', 'mp')
- grad_key: bfloat16 [16384, 2560], P('dp', 'mp')
- grad_value: bfloat16 [16384, 2560], P('dp', 'mp')
- grad_residual: bfloat16 [16384, 5120], P(('dp', 'mp'))
- grad_out_weight: float32 [5120, 2560], P('dp', 'mp')
- grad_gain: float32 [5120], P('dp')
Inputs may be any that keep to these rules, and one draw needn't show every extreme that they name: `doc_ids`: within each sequence of 256 tokens the document numbers start at 0, never fall and rise by one at each new document; every sequence holds exactly 2 documents, each starting at a position that is a multiple of 8 within its sequence.
All inputs are finite; a program needn't handle non-finite values.
Results may differ from a plain program's by a relative error of at most 0.023.
Values may be sent and summed in bfloat16 or wider, within the bound.
No kernel may reach another device: no remote copies, remote signals or barrier semaphores. Data moves between devices by JAX's collectives and lax.ppermute only.
A program may use at most 128 MiB of HBM per device.

v0:
```python
import math

import jax
import jax.numpy as jnp
from jax import lax
from jax.sharding import PartitionSpec as P

HD = 128


def attention_probs(query3, key3, doc_ids):
    seq = query3.shape[0]
    scale = 1.0 / math.sqrt(HD)
    scores = jnp.einsum("thd,shd->hts", query3, key3, preferred_element_type=jnp.float32) * scale
    pos = lax.iota(jnp.int32, seq)
    allowed = (pos[None, :] <= pos[:, None]) & (doc_ids[None, :] == doc_ids[:, None])
    scores = jnp.where(allowed[None], scores, -1e30)
    top = jnp.max(scores, axis=2, keepdims=True)
    weights = jnp.exp(scores - top)
    return weights / jnp.sum(weights, axis=2, keepdims=True)


def project_rows(attended, weight_full):
    return lax.dot_general(
        attended, weight_full, (((1,), (1,)), ((), ())), preferred_element_type=jnp.float32
    )


def norm_backward(mixed, cotangent, norm_gain):
    inv = lax.rsqrt(jnp.mean(mixed * mixed, axis=1, keepdims=True) + 1e-05)
    cot_f = cotangent.astype(jnp.float32)
    gscaled = cot_f * norm_gain
    grad_h = inv * (gscaled - mixed * inv * inv * jnp.mean(gscaled * mixed, axis=1, keepdims=True))
    return (grad_h.astype(jnp.bfloat16), cot_f * mixed * inv)


def on_device(query, key, value, residual, cotangent, out_weight, norm_gain, doc_ids):
    seq, width = query.shape
    heads = width // HD
    n_dp = lax.axis_size("dp")
    scale = 1.0 / math.sqrt(HD)
    query3 = query.reshape(seq, heads, HD)
    key3 = key.reshape(seq, heads, HD)
    value3 = value.reshape(seq, heads, HD)
    probs = attention_probs(query3, key3, doc_ids)
    probs_b = probs.astype(jnp.bfloat16)
    attended = jnp.einsum("hts,shd->thd", probs_b, value3, preferred_element_type=jnp.float32)
    attended = attended.astype(jnp.bfloat16).reshape(seq, width)
    weight_full = lax.all_gather(out_weight, "dp", axis=0, tiled=True)
    branch = lax.psum_scatter(
        project_rows(attended, weight_full).astype(jnp.bfloat16),
        "mp",
        scatter_dimension=0,
        tiled=True,
    ).astype(jnp.float32)
    mixed = residual.astype(jnp.float32) + branch
    grad_residual, stat_rows = norm_backward(mixed, cotangent, norm_gain)
    gain_term = jnp.sum(stat_rows, axis=0)
    grad_rows = lax.all_gather(grad_residual, "mp", axis=0, tiled=True)
    token_dims = (((0,), (0,)), ((), ()))
    piece = out_weight.shape[0]
    grad_weight = lax.psum_scatter(
        lax.dot_general(grad_rows, attended, token_dims, preferred_element_type=jnp.float32) / n_dp,
        "dp",
        scatter_dimension=0,
        tiled=True,
    )
    total = lax.psum(gain_term / n_dp, ("dp", "mp"))
    grad_gain = lax.dynamic_slice_in_dim(total, lax.axis_index("dp") * piece, piece, 0)
    grad_attended = jnp.dot(grad_rows, weight_full, preferred_element_type=jnp.float32).astype(
        jnp.bfloat16
    )
    grad3 = grad_attended.reshape(seq, heads, HD)
    grad_value = jnp.einsum("hts,thd->shd", probs_b, grad3, preferred_element_type=jnp.float32)
    grad_value = grad_value.astype(jnp.bfloat16).reshape(seq, width)
    grad_probs = jnp.einsum("thd,shd->hts", grad3, value3, preferred_element_type=jnp.float32)
    delta = jnp.sum(probs * grad_probs, axis=2, keepdims=True)
    grad_scores = (probs * (grad_probs - delta)).astype(jnp.bfloat16)
    grad_query = (
        jnp.einsum("hts,shd->thd", grad_scores, key3, preferred_element_type=jnp.float32) * scale
    )
    grad_key = (
        jnp.einsum("hts,thd->shd", grad_scores, query3, preferred_element_type=jnp.float32) * scale
    )
    grad_query = grad_query.astype(jnp.bfloat16).reshape(seq, width)
    grad_key = grad_key.astype(jnp.bfloat16).reshape(seq, width)
    return (grad_query, grad_key, grad_value, grad_residual, grad_weight, grad_gain)


def solution(mesh):
    placed = (
        P("dp", "mp"),
        P("dp", "mp"),
        P("dp", "mp"),
        P(("dp", "mp"), None),
        P(("dp", "mp"), None),
        P("dp", "mp"),
        P(),
        P("dp"),
    )
    return jax.shard_map(
        on_device,
        mesh=mesh,
        in_specs=placed,
        out_specs=(
            P("dp", "mp"),
            P("dp", "mp"),
            P("dp", "mp"),
            P(("dp", "mp"), None),
            P("dp", "mp"),
            P("dp"),
        ),
        check_vma=False,
    )
```

profile of v0, /device:TPU:1, one launch (start us, length us, event | category | flops | bytes accessed | tf_op | source)
XLA Modules:
  0.0 569.8 jit_solution(4263108972658069682)
XLA Ops:
  7.2 0.7 all-gather.3.cloned.1.call-update
  7.9 0.0 reduce-scatter.3.cloned.1.call-start
  8.0 1.1 copy.29
  9.1 1.1 copy.30
  10.3 0.2 copy.33
  10.5 0.1 fusion.15
  10.6 0.6 fusion.19
  11.2 0.3 convolution_convert_fusion.1
  11.5 0.8 copy-done.4
  12.3 113.4 %all-gather.3.cloned.1.call-done = bf16[5120,640]{1,0:T(8,128)(2,1)} async-done(((bf16[80,640]{1,0:T(8,128)(2,1)}), bf16[5120,640]{1,0:T(8,128)(2,1)}) %all-gather.3.cloned.1.call-update) | async-done | bytes 6553616 | tf_op jit(solution)/shard_map/all_gather | solution.py:49
  125.7 6.6 %convolution_convert_fusion = bf16[256,5120]{1,0:T(8,128)(2,1)} fusion(bf16[256,640]{0,1:T(8,128)(2,1)S(1)} %bitcast.43, bf16[5120,640]{1,0:T(8,128)(2,1)} %all-gather.3.cloned.1.call-done), kind=kOutput, calls=%fused_computation.2 | convolution fusion | flops 1679032320 | bytes 9502720 | tf_op jit(solution)/shard_map/dot_general | solution.py:24
  132.3 0.0 all-gather.5.cloned.1.call-start
  132.4 57.5 %reduce-scatter.3.cloned.1.call-done = bf16[64,5120]{1,0:T(8,128)(2,1)} async-done(((bf16[256,5120]{1,0:T(8,128)(2,1)}), bf16[64,5120]{1,0:T(8,128)(2,1)}) %reduce-scatter.3.cloned.1.call-update) | async-done | bytes 655376 | tf_op jit(solution)/shard_map/reduce_scatter | solution.py:50
  189.9 1.5 multiply_reduce_fusion.1
  191.4 0.6 fusion.10
  192.0 1.3 fusion.8
  193.3 0.0 reduce-scatter.5.cloned.1.call-start
  193.4 58.9 %all-gather.5.cloned.1.call-done = bf16[256,5120]{1,0:T(8,128)(2,1)} async-done(((bf16[64,5120]{1,0:T(8,128)(2,1)}), bf16[256,5120]{1,0:T(8,128)(2,1)}) %all-gather.5.cloned.1.call-update) | async-done | bytes 2621456 | tf_op jit(solution)/shard_map/all_gather | solution.py:59
  252.3 8.7 %convolution_multiply_fusion = f32[5120,640]{1,0:T(8,128)} fusion(bf16[256,5120]{1,0:T(8,128)(2,1)} %all-gather.5.cloned.1.call-done, bf16[256,640]{0,1:T(8,128)(2,1)S(1)} %bitcast.44), kind=kOutput, calls=%fused_computation.1 | convolution fusion | flops 1680998400 | bytes 16056320 | tf_op jit(solution)/shard_map/dot_general | solution.py:63
  261.0 77.7 %psum.7 = f32[5120]{0:T(1024)S(1)} all-reduce(f32[5120]{0:T(1024)S(1)} %broadcast_multiply_fusion), channel_id=1, replica_groups=mesh['dp'=64,'mp'=4] {'dp','mp'}, use_global_device_ids=true, to_apply=%region_8.9 | all-reduce | flops 5120 | bytes 40960 | tf_op jit(solution)/shard_map/psum | solution.py:68
  338.7 0.6 dynamic_slice.3
  339.2 5.8 %convolution_convert_fusion.3 = bf16[256,640]{1,0:T(8,128)(2,1)} fusion(bf16[256,5120]{1,0:T(8,128)(2,1)S(1)} %copy-done.2, bf16[5120,640]{1,0:T(8,128)(2,1)} %all-gather.3.cloned.1.call-done), kind=kOutput, calls=%fused_computation.26 | convolution fusion | flops 1677885440 | bytes 9502720 | tf_op jit(solution)/shard_map/dot_general | solution.py:70
  345.0 1.1 copy.35
  346.2 1.8 convolution_convert_fusion.2
  348.0 0.9 copy.43
  348.9 0.4 multiply_reduce_fusion
  349.3 0.2 multiply_convert_fusion
  349.6 0.3 fusion.12
  349.8 0.9 copy.41
  350.7 0.4 fusion.11
  351.1 0.9 copy.42
  352.0 211.3 %reduce-scatter.5.cloned.1.call-done = f32[80,640]{1,0:T(8,128)} async-done(((f32[5120,640]{1,0:T(8,128)}), f32[80,640]{1,0:T(8,128)}) %reduce-scatter.5.cloned.1.call-update) | async-done | bytes 204816 | tf_op jit(solution)/shard_map/reduce_scatter | solution.py:62
  (28 shorter events, 0.2 us)
Async XLA Ops:
  7.2 3.1 copy-start.6
  7.2 3.3 copy-start.10
  7.2 118.5 %all-gather.3.cloned.1.call-start = ((), (), s32[]{:S(2)}) async-start(), calls=%async_computation.2 | async-start | bytes 6656000 | tf_op jit(solution)/shard_map/all_gather | solution.py:49
  7.9 182.0 %reduce-scatter.3.cloned.1.call-start = ((), (), s32[]{:S(2)}) async-start(), calls=%async_computation.3 | async-start | bytes 3276800 | tf_op jit(solution)/shard_map/reduce_scatter | solution.py:50
  10.5 0.8 copy-start.7
  11.2 1.1 copy-start.4
  132.3 57.6 %copy-start = (bf16[64,5120]{1,0:T(8,128)(2,1)S(1)}, bf16[64,5120]{1,0:T(8,128)(2,1)}, u32[]{:S(2)}) copy-start(bf16[64,5120]{1,0:T(8,128)(2,1)} %param.11) | copy-start | bytes 1966084
  132.3 59.1 %copy-start.9 = (f32[5120]{0:T(1024)S(1)}, f32[5120]{0:T(1024)}, u32[]{:S(2)}) copy-start(f32[5120]{0:T(1024)} %param.14) | copy-start | bytes 61444
  132.3 59.1 %copy-start.3 = (bf16[64,5120]{1,0:T(8,128)(2,1)S(1)}, bf16[64,5120]{1,0:T(8,128)(2,1)}, u32[]{:S(2)}) copy-start(bf16[64,5120]{1,0:T(8,128)(2,1)} %param.12) | copy-start | bytes 1966084
  132.3 119.9 %all-gather.5.cloned.1.call-start = ((), (), s32[]{:S(2)}) async-start(), calls=%async_computation.4 | async-start | bytes 3276800 | tf_op jit(solution)/shard_map/all_gather | solution.py:59
  189.9 1.5 copy-start.1
  193.3 370.0 %reduce-scatter.5.cloned.1.call-start = ((), (), s32[]{:S(2)}) async-start(), calls=%async_computation.5 | async-start | bytes 13312000 | tf_op jit(solution)/shard_map/reduce_scatter | solution.py:62
  260.9 78.3 %copy-start.2 = (bf16[256,5120]{1,0:T(8,128)(2,1)S(1)}, bf16[256,5120]{1,0:T(8,128)(2,1)}, u32[]{:S(2)}) copy-start(bf16[256,5120]{1,0:T(8,128)(2,1)} %all-gather.5.cloned.1.call-done) | copy-start | bytes 7864324
  346.2 2.8 copy-start.5
  346.2 2.7 copy-start.8
Sparse Core Ops, SparseCore 0:
  9.9 115.7 all-gather.2
  132.5 57.3 reduce-scatter.2
  193.5 58.7 all-gather.4
  261.1 302.1 reduce-scatter.4
where the time goes:
time: 573 us; the launch traced here: 570 us
  waiting for transfers between devices  442 us (77%)
  blocking collectives  77.7 us (14%)
  matrix products  24.8 us (4%)
  between operations  14 us (2%)
  local copies, waits for them, and re-layouts  7.76 us (1%)
    reduce_scatter x1, waiting for transfers between devices, on_device(): lax.psum_scatter(lax.dot_general(grad_rows, attended, token_dims, preferr...  211 us
    all_gather x1, waiting for transfers between devices, on_device(): weight_full = lax.all_gather(out_weight, 'dp', axis=0, tiled=True)  113 us
    psum x1, blocking collectives, on_device(): total = lax.psum(gain_term / n_dp, ('dp', 'mp'))  77.7 us
    all_gather x1, waiting for transfers between devices, on_device(): grad_rows = lax.all_gather(grad_residual, 'mp', axis=0, tiled=True)  58.9 us
    reduce_scatter x1, waiting for transfers between devices, on_device(): lax.psum_scatter(project_rows(attended, weight_full).astype(jnp.bfloat16)...  57.5 us
  transfers between devices with their start and end apart: 4, of which 4 were waited for; matrix products, arithmetic and copies ran while one was open for 3% of the time, Pallas kernels for 0%

commit v1 on v0

v1 whole, which is shorter than its diff:
```python
import math

import jax
import jax.numpy as jnp
from jax import lax
from jax.experimental import pallas as pl
from jax.experimental.pallas import tpu as pltpu
from jax.sharding import PartitionSpec as P

HD = 128
BF = jnp.bfloat16
F32 = jnp.float32
GROUPS = ((0,), (1,), (2,), (3,))
VMEM_LIMIT = 40 * 1024 * 1024


def dp_perm(dx=0, dy=0, flip_w=False, flip_c=False):
    pairs = []
    for i in range(64):
        c, y, w, x = i % 2, i // 2 % 4, i // 8 % 2, i // 16
        w, c = w ^ flip_w, c ^ flip_c
        x, y = (x + dx) % 4, (y + dy) % 4
        pairs.append((i, ((x * 2 + w) * 4 + y) * 2 + c))
    return pairs


def send_dp(value, **step):
    return lax.ppermute(value, "dp", dp_perm(**step))


def send_mp(value, step):
    return lax.ppermute(value, "mp", [(i, (i + step) % 4) for i in range(4)])


def attention_probs(query3, key3, doc_ids):
    seq = query3.shape[0]
    scale = 1.0 / math.sqrt(HD)
    scores = jnp.einsum("thd,shd->hts", query3, key3, preferred_element_type=F32) * scale
    pos = lax.iota(jnp.int32, seq)
    allowed = (pos[None, :] <= pos[:, None]) & (doc_ids[None, :] == doc_ids[:, None])
    scores = jnp.where(allowed[None], scores, -1e30)
    top = jnp.max(scores, axis=2, keepdims=True)
    weights = jnp.exp(scores - top)
    return weights / jnp.sum(weights, axis=2, keepdims=True)


def turn_tokens(pos, att_ref, att_s):
    rows = att_ref.shape[0] // 4
    for k in range(4):
        start = pl.multiple_of(((pos[2] + k) % 4) * rows, 16)
        att_s[pl.ds(k * rows, rows), :] = att_ref[pl.ds(start, rows), :]


def branch_kernel(pos, att_ref, cat_ref, oth_ref, w_ref, p0, p1, p2a, p2b, p3, att_s):
    _, nj, _, piece, _ = cat_ref.shape
    y, c = pos[0], pos[1]
    turn_tokens(pos, att_ref, att_s)
    rows = att_ref.shape[0] // 4
    half = rows // 2
    span = 16 * piece
    for j in range(nj):
        for w in range(2):
            for k in range(4):
                base = ((j * 2 + w) * 4 + (y + k) % 4) * 2
                mine = pl.multiple_of((base + c) * piece, 16)
                other = pl.multiple_of((base + 1 - c) * piece, 16)
                w_ref[pl.ds(mine, piece), :] = cat_ref[k, j, w]
                w_ref[pl.ds(other, piece), :] = oth_ref[k, j, w]
        cols = pl.ds(j * span, span)
        prod = lax.dot_general(
            att_s[...], w_ref[cols, :], (((1,), (1,)), ((), ())), preferred_element_type=F32
        ).astype(BF)
        p0[:, cols] = prod[:rows]
        p1[:, cols] = prod[rows : 2 * rows]
        p2a[:, cols] = prod[2 * rows : 2 * rows + half]
        p2b[:, cols] = prod[2 * rows + half : 3 * rows]
        p3[:, cols] = prod[3 * rows :]


def branch_part(pos, attended, cat, oth):
    _, nj, _, piece, width = cat.shape
    seq = attended.shape[0]
    rows, span = seq // 4, nj * 16 * piece
    sds = jax.ShapeDtypeStruct
    vm = pl.BlockSpec(memory_space=pltpu.VMEM)
    return pl.pallas_call(
        branch_kernel,
        in_specs=[pl.BlockSpec(memory_space=pltpu.SMEM), vm, vm, vm],
        out_specs=[vm] * 6,
        out_shape=[
            sds((span, width), BF),
            sds((rows, span), BF),
            sds((rows, span), BF),
            sds((rows // 2, span), BF),
            sds((rows // 2, span), BF),
            sds((rows, span), BF),
        ],
        scratch_shapes=[pltpu.VMEM((seq, width), BF)],
        compiler_params=pltpu.CompilerParams(vmem_limit_bytes=VMEM_LIMIT),
        cost_estimate=pl.CostEstimate(
            flops=2 * seq * width * span,
            bytes_accessed=2 * (3 * span * width + seq * span),
            transcendentals=0,
        ),
        name="branch_part",
    )(pos, attended, cat, oth)


def grads_kernel(pos, g0, gp, ga, gb, gm, att_ref, w_ref, acc_ref, keep, send, acc_out, att_s, rows_s):
    _, nj, _, piece, _ = keep.shape
    y, c = pos[0], pos[1]
    turn_tokens(pos, att_ref, att_s)
    rows = g0.shape[0]
    half = rows // 2
    span = 16 * piece
    rows_s[pl.ds(0, rows), :] = g0[...]
    rows_s[pl.ds(rows, rows), :] = gp[...]
    rows_s[pl.ds(2 * rows, half), :] = ga[...]
    rows_s[pl.ds(2 * rows + half, half), :] = gb[...]
    rows_s[pl.ds(3 * rows, rows), :] = gm[...]
    acc = acc_ref[...]
    for j in range(nj):
        cols = pl.ds(j * span, span)
        acc = acc + jnp.dot(rows_s[:, cols], w_ref[cols, :], preferred_element_type=F32)
        prod = lax.dot_general(
            rows_s[:, cols], att_s[...], (((0,), (0,)), ((), ())), preferred_element_type=F32
        ).astype(BF)
        for w in range(2):
            for q in range(4):
                k = (q - y + 4) % 4
                base = (w * 4 + q) * 2
                even = prod[base * piece : (base + 1) * piece]
                odd = prod[(base + 1) * piece : (base + 2) * piece]
                keep[k, j, w] = jnp.where(c == 0, even, odd)
                send[k, j, w] = jnp.where(c == 0, odd, even)
    acc_out[...] = acc


def grads_part(nj, pos, g0, gp, ga, gb, gm, attended, weight, acc):
    span, width = weight.shape
    seq = attended.shape[0]
    piece = span // (16 * nj)
    sds = jax.ShapeDtypeStruct
    vm = pl.BlockSpec(memory_space=pltpu.VMEM)
    return pl.pallas_call(
        grads_kernel,
        in_specs=[pl.BlockSpec(memory_space=pltpu.SMEM)] + [vm] * 8,
        out_specs=[vm] * 3,
        out_shape=[
            sds((4, nj, 2, piece, width), BF),
            sds((4, nj, 2, piece, width), BF),
            sds((seq, width), F32),
        ],
        scratch_shapes=[pltpu.VMEM((seq, width), BF), pltpu.VMEM((seq, span), BF)],
        compiler_params=pltpu.CompilerParams(vmem_limit_bytes=VMEM_LIMIT),
        cost_estimate=pl.CostEstimate(
            flops=4 * seq * width * span,
            bytes_accessed=2 * (2 * span * width + seq * span),
            transcendentals=0,
        ),
        name="grads_part",
    )(pos, g0, gp, ga, gb, gm, attended, weight, acc)


def sum_f32(*parts):
    total = parts[0].astype(F32)
    for part in parts[1:]:
        total = total + part.astype(F32)
    return total


def on_device(query, key, value, residual, cotangent, out_weight, norm_gain, doc_ids):
    seq, width = query.shape
    heads = width // HD
    piece = out_weight.shape[0]
    rows, d_model = residual.shape
    half = rows // 2
    span = d_model // 4
    scale = 1.0 / math.sqrt(HD)
    dp = lax.axis_index("dp")
    m = lax.axis_index("mp")
    x, w, y, c = dp // 16, dp // 8 % 2, dp // 2 % 4, dp % 2
    pos = jnp.stack([y, c, m]).astype(jnp.int32)

    across = send_dp(out_weight, flip_w=True)
    pair = jnp.where(w == 0, jnp.stack([out_weight, across]), jnp.stack([across, out_weight]))
    planes = [pair] + [send_dp(pair, dx=-j) for j in (1, 2, 3)]

    query3 = query.reshape(seq, heads, HD)
    key3 = key.reshape(seq, heads, HD)
    value3 = value.reshape(seq, heads, HD)
    probs = attention_probs(query3, key3, doc_ids)
    probs_b = probs.astype(BF)
    attended = jnp.einsum("hts,shd->thd", probs_b, value3, preferred_element_type=F32)
    attended = attended.astype(BF).reshape(seq, width)

    def plane_cols(array, j):
        return lax.dynamic_slice_in_dim(array, ((x + j) % 4) * span, span, array.ndim - 1)

    weights, mixed, gscaled, cot = [], [], [], []
    sq = jnp.zeros((rows, 1), F32)
    dot = jnp.zeros((rows, 1), F32)
    for group in GROUPS:
        mine = jnp.stack([planes[j] for j in group])
        cat = jnp.stack([mine] + [send_dp(mine, dy=-k) for k in (1, 2, 3)])
        oth = send_dp(cat, flip_c=True)
        weight, p0, p1, p2a, p2b, p3 = branch_part(pos, attended, cat, oth)
        weights.append(weight)
        ra = send_mp(p2a, 1)
        rb = send_mp(p2b, -1)
        up = jnp.concatenate([sum_f32(p1[:half], ra).astype(BF), p1[half:]])
        down = jnp.concatenate([p3[:half], sum_f32(p3[half:], rb).astype(BF)])
        branch = sum_f32(p0, send_mp(up, 1), send_mp(down, -1))
        res = jnp.concatenate([plane_cols(residual, j) for j in group], 1).astype(F32)
        ct = jnp.concatenate([plane_cols(cotangent, j) for j in group], 1).astype(F32)
        gain = jnp.concatenate([plane_cols(norm_gain, j) for j in group])
        mx = res + branch
        gs = ct * gain
        sq = sq + jnp.sum(mx * mx, axis=1, keepdims=True)
        dot = dot + jnp.sum(gs * mx, axis=1, keepdims=True)
        mixed.append(mx)
        gscaled.append(gs)
        cot.append(ct)

    inv = lax.rsqrt(sq / d_model + 1e-05)
    mean_dot = dot / d_model

    grad_residual = jnp.zeros((rows, d_model), BF)
    gain_rows = jnp.zeros((4, span), F32)
    acc = jnp.zeros((seq, width), F32)
    outgoing = {}
    for index, group in enumerate(GROUPS):
        mx, gs, ct = mixed[index], gscaled[index], cot[index]
        g0 = (inv * (gs - mx * inv * inv * mean_dot)).astype(BF)
        stat = jnp.sum(ct * mx * inv, axis=0)
        for n, j in enumerate(group):
            at = (x + j) % 4
            grad_residual = lax.dynamic_update_slice_in_dim(
                grad_residual, g0[:, n * span : (n + 1) * span], at * span, 1
            )
            gain_rows = lax.dynamic_update_slice_in_dim(
                gain_rows, stat[None, n * span : (n + 1) * span], at, 0
            )
        gm = send_mp(g0, 1)
        gp = send_mp(g0, -1)
        ga = send_mp(gm[:half], 1)
        gb = send_mp(gp[half:], -1)
        keep, send, acc = grads_part(
            len(group), pos, g0, gp, ga, gb, gm, attended, weights[index], acc
        )
        got = send_dp(send, flip_c=True)
        both = sum_f32(keep, got).astype(BF)
        part = sum_f32(both[0], *[send_dp(both[k], dy=k) for k in (1, 2, 3)]).astype(BF)
        for n, j in enumerate(group):
            outgoing[j] = part[n]

    total = sum_f32(outgoing[0], *[send_dp(outgoing[j], dx=j) for j in (1, 2, 3)])
    home = jnp.where(w == 0, total[0], total[1])
    away = jnp.where(w == 0, total[1], total[0]).astype(BF)
    grad_weight = (home + send_dp(away, flip_w=True).astype(F32)) / 64

    gain_total = gain_rows.reshape(d_model // 128, 128)
    gain_total = gain_total + lax.ppermute(gain_total, "mp", [(i, i ^ 1) for i in range(4)])
    gain_total = gain_total + lax.ppermute(gain_total, "mp", [(i, i ^ 2) for i in range(4)])
    for bit in (1, 8, 2, 4, 16, 32):
        gain_total = gain_total + lax.ppermute(gain_total, "dp", [(i, i ^ bit) for i in range(64)])
    grad_gain = lax.dynamic_slice_in_dim(gain_total.reshape(d_model) / 64, dp * piece, piece, 0)

    acc = jnp.concatenate([acc, acc])
    grad_attended = lax.dynamic_slice_in_dim(acc, ((4 - m) % 4) * rows, seq, 0).astype(BF)
    grad3 = grad_attended.reshape(seq, heads, HD)
    grad_value = jnp.einsum("hts,thd->shd", probs_b, grad3, preferred_element_type=F32)
    grad_value = grad_value.astype(BF).reshape(seq, width)
    grad_probs = jnp.einsum("thd,shd->hts", grad3, value3, preferred_element_type=F32)
    delta = jnp.sum(probs * grad_probs, axis=2, keepdims=True)
    grad_scores = (probs * (grad_probs - delta)).astype(BF)
    grad_query = jnp.einsum("hts,shd->thd", grad_scores, key3, preferred_element_type=F32) * scale
    grad_key = jnp.einsum("hts,thd->shd", grad_scores, query3, preferred_element_type=F32) * scale
    grad_query = grad_query.astype(BF).reshape(seq, width)
    grad_key = grad_key.astype(BF).reshape(seq, width)
    return (grad_query, grad_key, grad_value, grad_residual, grad_weight, grad_gain)


def solution(mesh):
    placed = (
        P("dp", "mp"),
        P("dp", "mp"),
        P("dp", "mp"),
        P(("dp", "mp"), None),
        P(("dp", "mp"), None),
        P("dp", "mp"),
        P(),
        P("dp"),
    )
    return jax.shard_map(
        on_device,
        mesh=mesh,
        in_specs=placed,
        out_specs=(
            P("dp", "mp"),
            P("dp", "mp"),
            P("dp", "mp"),
            P(("dp", "mp"), None),
            P("dp", "mp"),
            P("dp"),
        ),
        check_vma=False,
    )
```

time: 573 us -> 288 us (0.50)
  the two profiles are of different devices: /device:TPU:1 before, /device:TPU:8 now
where the time goes in v1:
time: 288 us; the launch traced here: 283 us
  starting transfers between devices  159 us (55%)
  waiting for transfers between devices  56.7 us (20%)
  other arithmetic  23.5 us (8%)
  local copies, waits for them, and re-layouts  18.3 us (6%)
  Pallas kernels  16.9 us (6%)
  matrix products  6.41 us (2%)
    ppermute x32, starting transfers between devices, send_mp(): return lax.ppermute(value, 'mp', [(i, (i + step) % 4) for i in range(4)])  78.6 us
    ppermute x40, starting transfers between devices, send_dp(): return lax.ppermute(value, 'dp', dp_perm(**step))  65.5 us
    ppermute x40, waiting for transfers between devices, send_dp(): return lax.ppermute(value, 'dp', dp_perm(**step))  24.9 us
    ppermute x32, waiting for transfers between devices, send_mp(): return lax.ppermute(value, 'mp', [(i, (i + step) % 4) for i in range(4)])  17.5 us
    unnamed x94, local copies, waits for them, and re-layouts  13.7 us
    pallas_call x4, Pallas kernels, grads_part(): pl.pallas_call(grads_kernel, in_specs=[pl.BlockSpec(memory_space=pltpu.SM...  11.3 us
    ppermute x6, starting transfers between devices, on_device(): lax.ppermute(gain_total, 'dp', [(i, i ^ bit) for i in range(64)])  8.32 us
    ppermute x6, waiting for transfers between devices, on_device(): lax.ppermute(gain_total, 'dp', [(i, i ^ bit) for i in range(64)])  7.88 us
  transfers between devices with their start and end apart: 80, of which 28 were waited for; matrix products, arithmetic and copies ran while one was open for 12% of the time, Pallas kernels for 6%

profile of v1, /device:TPU:8, one launch (start us, length us, event | category | flops | bytes accessed | tf_op | source)
XLA Modules:
  0.0 282.6 jit_solution(4096642586910628312)
XLA Ops:
  2.7 3.1 %collective-permute-done = bf16[80,640]{1,0:T(8,128)(2,1)S(1)} collective-permute-done((bf16[80,640]{1,0:T(8,128)(2,1)}, bf16[80,640]{1,0:T(8,128)(2,1)S(1)}, u32[]{:S(2)}, u32[]{:S(2)}) %collective-permute-start) | collective-permute-done | bytes 102432 | tf_op jit(solution)/shard_map/ppermute | solution.py:28
  13.5 3.0 %collective-permute-start.18 = (bf16[2,80,640]{2,1,0:T(8,128)(2,1)}, bf16[2,80,640]{2,1,0:T(8,128)(2,1)}, u32[]{:S(2)}, u32[]{:S(2)}) collective-permute-start(bf16[2,80,640]{2,1,0:T(8,128)(2,1)} %maximum_select_fusion.2), channel_id=1, source_target_pairs={{0,128},{4,132},{8,136},{12,140},{16,144},{20,148},{24,152},{28,15... | collective-permute-start | bytes 614408 | tf_op jit(solution)/shard_map/ppermute | solution.py:28
  30.0 6.6 %collective-permute-start.29 = (bf16[1,2,80,640]{3,2,1,0:T(8,128)(2,1)}, bf16[1,2,80,640]{3,2,1,0:T(8,128)(2,1)}, u32[]{:S(2)}, u32[]{:S(2)}) collective-permute-start(bf16[1,2,80,640]{3,2,1,0:T(8,128)(2,1)} %bitcast.29), channel_id=1, source_target_pairs={{0,16},{4,20},{8,24},{12,28},{16,0},{20,4},{24,8},{28,12},{32,48},... | collective-permute-start | bytes 614408 | tf_op jit(solution)/shard_map/ppermute | solution.py:28
  42.3 3.5 %collective-permute-start.11 = (bf16[1,2,80,640]{3,2,1,0:T(8,128)(2,1)}, bf16[1,2,80,640]{3,2,1,0:T(8,128)(2,1)S(1)}, u32[]{:S(2)}, u32[]{:S(2)}) collective-permute-start(bf16[1,2,80,640]{3,2,1,0:T(8,128)(2,1)} %bitcast.135), channel_id=1, source_target_pairs={{0,16},{4,20},{8,24},{12,28},{16,0},{20,4},{24,8},{28,12},{32,48},... | collective-permute-start | bytes 614408 | tf_op jit(solution)/shard_map/ppermute | solution.py:28
  54.4 3.4 %collective-permute-start.5 = (bf16[32,1280]{1,0:T(8,128)(2,1)S(1)}, bf16[32,1280]{1,0:T(8,128)(2,1)S(1)}, u32[]{:S(2)}, u32[]{:S(2)}) collective-permute-start(bf16[32,1280]{1,0:T(8,128)(2,1)S(1)} %get-tuple-element.44), channel_id=1, source_target_pairs={{0,1},{1,2},{2,3},{3,0},{4,5},{5,6},{6,7},{7,4},{8,9},{9,10},{10,1... | collective-permute-start | bytes 245768 | tf_op jit(solution)/shard_map/ppermute | solution.py:32
  58.0 6.0 %collective-permute-start.7 = (bf16[32,1280]{1,0:T(8,128)(2,1)S(1)}, bf16[32,1280]{1,0:T(8,128)(2,1)S(1)}, u32[]{:S(2)}, u32[]{:S(2)}) collective-permute-start(bf16[32,1280]{1,0:T(8,128)(2,1)S(1)} %get-tuple-element.46), channel_id=1, source_target_pairs={{0,3},{1,0},{2,1},{3,2},{4,7},{5,4},{6,5},{7,6},{8,11},{9,8},{10,9... | collective-permute-start | bytes 245768 | tf_op jit(solution)/shard_map/ppermute | solution.py:32
  70.0 3.8 %collective-permute-start.23 = (bf16[32,1280]{1,0:T(8,128)(2,1)S(1)}, bf16[32,1280]{1,0:T(8,128)(2,1)S(1)}, u32[]{:S(2)}, u32[]{:S(2)}) collective-permute-start(bf16[32,1280]{1,0:T(8,128)(2,1)S(1)} %get-tuple-element.54), channel_id=1, source_target_pairs={{0,1},{1,2},{2,3},{3,0},{4,5},{5,6},{6,7},{7,4},{8,9},{9,10},{10,1... | collective-permute-start | bytes 245768 | tf_op jit(solution)/shard_map/ppermute | solution.py:32
  75.4 3.0 %collective-permute-start.25 = (bf16[32,1280]{1,0:T(8,128)(2,1)S(1)}, bf16[32,1280]{1,0:T(8,128)(2,1)S(1)}, u32[]{:S(2)}, u32[]{:S(2)}) collective-permute-start(bf16[32,1280]{1,0:T(8,128)(2,1)S(1)} %get-tuple-element.56), channel_id=1, source_target_pairs={{0,3},{1,0},{2,1},{3,2},{4,7},{5,4},{6,5},{7,6},{8,11},{9,8},{10,9... | collective-permute-start | bytes 245768 | tf_op jit(solution)/shard_map/ppermute | solution.py:32
  82.6 13.0 %collective-permute-start.34 = (bf16[32,1280]{1,0:T(8,128)(2,1)S(1)}, bf16[32,1280]{1,0:T(8,128)(2,1)S(1)}, u32[]{:S(2)}, u32[]{:S(2)}) collective-permute-start(bf16[32,1280]{1,0:T(8,128)(2,1)S(1)} %get-tuple-element.61), channel_id=1, source_target_pairs={{0,3},{1,0},{2,1},{3,2},{4,7},{5,4},{6,5},{7,6},{8,11},{9,8},{10,9... | collective-permute-start | bytes 245768 | tf_op jit(solution)/shard_map/ppermute | solution.py:32
  96.4 4.1 %collective-permute-start.16 = (bf16[32,1280]{1,0:T(8,128)(2,1)S(1)}, bf16[32,1280]{1,0:T(8,128)(2,1)S(1)}, u32[]{:S(2)}, u32[]{:S(2)}) collective-permute-start(bf16[32,1280]{1,0:T(8,128)(2,1)S(1)} %get-tuple-element.51), channel_id=1, source_target_pairs={{0,3},{1,0},{2,1},{3,2},{4,7},{5,4},{6,5},{7,6},{8,11},{9,8},{10,9... | collective-permute-start | bytes 245768 | tf_op jit(solution)/shard_map/ppermute | solution.py:32
  103.0 3.1 %collective-permute-start.26 = (bf16[64,1280]{1,0:T(8,128)(2,1)}, bf16[64,1280]{1,0:T(8,128)(2,1)S(1)}, u32[]{:S(2)}, u32[]{:S(2)}) collective-permute-start(bf16[64,1280]{1,0:T(8,128)(2,1)} %pad_maximum_fusion.9), channel_id=1, source_target_pairs={{0,3},{1,0},{2,1},{3,2},{4,7},{5,4},{6,5},{7,6},{8,11},{9,8},{10,9... | collective-permute-start | bytes 491528 | tf_op jit(solution)/shard_map/ppermute | solution.py:32
  107.6 4.1 %collective-permute-start.35 = (bf16[64,1280]{1,0:T(8,128)(2,1)}, bf16[64,1280]{1,0:T(8,128)(2,1)S(1)}, u32[]{:S(2)}, u32[]{:S(2)}) collective-permute-start(bf16[64,1280]{1,0:T(8,128)(2,1)} %pad_maximum_fusion.11), channel_id=1, source_target_pairs={{0,3},{1,0},{2,1},{3,2},{4,7},{5,4},{6,5},{7,6},{8,11},{9,8},{10,9... | collective-permute-start | bytes 491528 | tf_op jit(solution)/shard_map/ppermute | solution.py:32
  116.8 3.7 %collective-permute-done.33 = bf16[64,1280]{1,0:T(8,128)(2,1)S(1)} collective-permute-done((bf16[64,1280]{1,0:T(8,128)(2,1)}, bf16[64,1280]{1,0:T(8,128)(2,1)S(1)}, u32[]{:S(2)}, u32[]{:S(2)}) %collective-permute-start.33) | collective-permute-done | bytes 163872 | tf_op jit(solution)/shard_map/ppermute | solution.py:32
  128.8 3.3 %collective-permute-start.72 = (f32[40,128]{1,0:T(8,128)S(1)}, f32[40,128]{1,0:T(8,128)S(1)}, u32[]{:S(2)}, u32[]{:S(2)}) collective-permute-start(f32[40,128]{1,0:T(8,128)S(1)} %reshape.314), channel_id=1, source_target_pairs={{0,1},{1,0},{2,3},{3,2},{4,5},{5,4},{6,7},{7,6},{8,9},{9,8},{10,11... | collective-permute-start | bytes 61448 | tf_op jit(solution)/shard_map/ppermute | solution.py:263
  134.1 3.2 %collective-permute-start.73 = (f32[40,128]{1,0:T(8,128)S(1)}, f32[40,128]{1,0:T(8,128)S(1)}, u32[]{:S(2)}, u32[]{:S(2)}) collective-permute-start(f32[40,128]{1,0:T(8,128)S(1)} %add.371), channel_id=1, source_target_pairs={{0,2},{1,3},{2,0},{3,1},{4,6},{5,7},{6,4},{7,5},{8,10},{9,11},{10,... | collective-permute-start | bytes 61448 | tf_op jit(solution)/shard_map/ppermute | solution.py:264
  137.3 4.4 %collective-permute-done.73 = f32[40,128]{1,0:T(8,128)S(1)} collective-permute-done((f32[40,128]{1,0:T(8,128)S(1)}, f32[40,128]{1,0:T(8,128)S(1)}, u32[]{:S(2)}, u32[]{:S(2)}) %collective-permute-start.73) | collective-permute-done | bytes 20512 | tf_op jit(solution)/shard_map/ppermute | solution.py:264
  149.2 5.2 %collective-permute-start.76 = (f32[40,128]{1,0:T(8,128)S(1)}, f32[40,128]{1,0:T(8,128)S(1)}, u32[]{:S(2)}, u32[]{:S(2)}) collective-permute-start(f32[40,128]{1,0:T(8,128)S(1)} %add.374), channel_id=1, source_target_pairs={{0,8},{4,12},{8,0},{12,4},{16,24},{20,28},{24,16},{28,20},{32,40},... | collective-permute-start | bytes 61448 | tf_op jit(solution)/shard_map/ppermute | solution.py:266
  162.0 3.1 %collective-permute-done.77 = f32[40,128]{1,0:T(8,128)S(1)} collective-permute-done((f32[40,128]{1,0:T(8,128)S(1)}, f32[40,128]{1,0:T(8,128)S(1)}, u32[]{:S(2)}, u32[]{:S(2)}) %collective-permute-start.77) | collective-permute-done | bytes 20512 | tf_op jit(solution)/shard_map/ppermute | solution.py:266
  165.3 3.6 %collective-permute-done.78 = f32[40,128]{1,0:T(8,128)S(1)} collective-permute-done((f32[40,128]{1,0:T(8,128)S(1)}, f32[40,128]{1,0:T(8,128)S(1)}, u32[]{:S(2)}, u32[]{:S(2)}) %collective-permute-start.78) | collective-permute-done | bytes 20512 | tf_op jit(solution)/shard_map/ppermute | solution.py:266
  169.3 3.7 %collective-permute-start.40 = (bf16[64,1280]{1,0:T(8,128)(2,1)S(1)}, bf16[64,1280]{1,0:T(8,128)(2,1)}, u32[]{:S(2)}, u32[]{:S(2)}) collective-permute-start(bf16[64,1280]{1,0:T(8,128)(2,1)S(1)} %get-tuple-element.107.g0), channel_id=1, source_target_pairs={{0,3},{1,0},{2,1},{3,2},{4,7},{5,4},{6,5},{7,6},{8,11},{9,8},{10,9... | collective-permute-start | bytes 491528 | tf_op jit(solution)/shard_map/ppermute | solution.py:32
  174.7 4.2 %collective-permute-start.36 = (bf16[64,1280]{1,0:T(8,128)(2,1)S(1)}, bf16[64,1280]{1,0:T(8,128)(2,1)S(1)}, u32[]{:S(2)}, u32[]{:S(2)}) collective-permute-start(bf16[64,1280]{1,0:T(8,128)(2,1)S(1)} %get-tuple-element.105.g0), channel_id=1, source_target_pairs={{0,3},{1,0},{2,1},{3,2},{4,7},{5,4},{6,5},{7,6},{8,11},{9,8},{10,9... | collective-permute-start | bytes 491528 | tf_op jit(solution)/shard_map/ppermute | solution.py:32
  181.6 3.1 %collective-permute-done.41.gm = bf16[64,1280]{1,0:T(8,128)(2,1)} collective-permute-done((bf16[64,1280]{1,0:T(8,128)(2,1)S(1)}, bf16[64,1280]{1,0:T(8,128)(2,1)}, u32[]{:S(2)}, u32[]{:S(2)}) %collective-permute-start.41) | collective-permute-done | bytes 163872 | tf_op jit(solution)/shard_map/ppermute | solution.py:32
  184.7 2.9 %collective-permute-start.46 = (bf16[32,1280]{1,0:T(8,128)(2,1)S(1)}, bf16[32,1280]{1,0:T(8,128)(2,1)S(1)}, u32[]{:S(2)}, u32[]{:S(2)}) collective-permute-start(bf16[32,1280]{1,0:T(8,128)(2,1)S(1)} %slice.174), channel_id=1, source_target_pairs={{0,1},{1,2},{2,3},{3,0},{4,5},{5,6},{6,7},{7,4},{8,9},{9,10},{10,1... | collective-permute-start | bytes 245768 | tf_op jit(solution)/shard_map/ppermute | solution.py:32
  201.7 3.5 %collective-permute-start.39 = (bf16[32,1280]{1,0:T(8,128)(2,1)S(1)}, bf16[32,1280]{1,0:T(8,128)(2,1)S(1)}, u32[]{:S(2)}, u32[]{:S(2)}) collective-permute-start(bf16[32,1280]{1,0:T(8,128)(2,1)S(1)} %slice.171), channel_id=1, source_target_pairs={{0,3},{1,0},{2,1},{3,2},{4,7},{5,4},{6,5},{7,6},{8,11},{9,8},{10,9... | collective-permute-start | bytes 245768 | tf_op jit(solution)/shard_map/ppermute | solution.py:32
  208.4 3.3 %grads_part.6 = (bf16[4,1,2,80,640]{4,3,2,1,0:T(8,128)(2,1)S(1)}, bf16[4,1,2,80,640]{4,3,2,1,0:T(8,128)(2,1)}, f32[256,640]{1,0:T(8,128)S(1)}) custom-call(s32[3]{0:T(128)S(1)} %pad_add_fusion.pos, bf16[64,1280]{1,0:T(8,128)(2,1)S(1)} %get-tuple-element.107.g0, bf16[64,1280]{1,0:T(8,128)(2,1)} %collective-permute-done.40.gp, ...), custom_call_target="tpu_custom_call" | custom-call | flops 838860800 | bytes 3932160 | tf_op jit(solution)/shard_map/grads_part/pallas_call | solution.py:145
  231.6 5.4 %collective-permute-done.57 = bf16[1,2,80,640]{3,2,1,0:T(8,128)(2,1)S(1)} collective-permute-done((bf16[1,2,80,640]{3,2,1,0:T(8,128)(2,1)S(1)}, bf16[1,2,80,640]{3,2,1,0:T(8,128)(2,1)S(1)}, u32[]{:S(2)}, u32[]{:S(2)}) %collective-permute-start.57) | collective-permute-done | bytes 204832 | tf_op jit(solution)/shard_map/ppermute | solution.py:28
  236.9 7.9 %collective-permute-start.63 = (bf16[1,2,80,640]{3,2,1,0:T(8,128)(2,1)S(1)}, bf16[1,2,80,640]{3,2,1,0:T(8,128)(2,1)S(1)}, u32[]{:S(2)}, u32[]{:S(2)}) collective-permute-start(bf16[1,2,80,640]{3,2,1,0:T(8,128)(2,1)S(1)} %get-tuple-element.128), channel_id=1, source_target_pairs={{0,16},{4,20},{8,24},{12,28},{16,0},{20,4},{24,8},{28,12},{32,48},... | collective-permute-start | bytes 614408 | tf_op jit(solution)/shard_map/ppermute | solution.py:28
  245.0 3.4 %collective-permute-done.62 = bf16[1,2,80,640]{3,2,1,0:T(8,128)(2,1)S(1)} collective-permute-done((bf16[1,2,80,640]{3,2,1,0:T(8,128)(2,1)S(1)}, bf16[1,2,80,640]{3,2,1,0:T(8,128)(2,1)S(1)}, u32[]{:S(2)}, u32[]{:S(2)}) %collective-permute-start.62) | collective-permute-done | bytes 204832 | tf_op jit(solution)/shard_map/ppermute | solution.py:28
  249.8 9.8 %collective-permute-start.68 = (bf16[1,2,80,640]{3,2,1,0:T(8,128)(2,1)S(1)}, bf16[1,2,80,640]{3,2,1,0:T(8,128)(2,1)S(1)}, u32[]{:S(2)}, u32[]{:S(2)}) collective-permute-start(bf16[1,2,80,640]{3,2,1,0:T(8,128)(2,1)S(1)} %get-tuple-element.131), channel_id=1, source_target_pairs={{0,16},{4,20},{8,24},{12,28},{16,0},{20,4},{24,8},{28,12},{32,48},... | collective-permute-start | bytes 614408 | tf_op jit(solution)/shard_map/ppermute | solution.py:28
  261.2 5.4 %collective-permute-start.55 = (bf16[1,2,80,640]{3,2,1,0:T(8,128)(2,1)S(1)}, bf16[1,2,80,640]{3,2,1,0:T(8,128)(2,1)S(1)}, u32[]{:S(2)}, u32[]{:S(2)}) collective-permute-start(bf16[1,2,80,640]{3,2,1,0:T(8,128)(2,1)S(1)} %get-tuple-element.121), channel_id=1, source_target_pairs={{0,24},{4,28},{8,0},{12,4},{16,8},{20,12},{24,16},{28,20},{32,56},... | collective-permute-start | bytes 614408 | tf_op jit(solution)/shard_map/ppermute | solution.py:28
  266.7 3.5 %collective-permute-start.65 = (bf16[2,80,640]{2,1,0:T(8,128)(2,1)S(1)}, bf16[2,80,640]{2,1,0:T(8,128)(2,1)S(1)}, u32[]{:S(2)}, u32[]{:S(2)}) collective-permute-start(bf16[2,80,640]{2,1,0:T(8,128)(2,1)S(1)} %fusion.55), channel_id=1, source_target_pairs={{0,128},{4,132},{8,136},{12,140},{16,144},{20,148},{24,152},{28,15... | collective-permute-start | bytes 614408 | tf_op jit(solution)/shard_map/ppermute | solution.py:28
  270.8 2.8 collective-permute-done.60
  (325 shorter events, 138.6 us)
Async XLA Ops:
  6.8 17.0 %collective-permute-start.1 = (bf16[1,2,80,640]{3,2,1,0:T(8,128)(2,1)S(1)}, bf16[1,2,80,640]{3,2,1,0:T(8,128)(2,1)S(1)}, u32[]{:S(2)}, u32[]{:S(2)}) collective-permute-start(bf16[1,2,80,640]{3,2,1,0:T(8,128)(2,1)S(1)} %maximum_select_fusion.1), channel_id=1, source_target_pairs={{0,24},{4,28},{8,0},{12,4},{16,8},{20,12},{24,16},{28,20},{32,56},... | collective-permute-start | bytes 614408 | tf_op jit(solution)/shard_map/ppermute | solution.py:28
  8.9 15.1 %collective-permute-start.2 = (bf16[1,2,80,640]{3,2,1,0:T(8,128)(2,1)S(1)}, bf16[1,2,80,640]{3,2,1,0:T(8,128)(2,1)S(1)}, u32[]{:S(2)}, u32[]{:S(2)}) collective-permute-start(bf16[1,2,80,640]{3,2,1,0:T(8,128)(2,1)S(1)} %maximum_select_fusion.1), channel_id=1, source_target_pairs={{0,16},{4,20},{8,24},{12,28},{16,0},{20,4},{24,8},{28,12},{32,48},... | collective-permute-start | bytes 614408 | tf_op jit(solution)/shard_map/ppermute | solution.py:28
  24.1 26.4 %collective-permute-start.4 = (bf16[4,1,2,80,640]{4,3,2,1,0:T(8,128)(2,1)S(1)}, bf16[4,1,2,80,640]{4,3,2,1,0:T(8,128)(2,1)S(1)}, u32[]{:S(2)}, u32[]{:S(2)}) collective-permute-start(bf16[4,1,2,80,640]{4,3,2,1,0:T(8,128)(2,1)S(1)} %pad_maximum_fusion.cat_ref), channel_id=1, source_target_pairs={{0,4},{4,0},{8,12},{12,8},{16,20},{20,16},{24,28},{28,24},{32,36},... | collective-permute-start | bytes 2457608 | tf_op jit(solution)/shard_map/ppermute | solution.py:28
  30.0 15.9 %collective-permute-start.29 = (bf16[1,2,80,640]{3,2,1,0:T(8,128)(2,1)}, bf16[1,2,80,640]{3,2,1,0:T(8,128)(2,1)}, u32[]{:S(2)}, u32[]{:S(2)}) collective-permute-start(bf16[1,2,80,640]{3,2,1,0:T(8,128)(2,1)} %bitcast.29), channel_id=1, source_target_pairs={{0,16},{4,20},{8,24},{12,28},{16,0},{20,4},{24,8},{28,12},{32,48},... | collective-permute-start | bytes 614408 | tf_op jit(solution)/shard_map/ppermute | solution.py:28
  42.3 15.5 %collective-permute-start.11 = (bf16[1,2,80,640]{3,2,1,0:T(8,128)(2,1)}, bf16[1,2,80,640]{3,2,1,0:T(8,128)(2,1)S(1)}, u32[]{:S(2)}, u32[]{:S(2)}) collective-permute-start(bf16[1,2,80,640]{3,2,1,0:T(8,128)(2,1)} %bitcast.135), channel_id=1, source_target_pairs={{0,16},{4,20},{8,24},{12,28},{16,0},{20,4},{24,8},{28,12},{32,48},... | collective-permute-start | bytes 614408 | tf_op jit(solution)/shard_map/ppermute | solution.py:28
  49.2 18.2 %collective-permute-start.22 = (bf16[4,1,2,80,640]{4,3,2,1,0:T(8,128)(2,1)S(1)}, bf16[4,1,2,80,640]{4,3,2,1,0:T(8,128)(2,1)S(1)}, u32[]{:S(2)}, u32[]{:S(2)}) collective-permute-start(bf16[4,1,2,80,640]{4,3,2,1,0:T(8,128)(2,1)S(1)} %pad_maximum_fusion.2.cat_ref), channel_id=1, source_target_pairs={{0,4},{4,0},{8,12},{12,8},{16,20},{20,16},{24,28},{28,24},{32,36},... | collective-permute-start | bytes 2457608 | tf_op jit(solution)/shard_map/ppermute | solution.py:28
  51.4 24.0 %collective-permute-start.31 = (bf16[4,1,2,80,640]{4,3,2,1,0:T(8,128)(2,1)S(1)}, bf16[4,1,2,80,640]{4,3,2,1,0:T(8,128)(2,1)S(1)}, u32[]{:S(2)}, u32[]{:S(2)}) collective-permute-start(bf16[4,1,2,80,640]{4,3,2,1,0:T(8,128)(2,1)S(1)} %pad_maximum_fusion.3.cat_ref), channel_id=1, source_target_pairs={{0,4},{4,0},{8,12},{12,8},{16,20},{20,16},{24,28},{28,24},{32,36},... | collective-permute-start | bytes 2457608 | tf_op jit(solution)/shard_map/ppermute | solution.py:28
  57.9 23.1 %collective-permute-start.13 = (bf16[4,1,2,80,640]{4,3,2,1,0:T(8,128)(2,1)S(1)}, bf16[4,1,2,80,640]{4,3,2,1,0:T(8,128)(2,1)S(1)}, u32[]{:S(2)}, u32[]{:S(2)}) collective-permute-start(bf16[4,1,2,80,640]{4,3,2,1,0:T(8,128)(2,1)S(1)} %pad_maximum_fusion.1.cat_ref), channel_id=1, source_target_pairs={{0,4},{4,0},{8,12},{12,8},{16,20},{20,16},{24,28},{28,24},{32,36},... | collective-permute-start | bytes 2457608 | tf_op jit(solution)/shard_map/ppermute | solution.py:28
  64.1 43.4 %collective-permute-start.6 = (bf16[64,1280]{1,0:T(8,128)(2,1)S(1)}, bf16[64,1280]{1,0:T(8,128)(2,1)}, u32[]{:S(2)}, u32[]{:S(2)}) collective-permute-start(bf16[64,1280]{1,0:T(8,128)(2,1)S(1)} %pad_maximum_fusion.4), channel_id=1, source_target_pairs={{0,1},{1,2},{2,3},{3,0},{4,5},{5,6},{6,7},{7,4},{8,9},{9,10},{10,1... | collective-permute-start | bytes 491528 | tf_op jit(solution)/shard_map/ppermute | solution.py:32
  73.7 38.0 %collective-permute-start.8 = (bf16[64,1280]{1,0:T(8,128)(2,1)S(1)}, bf16[64,1280]{1,0:T(8,128)(2,1)}, u32[]{:S(2)}, u32[]{:S(2)}) collective-permute-start(bf16[64,1280]{1,0:T(8,128)(2,1)S(1)} %pad_maximum_fusion.5), channel_id=1, source_target_pairs={{0,3},{1,0},{2,1},{3,2},{4,7},{5,4},{6,5},{7,6},{8,11},{9,8},{10,9... | collective-permute-start | bytes 491528 | tf_op jit(solution)/shard_map/ppermute | solution.py:32
  75.4 20.2 %collective-permute-start.25 = (bf16[32,1280]{1,0:T(8,128)(2,1)S(1)}, bf16[32,1280]{1,0:T(8,128)(2,1)S(1)}, u32[]{:S(2)}, u32[]{:S(2)}) collective-permute-start(bf16[32,1280]{1,0:T(8,128)(2,1)S(1)} %get-tuple-element.56), channel_id=1, source_target_pairs={{0,3},{1,0},{2,1},{3,2},{4,7},{5,4},{6,5},{7,6},{8,11},{9,8},{10,9... | collective-permute-start | bytes 245768 | tf_op jit(solution)/shard_map/ppermute | solution.py:32
  81.0 15.4 %collective-permute-start.32 = (bf16[32,1280]{1,0:T(8,128)(2,1)S(1)}, bf16[32,1280]{1,0:T(8,128)(2,1)S(1)}, u32[]{:S(2)}, u32[]{:S(2)}) collective-permute-start(bf16[32,1280]{1,0:T(8,128)(2,1)S(1)} %get-tuple-element.59), channel_id=1, source_target_pairs={{0,1},{1,2},{2,3},{3,0},{4,5},{5,6},{6,7},{7,4},{8,9},{9,10},{10,1... | collective-permute-start | bytes 245768 | tf_op jit(solution)/shard_map/ppermute | solution.py:32
  82.6 18.7 %collective-permute-start.34 = (bf16[32,1280]{1,0:T(8,128)(2,1)S(1)}, bf16[32,1280]{1,0:T(8,128)(2,1)S(1)}, u32[]{:S(2)}, u32[]{:S(2)}) collective-permute-start(bf16[32,1280]{1,0:T(8,128)(2,1)S(1)} %get-tuple-element.61), channel_id=1, source_target_pairs={{0,3},{1,0},{2,1},{3,2},{4,7},{5,4},{6,5},{7,6},{8,11},{9,8},{10,9... | collective-permute-start | bytes 245768 | tf_op jit(solution)/shard_map/ppermute | solution.py:32
  107.6 15.4 %collective-permute-start.35 = (bf16[64,1280]{1,0:T(8,128)(2,1)}, bf16[64,1280]{1,0:T(8,128)(2,1)S(1)}, u32[]{:S(2)}, u32[]{:S(2)}) collective-permute-start(bf16[64,1280]{1,0:T(8,128)(2,1)} %pad_maximum_fusion.11), channel_id=1, source_target_pairs={{0,3},{1,0},{2,1},{3,2},{4,7},{5,4},{6,5},{7,6},{8,11},{9,8},{10,9... | collective-permute-start | bytes 491528 | tf_op jit(solution)/shard_map/ppermute | solution.py:32
  144.6 24.8 %collective-permute-start.49 = (bf16[64,1280]{1,0:T(8,128)(2,1)S(1)}, bf16[64,1280]{1,0:T(8,128)(2,1)S(1)}, u32[]{:S(2)}, u32[]{:S(2)}) collective-permute-start(bf16[64,1280]{1,0:T(8,128)(2,1)S(1)} %get-tuple-element.111.g0), channel_id=1, source_target_pairs={{0,1},{1,2},{2,3},{3,0},{4,5},{5,6},{6,7},{7,4},{8,9},{9,10},{10,1... | collective-permute-start | bytes 491528 | tf_op jit(solution)/shard_map/ppermute | solution.py:32
  147.0 26.0 %collective-permute-start.48 = (bf16[64,1280]{1,0:T(8,128)(2,1)S(1)}, bf16[64,1280]{1,0:T(8,128)(2,1)S(1)}, u32[]{:S(2)}, u32[]{:S(2)}) collective-permute-start(bf16[64,1280]{1,0:T(8,128)(2,1)S(1)} %get-tuple-element.111.g0), channel_id=1, source_target_pairs={{0,3},{1,0},{2,1},{3,2},{4,7},{5,4},{6,5},{7,6},{8,11},{9,8},{10,9... | collective-permute-start | bytes 491528 | tf_op jit(solution)/shard_map/ppermute | solution.py:32
  155.5 17.5 %collective-permute-start.45 = (bf16[64,1280]{1,0:T(8,128)(2,1)S(1)}, bf16[64,1280]{1,0:T(8,128)(2,1)S(1)}, u32[]{:S(2)}, u32[]{:S(2)}) collective-permute-start(bf16[64,1280]{1,0:T(8,128)(2,1)S(1)} %get-tuple-element.109.g0), channel_id=1, source_target_pairs={{0,1},{1,2},{2,3},{3,0},{4,5},{5,6},{6,7},{7,4},{8,9},{9,10},{10,1... | collective-permute-start | bytes 491528 | tf_op jit(solution)/shard_map/ppermute | solution.py:32
  157.2 17.4 %collective-permute-start.44 = (bf16[64,1280]{1,0:T(8,128)(2,1)S(1)}, bf16[64,1280]{1,0:T(8,128)(2,1)S(1)}, u32[]{:S(2)}, u32[]{:S(2)}) collective-permute-start(bf16[64,1280]{1,0:T(8,128)(2,1)S(1)} %get-tuple-element.109.g0), channel_id=1, source_target_pairs={{0,3},{1,0},{2,1},{3,2},{4,7},{5,4},{6,5},{7,6},{8,11},{9,8},{10,9... | collective-permute-start | bytes 491528 | tf_op jit(solution)/shard_map/ppermute | solution.py:32
  168.9 15.8 %collective-permute-start.41 = (bf16[64,1280]{1,0:T(8,128)(2,1)S(1)}, bf16[64,1280]{1,0:T(8,128)(2,1)}, u32[]{:S(2)}, u32[]{:S(2)}) collective-permute-start(bf16[64,1280]{1,0:T(8,128)(2,1)S(1)} %get-tuple-element.107.g0), channel_id=1, source_target_pairs={{0,1},{1,2},{2,3},{3,0},{4,5},{5,6},{6,7},{7,4},{8,9},{9,10},{10,1... | collective-permute-start | bytes 491528 | tf_op jit(solution)/shard_map/ppermute | solution.py:32
  169.3 15.4 %collective-permute-start.40 = (bf16[64,1280]{1,0:T(8,128)(2,1)S(1)}, bf16[64,1280]{1,0:T(8,128)(2,1)}, u32[]{:S(2)}, u32[]{:S(2)}) collective-permute-start(bf16[64,1280]{1,0:T(8,128)(2,1)S(1)} %get-tuple-element.107.g0), channel_id=1, source_target_pairs={{0,3},{1,0},{2,1},{3,2},{4,7},{5,4},{6,5},{7,6},{8,11},{9,8},{10,9... | collective-permute-start | bytes 491528 | tf_op jit(solution)/shard_map/ppermute | solution.py:32
  173.0 15.5 %collective-permute-start.37 = (bf16[64,1280]{1,0:T(8,128)(2,1)S(1)}, bf16[64,1280]{1,0:T(8,128)(2,1)S(1)}, u32[]{:S(2)}, u32[]{:S(2)}) collective-permute-start(bf16[64,1280]{1,0:T(8,128)(2,1)S(1)} %get-tuple-element.105.g0), channel_id=1, source_target_pairs={{0,1},{1,2},{2,3},{3,0},{4,5},{5,6},{6,7},{7,4},{8,9},{9,10},{10,1... | collective-permute-start | bytes 491528 | tf_op jit(solution)/shard_map/ppermute | solution.py:32
  174.7 17.3 %collective-permute-start.36 = (bf16[64,1280]{1,0:T(8,128)(2,1)S(1)}, bf16[64,1280]{1,0:T(8,128)(2,1)S(1)}, u32[]{:S(2)}, u32[]{:S(2)}) collective-permute-start(bf16[64,1280]{1,0:T(8,128)(2,1)S(1)} %get-tuple-element.105.g0), channel_id=1, source_target_pairs={{0,3},{1,0},{2,1},{3,2},{4,7},{5,4},{6,5},{7,6},{8,11},{9,8},{10,9... | collective-permute-start | bytes 491528 | tf_op jit(solution)/shard_map/ppermute | solution.py:32
  178.9 15.0 %collective-permute-start.50 = (bf16[32,1280]{1,0:T(8,128)(2,1)S(1)}, bf16[32,1280]{1,0:T(8,128)(2,1)S(1)}, u32[]{:S(2)}, u32[]{:S(2)}) collective-permute-start(bf16[32,1280]{1,0:T(8,128)(2,1)S(1)} %slice.176), channel_id=1, source_target_pairs={{0,1},{1,2},{2,3},{3,0},{4,5},{5,6},{6,7},{7,4},{8,9},{9,10},{10,1... | collective-permute-start | bytes 245768 | tf_op jit(solution)/shard_map/ppermute | solution.py:32
  184.7 17.0 %collective-permute-start.46 = (bf16[32,1280]{1,0:T(8,128)(2,1)S(1)}, bf16[32,1280]{1,0:T(8,128)(2,1)S(1)}, u32[]{:S(2)}, u32[]{:S(2)}) collective-permute-start(bf16[32,1280]{1,0:T(8,128)(2,1)S(1)} %slice.174), channel_id=1, source_target_pairs={{0,1},{1,2},{2,3},{3,0},{4,5},{5,6},{6,7},{7,4},{8,9},{9,10},{10,1... | collective-permute-start | bytes 245768 | tf_op jit(solution)/shard_map/ppermute | solution.py:32
  188.5 16.7 %collective-permute-start.47 = (bf16[32,1280]{1,0:T(8,128)(2,1)S(1)}, bf16[32,1280]{1,0:T(8,128)(2,1)S(1)}, u32[]{:S(2)}, u32[]{:S(2)}) collective-permute-start(bf16[32,1280]{1,0:T(8,128)(2,1)S(1)} %slice.175), channel_id=1, source_target_pairs={{0,3},{1,0},{2,1},{3,2},{4,7},{5,4},{6,5},{7,6},{8,11},{9,8},{10,9... | collective-permute-start | bytes 245768 | tf_op jit(solution)/shard_map/ppermute | solution.py:32
  192.0 15.9 %collective-permute-start.42 = (bf16[32,1280]{1,0:T(8,128)(2,1)S(1)}, bf16[32,1280]{1,0:T(8,128)(2,1)S(1)}, u32[]{:S(2)}, u32[]{:S(2)}) collective-permute-start(bf16[32,1280]{1,0:T(8,128)(2,1)S(1)} %slice.172), channel_id=1, source_target_pairs={{0,1},{1,2},{2,3},{3,0},{4,5},{5,6},{6,7},{7,4},{8,9},{9,10},{10,1... | collective-permute-start | bytes 245768 | tf_op jit(solution)/shard_map/ppermute | solution.py:32
  196.3 15.4 %collective-permute-start.38 = (bf16[32,1280]{1,0:T(8,128)(2,1)S(1)}, bf16[32,1280]{1,0:T(8,128)(2,1)S(1)}, u32[]{:S(2)}, u32[]{:S(2)}) collective-permute-start(bf16[32,1280]{1,0:T(8,128)(2,1)S(1)} %slice.170), channel_id=1, source_target_pairs={{0,1},{1,2},{2,3},{3,0},{4,5},{5,6},{6,7},{7,4},{8,9},{9,10},{10,1... | collective-permute-start | bytes 245768 | tf_op jit(solution)/shard_map/ppermute | solution.py:32
  207.9 14.9 %collective-permute-start.56 = (bf16[4,1,2,80,640]{4,3,2,1,0:T(8,128)(2,1)}, bf16[4,1,2,80,640]{4,3,2,1,0:T(8,128)(2,1)}, u32[]{:S(2)}, u32[]{:S(2)}) collective-permute-start(bf16[4,1,2,80,640]{4,3,2,1,0:T(8,128)(2,1)} %get-tuple-element.73), channel_id=1, source_target_pairs={{0,4},{4,0},{8,12},{12,8},{16,20},{20,16},{24,28},{28,24},{32,36},... | collective-permute-start | bytes 2457608 | tf_op jit(solution)/shard_map/ppermute | solution.py:28
  220.1 50.2 %collective-permute-start.53 = (bf16[1,2,80,640]{3,2,1,0:T(8,128)(2,1)S(1)}, bf16[1,2,80,640]{3,2,1,0:T(8,128)(2,1)S(1)}, u32[]{:S(2)}, u32[]{:S(2)}) collective-permute-start(bf16[1,2,80,640]{3,2,1,0:T(8,128)(2,1)S(1)} %get-tuple-element.120), channel_id=1, source_target_pairs={{0,8},{4,12},{8,16},{12,20},{16,24},{20,28},{24,0},{28,4},{32,40},... | collective-permute-start | bytes 614408 | tf_op jit(solution)/shard_map/ppermute | solution.py:28
  220.7 50.1 %collective-permute-start.54 = (bf16[1,2,80,640]{3,2,1,0:T(8,128)(2,1)S(1)}, bf16[1,2,80,640]{3,2,1,0:T(8,128)(2,1)S(1)}, u32[]{:S(2)}, u32[]{:S(2)}) collective-permute-start(bf16[1,2,80,640]{3,2,1,0:T(8,128)(2,1)S(1)} %get-tuple-element.122), channel_id=1, source_target_pairs={{0,16},{4,20},{8,24},{12,28},{16,0},{20,4},{24,8},{28,12},{32,48},... | collective-permute-start | bytes 614408 | tf_op jit(solution)/shard_map/ppermute | solution.py:28
  228.7 16.1 %collective-permute-start.59 = (bf16[1,2,80,640]{3,2,1,0:T(8,128)(2,1)S(1)}, bf16[1,2,80,640]{3,2,1,0:T(8,128)(2,1)S(1)}, u32[]{:S(2)}, u32[]{:S(2)}) collective-permute-start(bf16[1,2,80,640]{3,2,1,0:T(8,128)(2,1)S(1)} %get-tuple-element.124), channel_id=1, source_target_pairs={{0,24},{4,28},{8,0},{12,4},{16,8},{20,12},{24,16},{28,20},{32,56},... | collective-permute-start | bytes 614408 | tf_op jit(solution)/shard_map/ppermute | solution.py:28
  249.8 16.9 %collective-permute-start.68 = (bf16[1,2,80,640]{3,2,1,0:T(8,128)(2,1)S(1)}, bf16[1,2,80,640]{3,2,1,0:T(8,128)(2,1)S(1)}, u32[]{:S(2)}, u32[]{:S(2)}) collective-permute-start(bf16[1,2,80,640]{3,2,1,0:T(8,128)(2,1)S(1)} %get-tuple-element.131), channel_id=1, source_target_pairs={{0,16},{4,20},{8,24},{12,28},{16,0},{20,4},{24,8},{28,12},{32,48},... | collective-permute-start | bytes 614408 | tf_op jit(solution)/shard_map/ppermute | solution.py:28
  (92 other events, 935.4 us)

commit v2 on v0

v2 whole, which is shorter than its diff:
```python
import math

import jax
import jax.numpy as jnp
from jax import lax
from jax.experimental import pallas as pl
from jax.experimental.pallas import tpu as pltpu
from jax.sharding import PartitionSpec as P

HD = 128
BF = jnp.bfloat16
F32 = jnp.float32
VMEM_LIMIT = 40 * 1024 * 1024


CHIPS = [[2 * i + c for i in range(32)] for c in range(2)]
FLIP_C = [(i, i ^ 1) for i in range(64)]


def swap(value, pairs):
    return lax.ppermute(value, "dp", pairs)


def send_mp(value, step):
    return lax.ppermute(value, "mp", [(i, (i + step) % 4) for i in range(4)])


def exchange(blocks, groups):
    return lax.all_to_all(blocks, "dp", 0, 0, axis_index_groups=groups)


def spread(block):
    return jnp.broadcast_to(block[None], (4, *block.shape))


def attention_probs(query3, key3, doc_ids):
    seq = query3.shape[0]
    scale = 1.0 / math.sqrt(HD)
    scores = jnp.einsum("thd,shd->hts", query3, key3, preferred_element_type=F32) * scale
    pos = lax.iota(jnp.int32, seq)
    allowed = (pos[None, :] <= pos[:, None]) & (doc_ids[None, :] == doc_ids[:, None])
    scores = jnp.where(allowed[None], scores, -1e30)
    top = jnp.max(scores, axis=2, keepdims=True)
    weights = jnp.exp(scores - top)
    return weights / jnp.sum(weights, axis=2, keepdims=True)


def turn_tokens(pos, att_ref, att_s):
    rows = att_ref.shape[0] // 4
    for k in range(4):
        start = pl.multiple_of(((pos[1] + k) % 4) * rows, 16)
        att_s[pl.ds(k * rows, rows), :] = att_ref[pl.ds(start, rows), :]


def branch_kernel(pos, att_ref, cat_ref, oth_ref, w_ref, p0, p1a, p1b, p2a, p2b, p3a, p3b, att_s):
    count, piece, _ = cat_ref.shape
    c = pos[0]
    rows = att_ref.shape[0] // 4
    half = rows // 2

    @pl.when(pl.program_id(0) == 0)
    def _():
        turn_tokens(pos, att_ref, att_s)

    for i in range(count):
        mine = pl.multiple_of((2 * i + c) * piece, 16)
        other = pl.multiple_of((2 * i + 1 - c) * piece, 16)
        w_ref[pl.ds(mine, piece), :] = cat_ref[i]
        w_ref[pl.ds(other, piece), :] = oth_ref[i]
    prod = lax.dot_general(
        att_s[...], w_ref[...], (((1,), (1,)), ((), ())), preferred_element_type=F32
    ).astype(BF)
    p0[...] = prod[:rows]
    p1a[...] = prod[rows : rows + half]
    p1b[...] = prod[rows + half : 2 * rows]
    p2a[...] = prod[2 * rows : 2 * rows + half]
    p2b[...] = prod[2 * rows + half : 3 * rows]
    p3a[...] = prod[3 * rows : 3 * rows + half]
    p3b[...] = prod[3 * rows + half :]


def branch_part(pos, attended, cat, oth):
    count, piece, width = cat.shape
    seq = attended.shape[0]
    rows, span, total = seq // 4, 16 * piece, 2 * count * piece
    sds = jax.ShapeDtypeStruct
    heights = (rows,) + (rows // 2,) * 6
    block = pl.BlockSpec((8, piece, width), lambda i: (i, 0, 0))
    return pl.pallas_call(
        branch_kernel,
        grid=(count // 8,),
        in_specs=[
            pl.BlockSpec(memory_space=pltpu.SMEM),
            pl.BlockSpec((seq, width), lambda i: (0, 0)),
            block,
            block,
        ],
        out_specs=[pl.BlockSpec((span, width), lambda i: (i, 0))]
        + [pl.BlockSpec((h, span), lambda i: (0, i)) for h in heights],
        out_shape=[sds((total, width), BF)] + [sds((h, total), BF) for h in heights],
        scratch_shapes=[pltpu.VMEM((seq, width), BF)],
        compiler_params=pltpu.CompilerParams(vmem_limit_bytes=VMEM_LIMIT),
        cost_estimate=pl.CostEstimate(
            flops=2 * seq * width * total,
            bytes_accessed=2 * (2 * total * width + seq * total),
            transcendentals=0,
        ),
        name="branch_part",
    )(pos, attended, cat, oth)


def grads_kernel(
    pos, _, g0, gp, ga, gb, gm, att_ref, w_ref, keep, send, out_ref, att_s, rows_s, acc
):
    count, piece, _ = keep.shape
    c, m = pos[0], pos[1]
    rows = g0.shape[0]
    half = rows // 2
    step = pl.program_id(0)

    @pl.when(step == 0)
    def _():
        turn_tokens(pos, att_ref, att_s)
        acc[...] = jnp.zeros_like(acc)

    rows_s[pl.ds(0, rows), :] = g0[...]
    rows_s[pl.ds(rows, rows), :] = gp[...]
    rows_s[pl.ds(2 * rows, half), :] = ga[...]
    rows_s[pl.ds(2 * rows + half, half), :] = gb[...]
    rows_s[pl.ds(3 * rows, rows), :] = gm[...]
    acc[...] += jnp.dot(rows_s[...], w_ref[...], preferred_element_type=F32)
    prod = lax.dot_general(
        rows_s[...], att_s[...], (((0,), (0,)), ((), ())), preferred_element_type=F32
    ).astype(BF)
    for i in range(count):
        even = prod[2 * i * piece : (2 * i + 1) * piece]
        odd = prod[(2 * i + 1) * piece : (2 * i + 2) * piece]
        keep[i] = jnp.where(c == 0, even, odd)
        send[i] = jnp.where(c == 0, odd, even)

    @pl.when(step == pl.num_programs(0) - 1)
    def _():
        for k in range(4):
            start = pl.multiple_of(((m + k) % 4) * rows, 16)
            out_ref[pl.ds(start, rows), :] = acc[pl.ds(k * rows, rows), :].astype(BF)


def grads_part(pos, gain, g0, gp, ga, gb, gm, attended, weight, piece):
    total, width = weight.shape
    seq = attended.shape[0]
    count, span = total // (2 * piece), 16 * piece
    sds = jax.ShapeDtypeStruct
    whole = pl.BlockSpec((seq, width), lambda i: (0, 0))
    block = pl.BlockSpec((8, piece, width), lambda i: (i, 0, 0))
    return pl.pallas_call(
        grads_kernel,
        grid=(count // 8,),
        in_specs=[pl.BlockSpec(memory_space=pltpu.SMEM), pl.BlockSpec(memory_space=pl.ANY)]
        + [pl.BlockSpec((g.shape[0], span), lambda i: (0, i)) for g in (g0, gp, ga, gb, gm)]
        + [whole, pl.BlockSpec((span, width), lambda i: (i, 0))],
        out_specs=[block, block, whole],
        out_shape=[
            sds((count, piece, width), BF),
            sds((count, piece, width), BF),
            sds((seq, width), BF),
        ],
        scratch_shapes=[
            pltpu.VMEM((seq, width), BF),
            pltpu.VMEM((seq, span), BF),
            pltpu.VMEM((seq, width), F32),
        ],
        compiler_params=pltpu.CompilerParams(vmem_limit_bytes=VMEM_LIMIT),
        cost_estimate=pl.CostEstimate(
            flops=4 * seq * width * total,
            bytes_accessed=2 * (2 * total * width + seq * total),
            transcendentals=0,
        ),
        name="grads_part",
    )(pos, gain, g0, gp, ga, gb, gm, attended, weight)


def sum_f32(*parts):
    total = parts[0].astype(F32)
    for part in parts[1:]:
        total = total + part.astype(F32)
    return total


def on_device(query, key, value, residual, cotangent, out_weight, norm_gain, doc_ids):
    seq, width = query.shape
    heads = width // HD
    piece = out_weight.shape[0]
    rows, d_model = residual.shape
    half = rows // 2
    scale = 1.0 / math.sqrt(HD)
    dp = lax.axis_index("dp")
    c = dp % 2
    m = lax.axis_index("mp")
    pos = jnp.stack([c, m]).astype(jnp.int32)

    copies = jnp.broadcast_to(out_weight[None], (32, piece, width))
    cat = exchange(copies, CHIPS)

    query3 = query.reshape(seq, heads, HD)
    key3 = key.reshape(seq, heads, HD)
    value3 = value.reshape(seq, heads, HD)
    probs = attention_probs(query3, key3, doc_ids)
    probs_b = probs.astype(BF)
    attended = jnp.einsum("hts,shd->thd", probs_b, value3, preferred_element_type=F32)
    attended = attended.astype(BF).reshape(seq, width)

    cat, attended = lax.optimization_barrier((cat, attended))
    oth = swap(cat, FLIP_C)
    weight, p0, p1a, p1b, p2a, p2b, p3a, p3b = branch_part(pos, attended, cat, oth)
    ra = send_mp(p2a, 1)
    rb = send_mp(p2b, -1)
    up_b = send_mp(p1b, 1)
    down_a = send_mp(p3a, -1)
    up_a = send_mp(sum_f32(p1a, ra).astype(BF), 1)
    down_b = send_mp(sum_f32(p3b, rb).astype(BF), -1)
    up = jnp.concatenate([up_a, up_b])
    down = jnp.concatenate([down_a, down_b])
    mixed = sum_f32(residual, p0, up, down)
    cot = cotangent.astype(F32)
    gscaled = cot * norm_gain
    inv = lax.rsqrt(jnp.mean(mixed * mixed, axis=1, keepdims=True) + 1e-05)
    mean_dot = jnp.mean(gscaled * mixed, axis=1, keepdims=True)
    grad_residual = (inv * (gscaled - mixed * inv * inv * mean_dot)).astype(BF)

    gain_rows = jnp.sum(cot * mixed * inv, axis=0).reshape(64, 1, piece)
    gain_rows = jnp.sum(lax.all_to_all(gain_rows, "dp", 0, 0), axis=0)
    gm = send_mp(grad_residual, 1)
    gp = send_mp(grad_residual, -1)
    gm, gp, gain_rows = lax.optimization_barrier((gm, gp, gain_rows))
    ga = send_mp(gm[:half], 1)
    gb = send_mp(gp[half:], -1)
    gain_rows = lax.all_to_all(spread(gain_rows), "mp", 0, 0)
    grad_gain = jnp.sum(gain_rows, axis=0).reshape(piece) / 64
    keep, send, grad_attended = grads_part(
        pos, grad_gain, grad_residual, gp, ga, gb, gm, attended, weight, piece
    )
    both = sum_f32(keep, swap(send, FLIP_C)).astype(BF)
    grad_weight = jnp.sum(exchange(both, CHIPS).astype(F32), axis=0) / 64

    grad3 = grad_attended.reshape(seq, heads, HD)
    grad_value = jnp.einsum("hts,thd->shd", probs_b, grad3, preferred_element_type=F32)
    grad_value = grad_value.astype(BF).reshape(seq, width)
    grad_probs = jnp.einsum("thd,shd->hts", grad3, value3, preferred_element_type=F32)
    delta = jnp.sum(probs * grad_probs, axis=2, keepdims=True)
    grad_scores = (probs * (grad_probs - delta)).astype(BF)
    grad_query = jnp.einsum("hts,shd->thd", grad_scores, key3, preferred_element_type=F32) * scale
    grad_key = jnp.einsum("hts,thd->shd", grad_scores, query3, preferred_element_type=F32) * scale
    grad_query = grad_query.astype(BF).reshape(seq, width)
    grad_key = grad_key.astype(BF).reshape(seq, width)
    return (grad_query, grad_key, grad_value, grad_residual, grad_weight, grad_gain)


def solution(mesh):
    placed = (
        P("dp", "mp"),
        P("dp", "mp"),
        P("dp", "mp"),
        P(("dp", "mp"), None),
        P(("dp", "mp"), None),
        P("dp", "mp"),
        P(),
        P("dp"),
    )
    return jax.shard_map(
        on_device,
        mesh=mesh,
        in_specs=placed,
        out_specs=(
            P("dp", "mp"),
            P("dp", "mp"),
            P("dp", "mp"),
            P(("dp", "mp"), None),
            P("dp", "mp"),
            P("dp"),
        ),
        check_vma=False,
    )
```

time: 573 us -> 254 us (0.44)
  waiting for transfers between devices: 442 us -> 121 us
  starting transfers between devices: 0.16 us -> 33 us
  blocking collectives: 77.7 us -> 50.5 us
  matrix products: 24.8 us -> 6.55 us
  Pallas kernels: 0 us -> 13.3 us
  between operations: 14 us -> 0.87 us
  local copies, waits for them, and re-layouts: 7.76 us -> 16.4 us
    reduce_scatter x2 -> x0, waiting for transfers between devices: 269 us -> none  [the longest x1 211 us: on_device(): lax.psum_scatter(lax.dot_general(grad_rows, attended, token_dims, preferr...]
    all_gather x2 -> x0, waiting for transfers between devices: 172 us -> none  [the longest x1 113 us: on_device(): weight_full = lax.all_gather(out_weight, 'dp', axis=0, tiled=True)]
    psum x1 -> x0, blocking collectives: 77.7 us -> none  [on_device(): total = lax.psum(gain_term / n_dp, ('dp', 'mp'))]
    all_to_all x0 -> x2, waiting for transfers between devices: none -> 74.3 us  [exchange(): return lax.all_to_all(blocks, 'dp', 0, 0, axis_index_groups=groups)]
    all_to_all x0 -> x2, blocking collectives: none -> 50.5 us  [the longest x1 32.9 us: on_device(): gain_rows = jnp.sum(lax.all_to_all(gain_rows, 'dp', 0, 0), axis=0)]
    ppermute x0 -> x12, waiting for transfers between devices: none -> 47.1 us  [the longest x10 37.9 us: send_mp(): return lax.ppermute(value, 'mp', [(i, (i + step) % 4) for i in range(4)])]
    dot_general x8 -> x5, matrix products: 24.2 us -> 3.83 us  [the longest x1 2.42 us: on_device(): jnp.einsum('hts,shd->thd', probs_b, value3, preferred_element_type=F32)]
    ppermute x0 -> x12, starting transfers between devices: none -> 18.8 us  [the longest x10 16.2 us: send_mp(): return lax.ppermute(value, 'mp', [(i, (i + step) % 4) for i in range(4)])]
  transfers between devices with their start and end apart: 4 -> 14, of which waited for: 4 -> 8; matrix products, arithmetic and copies ran while one was open for 3% -> 7% of each run, Pallas kernels for 0% -> 0%
where the time goes in v2:
time: 254 us; the launch traced here: 250 us
  waiting for transfers between devices  121 us (48%)
  blocking collectives  50.5 us (20%)
  starting transfers between devices  33 us (13%)
  local copies, waits for them, and re-layouts  16.4 us (6%)
  Pallas kernels  13.3 us (5%)
  other arithmetic  7.7 us (3%)
  matrix products  6.55 us (3%)
    all_to_all x2, waiting for transfers between devices, exchange(): return lax.all_to_all(blocks, 'dp', 0, 0, axis_index_groups=groups)  74.3 us
    ppermute x10, waiting for transfers between devices, send_mp(): return lax.ppermute(value, 'mp', [(i, (i + step) % 4) for i in range(4)])  37.9 us
    all_to_all x1, blocking collectives, on_device(): gain_rows = jnp.sum(lax.all_to_all(gain_rows, 'dp', 0, 0), axis=0)  32.9 us
    all_to_all x1, blocking collectives, on_device(): gain_rows = lax.all_to_all(spread(gain_rows), 'mp', 0, 0)  17.6 us
    ppermute x10, starting transfers between devices, send_mp(): return lax.ppermute(value, 'mp', [(i, (i + step) % 4) for i in range(4)])  16.2 us
    all_to_all x2, starting transfers between devices, exchange(): return lax.all_to_all(blocks, 'dp', 0, 0, axis_index_groups=groups)  14.2 us
    unnamed x30, local copies, waits for them, and re-layouts  10.7 us
    ppermute x2, waiting for transfers between devices, swap(): return lax.ppermute(value, 'dp', pairs)  9.13 us
  transfers between devices with their start and end apart: 14, of which 8 were waited for; matrix products, arithmetic and copies ran while one was open for 7% of the time, Pallas kernels for 0%

profile of v2, /device:TPU:1, one launch (start us, length us, event | category | flops | bytes accessed | tf_op | source)
XLA Modules:
  0.0 249.8 jit_solution(14493820922942417172)
XLA Ops:
  0.6 2.8 %broadcast_in_dim.20 = bf16[32,80,640]{2,1,0:T(8,128)(2,1)} broadcast(bf16[80,640]{1,0:T(8,128)(2,1)} %param.13), dimensions={1,2} | broadcast | bytes 3379200 | tf_op jit(solution)/shard_map/broadcast_in_dim | solution.py:201
  3.5 9.2 %all-to-all-start = ((bf16[32,80,640]{2,1,0:T(8,128)(2,1)}), bf16[32,80,640]{2,1,0:T(8,128)(2,1)S(1)}, u32[]{:S(2)}, u32[]{:S(2)}) async-start(bf16[32,80,640]{2,1,0:T(8,128)(2,1)} %broadcast_in_dim.20), calls=%async_computation | async-start | bytes 6553600 | tf_op jit(solution)/shard_map/all_to_all | solution.py:29
  12.7 1.9 copy.64
  14.6 1.9 copy.65
  16.4 1.9 copy.68
  18.4 2.7 %fusion.19 = (f32[5,256]{1,0:T(8,128)S(1)}, f32[5,256,256]{1,2,0:T(8,128)}) fusion(bf16[256,5,128]{0,2,1:T(8,128)(2,1)} %bitcast.32, bf16[256,5,128]{0,2,1:T(8,128)(2,1)} %bitcast.34, pred[256,256]{0,1:T(8,128)(4,1)S(1)} %fusion.15), kind=kOutput, calls=%fused_computation.41 | convolution fusion | flops 85197056 | bytes 2036736 | tf_op jit(solution)/shard_map/sub | solution.py:44
  21.2 2.4 convolution_convert_fusion
  23.6 33.6 %all-to-all-done.cat_ref = bf16[32,80,640]{2,1,0:T(8,128)(2,1)S(1)} async-done(((bf16[32,80,640]{2,1,0:T(8,128)(2,1)}), bf16[32,80,640]{2,1,0:T(8,128)(2,1)S(1)}, u32[]{:S(2)}, u32[]{:S(2)}) %all-to-all-start) | async-done | bytes 3276832 | tf_op jit(solution)/shard_map/all_to_all | solution.py:29
  57.2 2.0 collective-permute-start
  59.2 1.9 copy.70.att_ref
  61.1 3.7 %collective-permute-done.oth_ref = bf16[32,80,640]{2,1,0:T(8,128)(2,1)} collective-permute-done((bf16[32,80,640]{2,1,0:T(8,128)(2,1)S(1)}, bf16[32,80,640]{2,1,0:T(8,128)(2,1)}, u32[]{:S(2)}, u32[]{:S(2)}) %collective-permute-start) | collective-permute-done | bytes 3276832 | tf_op jit(solution)/shard_map/ppermute | solution.py:21
  64.7 1.0 copy-done
  65.7 6.4 %branch_part.1 = (bf16[5120,640]{1,0:T(8,128)(2,1)}, bf16[64,5120]{1,0:T(8,128)(2,1)S(1)}, bf16[32,5120]{1,0:T(8,128)(2,1)S(1)}, bf16[32,5120]{1,0:T(8,128)(2,1)...) custom-call(s32[2]{0:T(128)S(1)} %pad_add_fusion.pos, ...), custom_call_target="tpu_custom_call" | custom-call | flops 1677721600 | bytes 15728640 | tf_op jit(solution)/shard_map/branch_part/pallas_call | solution.py:89
  72.2 3.0 %collective-permute-start.1 = (bf16[32,5120]{1,0:T(8,128)(2,1)S(1)}, bf16[32,5120]{1,0:T(8,128)(2,1)S(1)}, u32[]{:S(2)}, u32[]{:S(2)}) collective-permute-start(bf16[32,5120]{1,0:T(8,128)(2,1)S(1)} %get-tuple-element.26), channel_id=1, source_target_pairs={{0,1},{1,2},{2,3},{3,0},{4,5},{5,6},{6,7},{7,4},{8,9},{9,10},{10,1... | collective-permute-start | bytes 983048 | tf_op jit(solution)/shard_map/ppermute | solution.py:25
  75.2 3.3 %collective-permute-start.3 = (bf16[32,5120]{1,0:T(8,128)(2,1)S(1)}, bf16[32,5120]{1,0:T(8,128)(2,1)S(1)}, u32[]{:S(2)}, u32[]{:S(2)}) collective-permute-start(bf16[32,5120]{1,0:T(8,128)(2,1)S(1)} %get-tuple-element.27), channel_id=1, source_target_pairs={{0,1},{1,2},{2,3},{3,0},{4,5},{5,6},{6,7},{7,4},{8,9},{9,10},{10,1... | collective-permute-start | bytes 983048 | tf_op jit(solution)/shard_map/ppermute | solution.py:25
  78.7 1.0 collective-permute-start.5
  79.7 25.7 %collective-permute-done.1 = bf16[32,5120]{1,0:T(8,128)(2,1)S(1)} collective-permute-done((bf16[32,5120]{1,0:T(8,128)(2,1)S(1)}, bf16[32,5120]{1,0:T(8,128)(2,1)S(1)}, u32[]{:S(2)}, u32[]{:S(2)}) %collective-permute-start.1) | collective-permute-done | bytes 327712 | tf_op jit(solution)/shard_map/ppermute | solution.py:25
  105.6 2.2 collective-permute-done.5
  107.9 1.6 collective-permute-start.6
  109.5 2.9 %collective-permute-done.3 = bf16[32,5120]{1,0:T(8,128)(2,1)S(1)} collective-permute-done((bf16[32,5120]{1,0:T(8,128)(2,1)S(1)}, bf16[32,5120]{1,0:T(8,128)(2,1)S(1)}, u32[]{:S(2)}, u32[]{:S(2)}) %collective-permute-start.3) | collective-permute-done | bytes 327712 | tf_op jit(solution)/shard_map/ppermute | solution.py:25
  112.4 7.0 %collective-permute-done.2 = bf16[32,5120]{1,0:T(8,128)(2,1)S(1)} collective-permute-done((bf16[32,5120]{1,0:T(8,128)(2,1)S(1)}, bf16[32,5120]{1,0:T(8,128)(2,1)S(1)}, u32[]{:S(2)}, u32[]{:S(2)}) %collective-permute-start.2) | collective-permute-done | bytes 327712 | tf_op jit(solution)/shard_map/ppermute | solution.py:25
  121.4 3.4 %collective-permute-start.8 = (bf16[64,5120]{1,0:T(8,128)(2,1)S(1)}, bf16[64,5120]{1,0:T(8,128)(2,1)S(1)}, u32[]{:S(2)}, u32[]{:S(2)}) collective-permute-start(bf16[64,5120]{1,0:T(8,128)(2,1)S(1)} %fusion.8.g0), channel_id=1, source_target_pairs={{0,3},{1,0},{2,1},{3,2},{4,7},{5,4},{6,5},{7,6},{8,11},{9,8},{10,9... | collective-permute-start | bytes 1966088 | tf_op jit(solution)/shard_map/ppermute | solution.py:25
  125.0 32.9 %all_to_all.20 = f32[64,1,80]{2,1,0:T(1,128)S(1)} all-to-all(f32[64,1,80]{2,1,0:T(1,128)S(1)} %reshape.107), channel_id=1, replica_groups=mesh['dp'=64,'mp'=4] {'dp'}, dimensions={0} | all-to-all | bytes 40960 | tf_op jit(solution)/shard_map/all_to_all | solution.py:231
  158.7 2.9 %collective-permute-start.9 = (bf16[32,5120]{1,0:T(8,128)(2,1)}, bf16[32,5120]{1,0:T(8,128)(2,1)S(1)}, u32[]{:S(2)}, u32[]{:S(2)}) collective-permute-start(bf16[32,5120]{1,0:T(8,128)(2,1)} %slice.6), channel_id=1, source_target_pairs={{0,1},{1,2},{2,3},{3,0},{4,5},{5,6},{6,7},{7,4},{8,9},{9,10},{10,1... | collective-permute-start | bytes 983048 | tf_op jit(solution)/shard_map/ppermute | solution.py:25
  162.3 17.6 %all_to_all.21 = f32[4,1,80]{2,1,0:T(1,128)S(1)} all-to-all(f32[4,1,80]{2,1,0:T(1,128)S(1)} %broadcast_in_dim.22), channel_id=1, replica_groups=mesh['dp'=64,'mp'=4] {'mp'}, dimensions={0} | all-to-all | bytes 2560 | tf_op jit(solution)/shard_map/all_to_all | solution.py:237
  180.0 6.9 %grads_part.1 = (bf16[32,80,640]{2,1,0:T(8,128)(2,1)S(1)}, bf16[32,80,640]{2,1,0:T(8,128)(2,1)S(1)}, bf16[256,640]{1,0:T(8,128)(2,1)S(1)}) custom-call(s32[2]{0:T(128)S(1)} %pad_add_fusion.pos, f32[80]{0:T(128)S(1)} %broadcast_multiply_fusion.1._, bf16[64,5120]{1,0:T(8,128)(2,1)S(1)} %fusion.8.g0, bf16[64,5120]{1,0:T(8,128)(2,1)S(1)} %collective-permute-done.8.gp, ...), custom_call_target="tpu_custom_call" | custom-call | flops 3355443200 | bytes 15728640 | tf_op jit(solution)/shard_map/grads_part/pallas_call | solution.py:155
  187.6 5.5 %collective-permute-done.11 = bf16[32,80,640]{2,1,0:T(8,128)(2,1)S(1)} collective-permute-done((bf16[32,80,640]{2,1,0:T(8,128)(2,1)S(1)}, bf16[32,80,640]{2,1,0:T(8,128)(2,1)S(1)}, u32[]{:S(2)}, u32[]{:S(2)}) %collective-permute-start.11) | collective-permute-done | bytes 3276832 | tf_op jit(solution)/shard_map/ppermute | solution.py:21
  193.1 2.6 %add_convert_fusion = bf16[32,80,640]{2,1,0:T(8,128)(2,1)} fusion(bf16[32,80,640]{2,1,0:T(8,128)(2,1)S(1)} %collective-permute-done.11, bf16[32,80,640]{2,1,0:T(8,128)(2,1)S(1)} %get-tuple-element.36), kind=kLoop, calls=%fused_computation.2 | loop fusion | flops 6553600 | bytes 9830400 | tf_op jit(solution)/shard_map/convert_element_type | solution.py:242
  195.7 5.0 %all-to-all-start.3 = ((bf16[32,80,640]{2,1,0:T(8,128)(2,1)}), bf16[32,80,640]{2,1,0:T(8,128)(2,1)}, u32[]{:S(2)}, u32[]{:S(2)}) async-start(bf16[32,80,640]{2,1,0:T(8,128)(2,1)} %add_convert_fusion), calls=%async_computation.3 | async-start | bytes 6553600 | tf_op jit(solution)/shard_map/all_to_all | solution.py:29
  201.3 0.9 copy.82
  206.0 40.6 %all-to-all-done.3 = bf16[32,80,640]{2,1,0:T(8,128)(2,1)} async-done(((bf16[32,80,640]{2,1,0:T(8,128)(2,1)}), bf16[32,80,640]{2,1,0:T(8,128)(2,1)}, u32[]{:S(2)}, u32[]{:S(2)}) %all-to-all-start.3) | async-done | bytes 3276832 | tf_op jit(solution)/shard_map/all_to_all | solution.py:29
  246.7 2.4 convert_reduce_fusion
  (59 shorter events, 10.0 us)
Async XLA Ops:
  3.5 53.7 %all-to-all-start = ((bf16[32,80,640]{2,1,0:T(8,128)(2,1)}), bf16[32,80,640]{2,1,0:T(8,128)(2,1)S(1)}, u32[]{:S(2)}, u32[]{:S(2)}) async-start(bf16[32,80,640]{2,1,0:T(8,128)(2,1)} %broadcast_in_dim.20), calls=%async_computation | async-start | bytes 6553600 | tf_op jit(solution)/shard_map/all_to_all | solution.py:29
  12.7 5.6 %copy-start.11 = (s32[256]{0:T(256)S(1)}, s32[256]{0:T(256)}, u32[]{:S(2)}) copy-start(s32[256]{0:T(256)} %param.15) | copy-start | bytes 3076
  57.2 7.6 %collective-permute-start = (bf16[32,80,640]{2,1,0:T(8,128)(2,1)S(1)}, bf16[32,80,640]{2,1,0:T(8,128)(2,1)}, u32[]{:S(2)}, u32[]{:S(2)}) collective-permute-start(bf16[32,80,640]{2,1,0:T(8,128)(2,1)S(1)} %all-to-all-done.cat_ref), channel_id=1, source_target_pairs={{0,4},{4,0},{8,12},{12,8},{16,20},{20,16},{24,28},{28,24},{32,36},... | collective-permute-start | bytes 9830408 | tf_op jit(solution)/shard_map/ppermute | solution.py:21
  64.7 1.0 copy-start
  72.2 47.3 %copy-start.8 = (bf16[64,5120]{1,0:T(8,128)(2,1)S(1)}, bf16[64,5120]{1,0:T(8,128)(2,1)}, u32[]{:S(2)}) copy-start(bf16[64,5120]{1,0:T(8,128)(2,1)} %param.11) | copy-start | bytes 1966084
  72.2 33.3 %collective-permute-start.1 = (bf16[32,5120]{1,0:T(8,128)(2,1)S(1)}, bf16[32,5120]{1,0:T(8,128)(2,1)S(1)}, u32[]{:S(2)}, u32[]{:S(2)}) collective-permute-start(bf16[32,5120]{1,0:T(8,128)(2,1)S(1)} %get-tuple-element.26), channel_id=1, source_target_pairs={{0,1},{1,2},{2,3},{3,0},{4,5},{5,6},{6,7},{7,4},{8,9},{9,10},{10,1... | collective-permute-start | bytes 983048 | tf_op jit(solution)/shard_map/ppermute | solution.py:25
  75.2 37.3 %collective-permute-start.3 = (bf16[32,5120]{1,0:T(8,128)(2,1)S(1)}, bf16[32,5120]{1,0:T(8,128)(2,1)S(1)}, u32[]{:S(2)}, u32[]{:S(2)}) collective-permute-start(bf16[32,5120]{1,0:T(8,128)(2,1)S(1)} %get-tuple-element.27), channel_id=1, source_target_pairs={{0,1},{1,2},{2,3},{3,0},{4,5},{5,6},{6,7},{7,4},{8,9},{9,10},{10,1... | collective-permute-start | bytes 983048 | tf_op jit(solution)/shard_map/ppermute | solution.py:25
  78.5 34.0 %collective-permute-start.4 = (bf16[32,5120]{1,0:T(8,128)(2,1)S(1)}, bf16[32,5120]{1,0:T(8,128)(2,1)S(1)}, u32[]{:S(2)}, u32[]{:S(2)}) collective-permute-start(bf16[32,5120]{1,0:T(8,128)(2,1)S(1)} %get-tuple-element.28), channel_id=1, source_target_pairs={{0,3},{1,0},{2,1},{3,2},{4,7},{5,4},{6,5},{7,6},{8,11},{9,8},{10,9... | collective-permute-start | bytes 983048 | tf_op jit(solution)/shard_map/ppermute | solution.py:25
  78.7 29.1 %collective-permute-start.5 = (bf16[32,5120]{1,0:T(8,128)(2,1)S(1)}, bf16[32,5120]{1,0:T(8,128)(2,1)S(1)}, u32[]{:S(2)}, u32[]{:S(2)}) collective-permute-start(bf16[32,5120]{1,0:T(8,128)(2,1)S(1)} %get-tuple-element.30), channel_id=1, source_target_pairs={{0,3},{1,0},{2,1},{3,2},{4,7},{5,4},{6,5},{7,6},{8,11},{9,8},{10,9... | collective-permute-start | bytes 983048 | tf_op jit(solution)/shard_map/ppermute | solution.py:25
  105.5 14.0 %collective-permute-start.2 = (bf16[32,5120]{1,0:T(8,128)(2,1)S(1)}, bf16[32,5120]{1,0:T(8,128)(2,1)S(1)}, u32[]{:S(2)}, u32[]{:S(2)}) collective-permute-start(bf16[32,5120]{1,0:T(8,128)(2,1)S(1)} %add_convert_fusion.2), channel_id=1, source_target_pairs={{0,1},{1,2},{2,3},{3,0},{4,5},{5,6},{6,7},{7,4},{8,9},{9,10},{10,1... | collective-permute-start | bytes 983048 | tf_op jit(solution)/shard_map/ppermute | solution.py:25
  107.9 11.6 %collective-permute-start.6 = (bf16[32,5120]{1,0:T(8,128)(2,1)S(1)}, bf16[32,5120]{1,0:T(8,128)(2,1)S(1)}, u32[]{:S(2)}, u32[]{:S(2)}) collective-permute-start(bf16[32,5120]{1,0:T(8,128)(2,1)S(1)} %add_convert_fusion.1), channel_id=1, source_target_pairs={{0,3},{1,0},{2,1},{3,2},{4,7},{5,4},{6,5},{7,6},{8,11},{9,8},{10,9... | collective-permute-start | bytes 983048 | tf_op jit(solution)/shard_map/ppermute | solution.py:25
  119.5 1.1 copy-start.4
  119.5 1.1 copy-start.10
  121.4 65.5 %copy-start.2 = (bf16[64,5120]{1,0:T(8,128)(2,1)}, bf16[64,5120]{1,0:T(8,128)(2,1)S(1)}, u32[]{:S(2)}) copy-start(bf16[64,5120]{1,0:T(8,128)(2,1)S(1)} %fusion.8.g0) | copy-start | bytes 1966084
  121.4 58.6 %copy-start.1 = (bf16[256,640]{1,0:T(8,128)(2,1)S(1)}, bf16[256,640]{1,0:T(8,128)(2,1)}, u32[]{:S(2)}) copy-start(bf16[256,640]{1,0:T(8,128)(2,1)} %copy.70.att_ref) | copy-start | bytes 983044
  121.4 36.5 %collective-permute-start.8 = (bf16[64,5120]{1,0:T(8,128)(2,1)S(1)}, bf16[64,5120]{1,0:T(8,128)(2,1)S(1)}, u32[]{:S(2)}, u32[]{:S(2)}) collective-permute-start(bf16[64,5120]{1,0:T(8,128)(2,1)S(1)} %fusion.8.g0), channel_id=1, source_target_pairs={{0,3},{1,0},{2,1},{3,2},{4,7},{5,4},{6,5},{7,6},{8,11},{9,8},{10,9... | collective-permute-start | bytes 1966088 | tf_op jit(solution)/shard_map/ppermute | solution.py:25
  124.9 33.1 %collective-permute-start.7 = (bf16[64,5120]{1,0:T(8,128)(2,1)S(1)}, bf16[64,5120]{1,0:T(8,128)(2,1)S(1)}, u32[]{:S(2)}, u32[]{:S(2)}) collective-permute-start(bf16[64,5120]{1,0:T(8,128)(2,1)S(1)} %fusion.8.g0), channel_id=1, source_target_pairs={{0,1},{1,2},{2,3},{3,0},{4,5},{5,6},{6,7},{7,4},{8,9},{9,10},{10,1... | collective-permute-start | bytes 1966088 | tf_op jit(solution)/shard_map/ppermute | solution.py:25
  158.7 21.3 %collective-permute-start.9 = (bf16[32,5120]{1,0:T(8,128)(2,1)}, bf16[32,5120]{1,0:T(8,128)(2,1)S(1)}, u32[]{:S(2)}, u32[]{:S(2)}) collective-permute-start(bf16[32,5120]{1,0:T(8,128)(2,1)} %slice.6), channel_id=1, source_target_pairs={{0,1},{1,2},{2,3},{3,0},{4,5},{5,6},{6,7},{7,4},{8,9},{9,10},{10,1... | collective-permute-start | bytes 983048 | tf_op jit(solution)/shard_map/ppermute | solution.py:25
  161.7 18.3 %collective-permute-start.10 = (bf16[32,5120]{1,0:T(8,128)(2,1)S(1)}, bf16[32,5120]{1,0:T(8,128)(2,1)S(1)}, u32[]{:S(2)}, u32[]{:S(2)}) collective-permute-start(bf16[32,5120]{1,0:T(8,128)(2,1)S(1)} %slice.7), channel_id=1, source_target_pairs={{0,3},{1,0},{2,1},{3,2},{4,7},{5,4},{6,5},{7,6},{8,11},{9,8},{10,9... | collective-permute-start | bytes 983048 | tf_op jit(solution)/shard_map/ppermute | solution.py:25
  180.0 6.9 %copy-start.3 = (f32[80]{0:T(128)}, f32[80]{0:T(128)S(1)}, u32[]{:S(2)}) copy-start(f32[80]{0:T(128)S(1)} %broadcast_multiply_fusion.1._) | copy-start | bytes 964
  186.9 6.2 %collective-permute-start.11 = (bf16[32,80,640]{2,1,0:T(8,128)(2,1)S(1)}, bf16[32,80,640]{2,1,0:T(8,128)(2,1)S(1)}, u32[]{:S(2)}, u32[]{:S(2)}) collective-permute-start(bf16[32,80,640]{2,1,0:T(8,128)(2,1)S(1)} %get-tuple-element.37), channel_id=1, source_target_pairs={{0,4},{4,0},{8,12},{12,8},{16,20},{20,16},{24,28},{28,24},{32,36},... | collective-permute-start | bytes 9830408 | tf_op jit(solution)/shard_map/ppermute | solution.py:21
  195.7 5.1 %copy-start.5 = (f32[5,256,256]{1,2,0:T(8,128)S(1)}, f32[5,256,256]{1,2,0:T(8,128)}, u32[]{:S(2)}) copy-start(f32[5,256,256]{1,2,0:T(8,128)} %get-tuple-element.67) | copy-start | bytes 3932164
  195.7 50.9 %all-to-all-start.3 = ((bf16[32,80,640]{2,1,0:T(8,128)(2,1)}), bf16[32,80,640]{2,1,0:T(8,128)(2,1)}, u32[]{:S(2)}, u32[]{:S(2)}) async-start(bf16[32,80,640]{2,1,0:T(8,128)(2,1)} %add_convert_fusion), calls=%async_computation.3 | async-start | bytes 6553600 | tf_op jit(solution)/shard_map/all_to_all | solution.py:29
  200.9 1.3 copy-start.9
  202.6 1.0 copy-start.7
  203.6 1.2 copy-start.6

commit v3 on v2

--- a/solution.py
+++ b/solution.py
@@ -13,7 +13,18 @@
 VMEM_LIMIT = 40 * 1024 * 1024
 
 
-CHIPS = [[2 * i + c for i in range(32)] for c in range(2)]
+def rings(along_y):
+    groups = []
+    for c in range(2):
+        for w in range(2):
+            for line in range(4):
+                places = [(line, k) if (c == 0) == along_y else (k, line) for k in range(4)]
+                groups.append([((x * 2 + w) * 4 + y) * 2 + c for x, y in places])
+    return groups
+
+
+NEAR, FAR = rings(True), rings(False)
+FLIP_W = [(i, i ^ 8) for i in range(64)]
 FLIP_C = [(i, i ^ 1) for i in range(64)]
 
 
@@ -52,8 +63,14 @@
         att_s[pl.ds(k * rows, rows), :] = att_ref[pl.ds(start, rows), :]
 
 
-def branch_kernel(pos, att_ref, cat_ref, oth_ref, w_ref, p0, p1a, p1b, p2a, p2b, p3a, p3b, att_s):
-    count, piece, _ = cat_ref.shape
+def place(c, x, y):
+    return jnp.where(c == 0, x, y), jnp.where(c == 0, y, x)
+
+
+def branch_kernel(pos, att_ref, *refs):
+    mine, other = refs[:4], refs[4:8]
+    w_ref, p0, p1a, p1b, p2a, p2b, p3a, p3b, att_s = refs[8:]
+    piece = mine[0].shape[3]
     c = pos[0]
     rows = att_ref.shape[0] // 4
     half = rows // 2
@@ -62,11 +79,11 @@
     def _():
         turn_tokens(pos, att_ref, att_s)
 
-    for i in range(count):
-        mine = pl.multiple_of((2 * i + c) * piece, 16)
-        other = pl.multiple_of((2 * i + 1 - c) * piece, 16)
-        w_ref[pl.ds(mine, piece), :] = cat_ref[i]
-        w_ref[pl.ds(other, piece), :] = oth_ref[i]
+    for w in range(2):
+        for y in range(4):
+            i = w * 4 + y
+            w_ref[pl.ds(pl.multiple_of((2 * i + c) * piece, 16), piece), :] = mine[y][0, 0, w]
+            w_ref[pl.ds(pl.multiple_of((2 * i + 1 - c) * piece, 16), piece), :] = other[y][0, 0, w]
     prod = lax.dot_general(
         att_s[...], w_ref[...], (((1,), (1,)), ((), ())), preferred_element_type=F32
     ).astype(BF)
@@ -80,25 +97,31 @@
 
 
 def branch_part(pos, attended, cat, oth):
-    count, piece, width = cat.shape
+    piece, width = cat.shape[3:]
     seq = attended.shape[0]
-    rows, span, total = seq // 4, 16 * piece, 2 * count * piece
+    rows, span = seq // 4, 16 * piece
+    total = 4 * span
     sds = jax.ShapeDtypeStruct
     heights = (rows,) + (rows // 2,) * 6
-    block = pl.BlockSpec((8, piece, width), lambda i: (i, 0, 0))
+
+    def block(flip, y):
+        def at(i, pos):
+            return *place(pos[0] ^ flip, i, y), 0, 0, 0
+
+        return pl.BlockSpec((1, 1, 2, piece, width), at)
+
     return pl.pallas_call(
         branch_kernel,
-        grid=(count // 8,),
-        in_specs=[
-            pl.BlockSpec(memory_space=pltpu.SMEM),
-            pl.BlockSpec((seq, width), lambda i: (0, 0)),
-            block,
-            block,
-        ],
-        out_specs=[pl.BlockSpec((span, width), lambda i: (i, 0))]
-        + [pl.BlockSpec((h, span), lambda i: (0, i)) for h in heights],
+        grid_spec=pltpu.PrefetchScalarGridSpec(
+            num_scalar_prefetch=1,
+            grid=(4,),
+            in_specs=[pl.BlockSpec((seq, width), lambda i, pos: (0, 0))]
+            + [block(flip, y) for flip in range(2) for y in range(4)],
+            out_specs=[pl.BlockSpec((span, width), lambda i, pos: (i, 0))]
+            + [pl.BlockSpec((h, span), lambda i, pos: (0, i)) for h in heights],
+            scratch_shapes=[pltpu.VMEM((seq, width), BF)],
+        ),
         out_shape=[sds((total, width), BF)] + [sds((h, total), BF) for h in heights],
-        scratch_shapes=[pltpu.VMEM((seq, width), BF)],
         compiler_params=pltpu.CompilerParams(vmem_limit_bytes=VMEM_LIMIT),
         cost_estimate=pl.CostEstimate(
             flops=2 * seq * width * total,
@@ -106,13 +129,13 @@
             transcendentals=0,
         ),
         name="branch_part",
-    )(pos, attended, cat, oth)
+    )(pos, attended, *[cat] * 4, *[oth] * 4)
 
 
 def grads_kernel(
-    pos, _, g0, gp, ga, gb, gm, att_ref, w_ref, keep, send, out_ref, att_s, rows_s, acc
+    pos, g0, gp, ga, gb, gm, att_ref, w_ref, keep, send, out_ref, att_s, rows_s, acc
 ):
-    count, piece, _ = keep.shape
+    piece = keep.shape[3]
     c, m = pos[0], pos[1]
     rows = g0.shape[0]
     half = rows // 2
@@ -132,11 +155,14 @@
     prod = lax.dot_general(
         rows_s[...], att_s[...], (((0,), (0,)), ((), ())), preferred_element_type=F32
     ).astype(BF)
-    for i in range(count):
-        even = prod[2 * i * piece : (2 * i + 1) * piece]
-        odd = prod[(2 * i + 1) * piece : (2 * i + 2) * piece]
-        keep[i] = jnp.where(c == 0, even, odd)
-        send[i] = jnp.where(c == 0, odd, even)
+    for w in range(2):
+        for y in range(4):
+            i = w * 4 + y
+            even = prod[2 * i * piece : (2 * i + 1) * piece]
+            odd = prod[(2 * i + 1) * piece : (2 * i + 2) * piece]
+            far, near = place(c, step, y)
+            keep[far, near, w] = jnp.where(c == 0, even, odd)
+            send[near, far, w] = jnp.where(c == 0, odd, even)
 
     @pl.when(step == pl.num_programs(0) - 1)
     def _():
@@ -145,23 +171,24 @@
             out_ref[pl.ds(start, rows), :] = acc[pl.ds(k * rows, rows), :].astype(BF)
 
 
-def grads_part(pos, gain, g0, gp, ga, gb, gm, attended, weight, piece):
+def grads_part(pos, g0, gp, ga, gb, gm, attended, weight, piece):
     total, width = weight.shape
     seq = attended.shape[0]
-    count, span = total // (2 * piece), 16 * piece
+    span = 16 * piece
+    shape = (4, 4, 2, piece, width)
     sds = jax.ShapeDtypeStruct
     whole = pl.BlockSpec((seq, width), lambda i: (0, 0))
-    block = pl.BlockSpec((8, piece, width), lambda i: (i, 0, 0))
+    block = pl.BlockSpec(shape, lambda i: (0, 0, 0, 0, 0))
     return pl.pallas_call(
         grads_kernel,
-        grid=(count // 8,),
-        in_specs=[pl.BlockSpec(memory_space=pltpu.SMEM), pl.BlockSpec(memory_space=pl.ANY)]
+        grid=(4,),
+        in_specs=[pl.BlockSpec(memory_space=pltpu.SMEM)]
         + [pl.BlockSpec((g.shape[0], span), lambda i: (0, i)) for g in (g0, gp, ga, gb, gm)]
         + [whole, pl.BlockSpec((span, width), lambda i: (i, 0))],
         out_specs=[block, block, whole],
         out_shape=[
-            sds((count, piece, width), BF),
-            sds((count, piece, width), BF),
+            sds(shape, BF),
+            sds(shape, BF),
             sds((seq, width), BF),
         ],
         scratch_shapes=[
@@ -176,7 +203,7 @@
             transcendentals=0,
         ),
         name="grads_part",
-    )(pos, gain, g0, gp, ga, gb, gm, attended, weight)
+    )(pos, g0, gp, ga, gb, gm, attended, weight)
 
 
 def sum_f32(*parts):
@@ -194,12 +221,13 @@
     half = rows // 2
     scale = 1.0 / math.sqrt(HD)
     dp = lax.axis_index("dp")
-    c = dp % 2
+    w, c = dp // 8 % 2, dp % 2
     m = lax.axis_index("mp")
     pos = jnp.stack([c, m]).astype(jnp.int32)
 
-    copies = jnp.broadcast_to(out_weight[None], (32, piece, width))
-    cat = exchange(copies, CHIPS)
+    across = swap(out_weight, FLIP_W)
+    pair = jnp.where(w == 0, jnp.stack([out_weight, across]), jnp.stack([across, out_weight]))
+    cat = exchange(spread(exchange(spread(pair), NEAR)), FAR)
 
     query3 = query.reshape(seq, heads, HD)
     key3 = key.reshape(seq, heads, HD)
@@ -227,20 +255,35 @@
     mean_dot = jnp.mean(gscaled * mixed, axis=1, keepdims=True)
     grad_residual = (inv * (gscaled - mixed * inv * inv * mean_dot)).astype(BF)
 
-    gain_rows = jnp.sum(cot * mixed * inv, axis=0).reshape(64, 1, piece)
-    gain_rows = jnp.sum(lax.all_to_all(gain_rows, "dp", 0, 0), axis=0)
+    tie = lax.optimization_barrier
+
+    def add_from(total, bits):
+        for bit in bits:
+            total = total + swap(total, [(i, i ^ bit) for i in range(64)])
+        return total
+
+    gain = jnp.sum(cot * mixed * inv, axis=0).reshape(d_model // 128, 128)
     gm = send_mp(grad_residual, 1)
     gp = send_mp(grad_residual, -1)
-    gm, gp, gain_rows = lax.optimization_barrier((gm, gp, gain_rows))
+    gm, gp, gain = tie((gm, gp, add_from(gain, (1, 2, 4))))
     ga = send_mp(gm[:half], 1)
     gb = send_mp(gp[half:], -1)
-    gain_rows = lax.all_to_all(spread(gain_rows), "mp", 0, 0)
-    grad_gain = jnp.sum(gain_rows, axis=0).reshape(piece) / 64
+    ga, gb, gain = tie((ga, gb, add_from(gain, (16, 32))))
     keep, send, grad_attended = grads_part(
-        pos, grad_gain, grad_residual, gp, ga, gb, gm, attended, weight, piece
+        pos, grad_residual, gp, ga, gb, gm, attended, weight, piece
     )
     both = sum_f32(keep, swap(send, FLIP_C)).astype(BF)
-    grad_weight = jnp.sum(exchange(both, CHIPS).astype(F32), axis=0) / 64
+    part = exchange(both, FAR)
+    gain = add_from(gain, (8,))
+    for bit in (1, 2):
+        gain = gain + lax.ppermute(gain, "mp", [(i, i ^ bit) for i in range(4)])
+    part, gain = tie((part, gain))
+    part = jnp.sum(part.astype(F32), axis=0).astype(BF)
+    total = jnp.sum(exchange(part, NEAR).astype(F32), axis=0) / 64
+    home = jnp.where(w == 0, total[0], total[1])
+    away = jnp.where(w == 0, total[1], total[0]).astype(BF)
+    grad_weight = home + swap(away, FLIP_W).astype(F32)
+    grad_gain = lax.dynamic_slice_in_dim(gain.reshape(d_model) / 64, dp * piece, piece, 0)
 
     grad3 = grad_attended.reshape(seq, heads, HD)
     grad_value = jnp.einsum("hts,thd->shd", probs_b, grad3, preferred_element_type=F32)

time: 254 us -> 238 us (0.937)
  blocking collectives: 50.5 us -> 13 us
  starting transfers between devices: 33 us -> 63.9 us
  waiting for transfers between devices: 121 us -> 111 us
    all_to_all x2 -> x3, waiting for transfers between devices: 74.3 us -> 21.6 us  [exchange(): return lax.all_to_all(blocks, 'dp', 0, 0, axis_index_groups=groups)]
    all_to_all x2 -> x1, blocking collectives: 50.5 us -> 13 us  [exchange(): return lax.all_to_all(blocks, 'dp', 0, 0, axis_index_groups=groups)]
    ppermute x2 -> x10, starting transfers between devices: 2.65 us -> 25 us  [swap(): return lax.ppermute(value, 'dp', pairs)]
    ppermute x10, waiting for transfers between devices: 37.9 us -> 56.6 us  [send_mp(): return lax.ppermute(value, 'mp', [(i, (i + step) % 4) for i in range(4)])]
    ppermute x2 -> x10, waiting for transfers between devices: 9.13 us -> 27.3 us  [swap(): return lax.ppermute(value, 'dp', pairs)]
    ppermute x10, starting transfers between devices: 16.2 us -> 22.6 us  [send_mp(): return lax.ppermute(value, 'mp', [(i, (i + step) % 4) for i in range(4)])]
    ppermute x0 -> x2, waiting for transfers between devices: none -> 5.91 us  [on_device(): gain = gain + lax.ppermute(gain, 'mp', [(i, i ^ bit) for i in range(4)])]
    ppermute x0 -> x2, starting transfers between devices: none -> 3.94 us  [on_device(): gain = gain + lax.ppermute(gain, 'mp', [(i, i ^ bit) for i in range(4)])]
  transfers between devices with their start and end apart: 14 -> 25, of which waited for: 8 -> 22; matrix products, arithmetic and copies ran while one was open for 7% -> 8% of each run, Pallas kernels for 0% -> 0%
where the time goes in v3:
time: 238 us; the launch traced here: 236 us
  waiting for transfers between devices  111 us (47%)
  starting transfers between devices  63.9 us (27%)
  local copies, waits for them, and re-layouts  15.6 us (7%)
  Pallas kernels  14.1 us (6%)
  blocking collectives  13 us (5%)
  other arithmetic  9.95 us (4%)
  matrix products  7.29 us (3%)
    ppermute x10, waiting for transfers between devices, send_mp(): return lax.ppermute(value, 'mp', [(i, (i + step) % 4) for i in range(4)])  56.6 us
    ppermute x10, waiting for transfers between devices, swap(): return lax.ppermute(value, 'dp', pairs)  27.3 us
    ppermute x10, starting transfers between devices, swap(): return lax.ppermute(value, 'dp', pairs)  25 us
    ppermute x10, starting transfers between devices, send_mp(): return lax.ppermute(value, 'mp', [(i, (i + step) % 4) for i in range(4)])  22.6 us
    all_to_all x3, waiting for transfers between devices, exchange(): return lax.all_to_all(blocks, 'dp', 0, 0, axis_index_groups=groups)  21.6 us
    all_to_all x1, blocking collectives, exchange(): return lax.all_to_all(blocks, 'dp', 0, 0, axis_index_groups=groups)  13 us
    all_to_all x3, starting transfers between devices, exchange(): return lax.all_to_all(blocks, 'dp', 0, 0, axis_index_groups=groups)  12.3 us
    unnamed x26, local copies, waits for them, and re-layouts  10.9 us
  transfers between devices with their start and end apart: 25, of which 22 were waited for; matrix products, arithmetic and copies ran while one was open for 8% of the time, Pallas kernels for 0%

profile of v3, /device:TPU:1, one launch (start us, length us, event | category | flops | bytes accessed | tf_op | source)
XLA Modules:
  0.0 236.0 jit_solution(10700728211832570925)
XLA Ops:
  0.6 2.6 %collective-permute-start = (bf16[80,640]{1,0:T(8,128)(2,1)}, bf16[80,640]{1,0:T(8,128)(2,1)S(1)}, u32[]{:S(2)}, u32[]{:S(2)}) collective-permute-start(bf16[80,640]{1,0:T(8,128)(2,1)} %param.13), channel_id=1, source_target_pairs={{0,32},{4,36},{8,40},{12,44},{16,48},{20,52},{24,56},{28,60},{32,0... | collective-permute-start | bytes 307208 | tf_op jit(solution)/shard_map/ppermute | solution.py:32
  6.5 13.0 %all_to_all.20 = bf16[4,2,80,640]{3,2,1,0:T(8,128)(2,1)S(1)} all-to-all(bf16[4,2,80,640]{3,2,1,0:T(8,128)(2,1)S(1)} %broadcast_in_dim.14), channel_id=1, replica_groups={{0,8,16,24},{64,72,80,88},{128,136,144,152},{192,200,208,216},{32,40,48..., dimensions={0} | all-to-all | bytes 1638400 | tf_op jit(solution)/shard_map/all_to_all | solution.py:40
  21.5 4.0 %all-to-all-start.1 = ((bf16[4,4,2,80,640]{4,3,2,1,0:T(8,128)(2,1)}), bf16[4,4,2,80,640]{4,3,2,1,0:T(8,128)(2,1)S(1)}, u32[]{:S(2)}, u32[]{:S(2)}) async-start(bf16[4,4,2,80,640]{4,3,2,1,0:T(8,128)(2,1)} %broadcast_in_dim.15), calls=%async_computation.1 | async-start | bytes 6553600 | tf_op jit(solution)/shard_map/all_to_all | solution.py:40
  31.3 2.7 %fusion.20 = (f32[5,256]{1,0:T(8,128)S(1)}, f32[5,256,256]{1,2,0:T(8,128)}) fusion(bf16[256,5,128]{0,2,1:T(8,128)(2,1)} %bitcast.40, bf16[256,5,128]{0,2,1:T(8,128)(2,1)} %bitcast.42, pred[256,256]{0,1:T(8,128)(4,1)S(1)} %fusion.15), kind=kOutput, calls=%fused_computation.46 | convolution fusion | flops 85197056 | bytes 2036736 | tf_op jit(solution)/shard_map/sub | solution.py:55
  34.0 2.4 %convolution_convert_fusion = bf16[5,256,128]{1,2,0:T(8,128)(2,1)} fusion(bf16[256,5,128]{0,2,1:T(8,128)(2,1)} %bitcast.46, f32[5,256,256]{1,2,0:T(8,128)} %get-tuple-element.71, f32[5,256]{1,0:T(8,128)S(1)} %get-tuple-element.70), kind=kOutput, calls=%fused_computation.24 | convolution fusion | flops 84705280 | bytes 1971200 | tf_op jit(solution)/shard_map/hts,shd->thd/dot_general | solution.py:237
  36.4 11.1 %all-to-all-done.1.refs_0_.refs_1_.refs_2_.refs_3_ = bf16[4,4,2,80,640]{4,3,2,1,0:T(8,128)(2,1)S(1)} async-done(((bf16[4,4,2,80,640]{4,3,2,1,0:T(8,128)(2,1)}), bf16[4,4,2,80,640]{4,3,2,1,0:T(8,128)(2,1)S(1)}, u32[]{:S(2)}, u32[]{:S(2)}) %all-to-all-start.1) | async-done | bytes 3276832 | tf_op jit(solution)/shard_map/all_to_all | solution.py:40
  47.5 3.8 %collective-permute-start.1 = (bf16[4,4,2,80,640]{4,3,2,1,0:T(8,128)(2,1)S(1)}, bf16[4,4,2,80,640]{4,3,2,1,0:T(8,128)(2,1)}, u32[]{:S(2)}, u32[]{:S(2)}) collective-permute-start(bf16[4,4,2,80,640]{4,3,2,1,0:T(8,128)(2,1)S(1)} %all-to-all-done.1.refs_0_.refs_1_.refs_2_.refs_3_), channel_id=1, source_target_pairs={{0,4},{4,0},{8,12},{12,8},{16,20},{20,16},{24,28},{28,24},{32,36},... | collective-permute-start | bytes 9830408 | tf_op jit(solution)/shard_map/ppermute | solution.py:32
  53.3 3.7 %collective-permute-done.1.refs_4_.refs_5_.refs_6_.refs_7_ = bf16[4,4,2,80,640]{4,3,2,1,0:T(8,128)(2,1)} collective-permute-done((bf16[4,4,2,80,640]{4,3,2,1,0:T(8,128)(2,1)S(1)}, bf16[4,4,2,80,640]{4,3,2,1,0:T(8,128)(2,1)}, u32[]{:S(2)}, u32[]{:S(2)}) %collective-permute-start.1) | collective-permute-done | bytes 3276832 | tf_op jit(solution)/shard_map/ppermute | solution.py:32
  57.9 7.2 %branch_part.1 = (bf16[5120,640]{1,0:T(8,128)(2,1)}, bf16[64,5120]{1,0:T(8,128)(2,1)S(1)}, bf16[32,5120]{1,0:T(8,128)(2,1)S(1)}, bf16[32,5120]{1,0:T(8,128)(2,1)...) custom-call(s32[2]{0:T(128)S(1)} %pad_add_fusion.pos, ...), custom_call_target="tpu_custom_call" | custom-call | flops 1677721600 | bytes 15728640 | tf_op jit(solution)/shard_map/branch_part/pallas_call | solution.py:113
  65.1 3.0 %collective-permute-start.2 = (bf16[32,5120]{1,0:T(8,128)(2,1)S(1)}, bf16[32,5120]{1,0:T(8,128)(2,1)S(1)}, u32[]{:S(2)}, u32[]{:S(2)}) collective-permute-start(bf16[32,5120]{1,0:T(8,128)(2,1)S(1)} %get-tuple-element.31), channel_id=1, source_target_pairs={{0,1},{1,2},{2,3},{3,0},{4,5},{5,6},{6,7},{7,4},{8,9},{9,10},{10,1... | collective-permute-start | bytes 983048 | tf_op jit(solution)/shard_map/ppermute | solution.py:36
  68.1 4.1 %collective-permute-start.4 = (bf16[32,5120]{1,0:T(8,128)(2,1)S(1)}, bf16[32,5120]{1,0:T(8,128)(2,1)S(1)}, u32[]{:S(2)}, u32[]{:S(2)}) collective-permute-start(bf16[32,5120]{1,0:T(8,128)(2,1)S(1)} %get-tuple-element.32), channel_id=1, source_target_pairs={{0,1},{1,2},{2,3},{3,0},{4,5},{5,6},{6,7},{7,4},{8,9},{9,10},{10,1... | collective-permute-start | bytes 983048 | tf_op jit(solution)/shard_map/ppermute | solution.py:36
  73.5 7.4 %collective-permute-done.2 = bf16[32,5120]{1,0:T(8,128)(2,1)S(1)} collective-permute-done((bf16[32,5120]{1,0:T(8,128)(2,1)S(1)}, bf16[32,5120]{1,0:T(8,128)(2,1)S(1)}, u32[]{:S(2)}, u32[]{:S(2)}) %collective-permute-start.2) | collective-permute-done | bytes 327712 | tf_op jit(solution)/shard_map/ppermute | solution.py:36
  81.9 21.4 %collective-permute-done.6 = bf16[32,5120]{1,0:T(8,128)(2,1)S(1)} collective-permute-done((bf16[32,5120]{1,0:T(8,128)(2,1)S(1)}, bf16[32,5120]{1,0:T(8,128)(2,1)S(1)}, u32[]{:S(2)}, u32[]{:S(2)}) %collective-permute-start.6) | collective-permute-done | bytes 327712 | tf_op jit(solution)/shard_map/ppermute | solution.py:36
  104.5 15.8 %collective-permute-done.7 = bf16[32,5120]{1,0:T(8,128)(2,1)S(1)} collective-permute-done((bf16[32,5120]{1,0:T(8,128)(2,1)S(1)}, bf16[32,5120]{1,0:T(8,128)(2,1)S(1)}, u32[]{:S(2)}, u32[]{:S(2)}) %collective-permute-start.7) | collective-permute-done | bytes 327712 | tf_op jit(solution)/shard_map/ppermute | solution.py:36
  127.0 2.6 %collective-permute-done.11 = f32[40,128]{1,0:T(8,128)S(1)} collective-permute-done((f32[40,128]{1,0:T(8,128)S(1)}, f32[40,128]{1,0:T(8,128)S(1)}, u32[]{:S(2)}, u32[]{:S(2)}) %collective-permute-start.11) | collective-permute-done | bytes 20512 | tf_op jit(solution)/shard_map/ppermute | solution.py:32
  130.4 3.7 %collective-permute-done.12 = f32[40,128]{1,0:T(8,128)S(1)} collective-permute-done((f32[40,128]{1,0:T(8,128)S(1)}, f32[40,128]{1,0:T(8,128)S(1)}, u32[]{:S(2)}, u32[]{:S(2)}) %collective-permute-start.12) | collective-permute-done | bytes 20512 | tf_op jit(solution)/shard_map/ppermute | solution.py:32
  134.1 10.0 %collective-permute-done.9.gp = bf16[64,5120]{1,0:T(8,128)(2,1)S(1)} collective-permute-done((bf16[64,5120]{1,0:T(8,128)(2,1)S(1)}, bf16[64,5120]{1,0:T(8,128)(2,1)S(1)}, u32[]{:S(2)}, u32[]{:S(2)}) %collective-permute-start.9) | collective-permute-done | bytes 655392 | tf_op jit(solution)/shard_map/ppermute | solution.py:36
  145.0 9.8 %collective-permute-start.13 = (bf16[32,5120]{1,0:T(8,128)(2,1)S(1)}, bf16[32,5120]{1,0:T(8,128)(2,1)S(1)}, u32[]{:S(2)}, u32[]{:S(2)}) collective-permute-start(bf16[32,5120]{1,0:T(8,128)(2,1)S(1)} %slice.14), channel_id=1, source_target_pairs={{0,1},{1,2},{2,3},{3,0},{4,5},{5,6},{6,7},{7,4},{8,9},{9,10},{10,1... | collective-permute-start | bytes 983048 | tf_op jit(solution)/shard_map/ppermute | solution.py:36
  158.0 3.5 %collective-permute-done.16 = f32[40,128]{1,0:T(8,128)S(1)} collective-permute-done((f32[40,128]{1,0:T(8,128)S(1)}, f32[40,128]{1,0:T(8,128)S(1)}, u32[]{:S(2)}, u32[]{:S(2)}) %collective-permute-start.16) | collective-permute-done | bytes 20512 | tf_op jit(solution)/shard_map/ppermute | solution.py:32
  162.6 6.9 %grads_part.1 = (bf16[4,4,2,80,640]{4,3,2,1,0:T(8,128)(2,1)S(1)}, bf16[4,4,2,80,640]{4,3,2,1,0:T(8,128)(2,1)S(1)}, bf16[256,640]{1,0:T(8,128)(2,1)S(1)}) custom-call(s32[2]{0:T(128)S(1)} %pad_add_fusion.pos, bf16[64,5120]{1,0:T(8,128)(2,1)S(1)} %fusion.8.g0, bf16[64,5120]{1,0:T(8,128)(2,1)S(1)} %collective-permute-done.9.gp, ...), custom_call_target="tpu_custom_call" | custom-call | flops 3355443200 | bytes 15728640 | tf_op jit(solution)/shard_map/grads_part/pallas_call | solution.py:182
  169.5 10.0 %collective-permute-start.17 = (bf16[4,4,2,80,640]{4,3,2,1,0:T(8,128)(2,1)S(1)}, bf16[4,4,2,80,640]{4,3,2,1,0:T(8,128)(2,1)S(1)}, u32[]{:S(2)}, u32[]{:S(2)}) collective-permute-start(bf16[4,4,2,80,640]{4,3,2,1,0:T(8,128)(2,1)S(1)} %get-tuple-element.44), channel_id=1, source_target_pairs={{0,4},{4,0},{8,12},{12,8},{16,20},{20,16},{24,28},{28,24},{32,36},... | collective-permute-start | bytes 9830408 | tf_op jit(solution)/shard_map/ppermute | solution.py:32
  179.5 5.5 %collective-permute-done.17 = bf16[4,4,2,80,640]{4,3,2,1,0:T(8,128)(2,1)S(1)} collective-permute-done((bf16[4,4,2,80,640]{4,3,2,1,0:T(8,128)(2,1)S(1)}, bf16[4,4,2,80,640]{4,3,2,1,0:T(8,128)(2,1)S(1)}, u32[]{:S(2)}, u32[]{:S(2)}) %collective-permute-start.17) | collective-permute-done | bytes 3276832 | tf_op jit(solution)/shard_map/ppermute | solution.py:32
  185.0 2.6 %add_convert_fusion = bf16[4,4,2,80,640]{4,3,2,1,0:T(8,128)(2,1)} fusion(bf16[4,4,2,80,640]{4,3,2,1,0:T(8,128)(2,1)S(1)} %collective-permute-done.17, bf16[4,4,2,80,640]{4,3,2,1,0:T(8,128)(2,1)S(1)} %get-tuple-element.43), kind=kLoop, calls=%fused_computation.1 | loop fusion | flops 6553600 | bytes 9830400 | tf_op jit(solution)/shard_map/convert_element_type | solution.py:275
  187.6 4.8 %all-to-all-start.2 = ((bf16[4,4,2,80,640]{4,3,2,1,0:T(8,128)(2,1)}), bf16[4,4,2,80,640]{4,3,2,1,0:T(8,128)(2,1)}, u32[]{:S(2)}, u32[]{:S(2)}) async-start(bf16[4,4,2,80,640]{4,3,2,1,0:T(8,128)(2,1)} %add_convert_fusion), calls=%async_computation.2 | async-start | bytes 6553600 | tf_op jit(solution)/shard_map/all_to_all | solution.py:40
  192.5 2.8 %collective-permute-start.18 = (f32[40,128]{1,0:T(8,128)S(1)}, f32[40,128]{1,0:T(8,128)S(1)}, u32[]{:S(2)}, u32[]{:S(2)}) collective-permute-start(f32[40,128]{1,0:T(8,128)S(1)} %add.80), channel_id=1, source_target_pairs={{0,32},{4,36},{8,40},{12,44},{16,48},{20,52},{24,56},{28,60},{32,0... | collective-permute-start | bytes 61448 | tf_op jit(solution)/shard_map/ppermute | solution.py:32
  200.8 2.4 collective-permute-start.20
  203.3 4.0 %collective-permute-done.20 = f32[40,128]{1,0:T(8,128)S(1)} collective-permute-done((f32[40,128]{1,0:T(8,128)S(1)}, f32[40,128]{1,0:T(8,128)S(1)}, u32[]{:S(2)}, u32[]{:S(2)}) %collective-permute-start.20) | collective-permute-done | bytes 20512 | tf_op jit(solution)/shard_map/ppermute | solution.py:279
  207.3 7.2 %all-to-all-done.2 = bf16[4,4,2,80,640]{4,3,2,1,0:T(8,128)(2,1)} async-done(((bf16[4,4,2,80,640]{4,3,2,1,0:T(8,128)(2,1)}), bf16[4,4,2,80,640]{4,3,2,1,0:T(8,128)(2,1)}, u32[]{:S(2)}, u32[]{:S(2)}) %all-to-all-start.2) | async-done | bytes 3276832 | tf_op jit(solution)/shard_map/all_to_all | solution.py:40
  214.5 3.5 %reduce_sum.71 = bf16[4,2,80,640]{3,2,1,0:T(8,128)(2,1)} reduce(bf16[4,4,2,80,640]{4,3,2,1,0:T(8,128)(2,1)} %all-to-all-done.2, bf16[]{:T(256)} %constant.63.clone.1), dimensions={0}, to_apply=%region_6.7 | reduce | flops 1228800 | bytes 4096002 | tf_op jit(solution)/shard_map/reduce_sum | solution.py:281
  218.0 3.5 %all-to-all-start.3 = ((bf16[4,2,80,640]{3,2,1,0:T(8,128)(2,1)}), bf16[4,2,80,640]{3,2,1,0:T(8,128)(2,1)S(1)}, u32[]{:S(2)}, u32[]{:S(2)}) async-start(bf16[4,2,80,640]{3,2,1,0:T(8,128)(2,1)} %reduce_sum.71), calls=%async_computation.3 | async-start | bytes 1638400 | tf_op jit(solution)/shard_map/all_to_all | solution.py:40
  227.0 3.3 %all-to-all-done.3 = bf16[4,2,80,640]{3,2,1,0:T(8,128)(2,1)S(1)} async-done(((bf16[4,2,80,640]{3,2,1,0:T(8,128)(2,1)}), bf16[4,2,80,640]{3,2,1,0:T(8,128)(2,1)S(1)}, u32[]{:S(2)}, u32[]{:S(2)}) %all-to-all-start.3) | async-done | bytes 819232 | tf_op jit(solution)/shard_map/all_to_all | solution.py:40
  230.5 2.8 %collective-permute-start.21 = (bf16[80,640]{1,0:T(8,128)(2,1)S(1)}, bf16[80,640]{1,0:T(8,128)(2,1)S(1)}, u32[]{:S(2)}, u32[]{:S(2)}) collective-permute-start(bf16[80,640]{1,0:T(8,128)(2,1)S(1)} %fusion.16), channel_id=1, source_target_pairs={{0,32},{4,36},{8,40},{12,44},{16,48},{20,52},{24,56},{28,60},{32,0... | collective-permute-start | bytes 307208 | tf_op jit(solution)/shard_map/ppermute | solution.py:32
  (86 shorter events, 44.2 us)
Async XLA Ops:
  0.6 4.8 %collective-permute-start = (bf16[80,640]{1,0:T(8,128)(2,1)}, bf16[80,640]{1,0:T(8,128)(2,1)S(1)}, u32[]{:S(2)}, u32[]{:S(2)}) collective-permute-start(bf16[80,640]{1,0:T(8,128)(2,1)} %param.13), channel_id=1, source_target_pairs={{0,32},{4,36},{8,40},{12,44},{16,48},{20,52},{24,56},{28,60},{32,0... | collective-permute-start | bytes 307208 | tf_op jit(solution)/shard_map/ppermute | solution.py:32
  21.5 26.0 %all-to-all-start.1 = ((bf16[4,4,2,80,640]{4,3,2,1,0:T(8,128)(2,1)}), bf16[4,4,2,80,640]{4,3,2,1,0:T(8,128)(2,1)S(1)}, u32[]{:S(2)}, u32[]{:S(2)}) async-start(bf16[4,4,2,80,640]{4,3,2,1,0:T(8,128)(2,1)} %broadcast_in_dim.15), calls=%async_computation.1 | async-start | bytes 6553600 | tf_op jit(solution)/shard_map/all_to_all | solution.py:40
  25.5 5.6 %copy-start.9 = (s32[256]{0:T(256)S(1)}, s32[256]{0:T(256)}, u32[]{:S(2)}) copy-start(s32[256]{0:T(256)} %param.15) | copy-start | bytes 3076
  47.5 9.4 %collective-permute-start.1 = (bf16[4,4,2,80,640]{4,3,2,1,0:T(8,128)(2,1)S(1)}, bf16[4,4,2,80,640]{4,3,2,1,0:T(8,128)(2,1)}, u32[]{:S(2)}, u32[]{:S(2)}) collective-permute-start(bf16[4,4,2,80,640]{4,3,2,1,0:T(8,128)(2,1)S(1)} %all-to-all-done.1.refs_0_.refs_1_.refs_2_.refs_3_), channel_id=1, source_target_pairs={{0,4},{4,0},{8,12},{12,8},{16,20},{20,16},{24,28},{28,24},{32,36},... | collective-permute-start | bytes 9830408 | tf_op jit(solution)/shard_map/ppermute | solution.py:32
  65.1 55.2 %copy-start.6 = (bf16[64,5120]{1,0:T(8,128)(2,1)S(1)}, bf16[64,5120]{1,0:T(8,128)(2,1)}, u32[]{:S(2)}) copy-start(bf16[64,5120]{1,0:T(8,128)(2,1)} %param.11) | copy-start | bytes 1966084
  65.1 15.7 %collective-permute-start.2 = (bf16[32,5120]{1,0:T(8,128)(2,1)S(1)}, bf16[32,5120]{1,0:T(8,128)(2,1)S(1)}, u32[]{:S(2)}, u32[]{:S(2)}) collective-permute-start(bf16[32,5120]{1,0:T(8,128)(2,1)S(1)} %get-tuple-element.31), channel_id=1, source_target_pairs={{0,1},{1,2},{2,3},{3,0},{4,5},{5,6},{6,7},{7,4},{8,9},{9,10},{10,1... | collective-permute-start | bytes 983048 | tf_op jit(solution)/shard_map/ppermute | solution.py:36
  68.1 36.4 %collective-permute-start.4 = (bf16[32,5120]{1,0:T(8,128)(2,1)S(1)}, bf16[32,5120]{1,0:T(8,128)(2,1)S(1)}, u32[]{:S(2)}, u32[]{:S(2)}) collective-permute-start(bf16[32,5120]{1,0:T(8,128)(2,1)S(1)} %get-tuple-element.32), channel_id=1, source_target_pairs={{0,1},{1,2},{2,3},{3,0},{4,5},{5,6},{6,7},{7,4},{8,9},{9,10},{10,1... | collective-permute-start | bytes 983048 | tf_op jit(solution)/shard_map/ppermute | solution.py:36
  72.2 32.3 %collective-permute-start.5 = (bf16[32,5120]{1,0:T(8,128)(2,1)S(1)}, bf16[32,5120]{1,0:T(8,128)(2,1)S(1)}, u32[]{:S(2)}, u32[]{:S(2)}) collective-permute-start(bf16[32,5120]{1,0:T(8,128)(2,1)S(1)} %get-tuple-element.33), channel_id=1, source_target_pairs={{0,3},{1,0},{2,1},{3,2},{4,7},{5,4},{6,5},{7,6},{8,11},{9,8},{10,9... | collective-permute-start | bytes 983048 | tf_op jit(solution)/shard_map/ppermute | solution.py:36
  72.2 31.1 %collective-permute-start.6 = (bf16[32,5120]{1,0:T(8,128)(2,1)S(1)}, bf16[32,5120]{1,0:T(8,128)(2,1)S(1)}, u32[]{:S(2)}, u32[]{:S(2)}) collective-permute-start(bf16[32,5120]{1,0:T(8,128)(2,1)S(1)} %get-tuple-element.35), channel_id=1, source_target_pairs={{0,3},{1,0},{2,1},{3,2},{4,7},{5,4},{6,5},{7,6},{8,11},{9,8},{10,9... | collective-permute-start | bytes 983048 | tf_op jit(solution)/shard_map/ppermute | solution.py:36
  80.9 23.6 %collective-permute-start.3 = (bf16[32,5120]{1,0:T(8,128)(2,1)S(1)}, bf16[32,5120]{1,0:T(8,128)(2,1)S(1)}, u32[]{:S(2)}, u32[]{:S(2)}) collective-permute-start(bf16[32,5120]{1,0:T(8,128)(2,1)S(1)} %add_convert_fusion.2), channel_id=1, source_target_pairs={{0,1},{1,2},{2,3},{3,0},{4,5},{5,6},{6,7},{7,4},{8,9},{9,10},{10,1... | collective-permute-start | bytes 983048 | tf_op jit(solution)/shard_map/ppermute | solution.py:36
  103.4 16.9 %collective-permute-start.7 = (bf16[32,5120]{1,0:T(8,128)(2,1)S(1)}, bf16[32,5120]{1,0:T(8,128)(2,1)S(1)}, u32[]{:S(2)}, u32[]{:S(2)}) collective-permute-start(bf16[32,5120]{1,0:T(8,128)(2,1)S(1)} %add_convert_fusion.1), channel_id=1, source_target_pairs={{0,3},{1,0},{2,1},{3,2},{4,7},{5,4},{6,5},{7,6},{8,11},{9,8},{10,9... | collective-permute-start | bytes 983048 | tf_op jit(solution)/shard_map/ppermute | solution.py:36
  122.3 47.2 %copy-start.1 = (bf16[64,5120]{1,0:T(8,128)(2,1)}, bf16[64,5120]{1,0:T(8,128)(2,1)S(1)}, u32[]{:S(2)}) copy-start(bf16[64,5120]{1,0:T(8,128)(2,1)S(1)} %fusion.8.g0) | copy-start | bytes 1966084
  122.3 21.8 %collective-permute-start.9 = (bf16[64,5120]{1,0:T(8,128)(2,1)S(1)}, bf16[64,5120]{1,0:T(8,128)(2,1)S(1)}, u32[]{:S(2)}, u32[]{:S(2)}) collective-permute-start(bf16[64,5120]{1,0:T(8,128)(2,1)S(1)} %fusion.8.g0), channel_id=1, source_target_pairs={{0,3},{1,0},{2,1},{3,2},{4,7},{5,4},{6,5},{7,6},{8,11},{9,8},{10,9... | collective-permute-start | bytes 1966088 | tf_op jit(solution)/shard_map/ppermute | solution.py:36
  123.2 21.8 %collective-permute-start.8 = (bf16[64,5120]{1,0:T(8,128)(2,1)S(1)}, bf16[64,5120]{1,0:T(8,128)(2,1)S(1)}, u32[]{:S(2)}, u32[]{:S(2)}) collective-permute-start(bf16[64,5120]{1,0:T(8,128)(2,1)S(1)} %fusion.8.g0), channel_id=1, source_target_pairs={{0,1},{1,2},{2,3},{3,0},{4,5},{5,6},{6,7},{7,4},{8,9},{9,10},{10,1... | collective-permute-start | bytes 1966088 | tf_op jit(solution)/shard_map/ppermute | solution.py:36
  124.7 1.9 collective-permute-start.10
  126.7 2.9 %collective-permute-start.11 = (f32[40,128]{1,0:T(8,128)S(1)}, f32[40,128]{1,0:T(8,128)S(1)}, u32[]{:S(2)}, u32[]{:S(2)}) collective-permute-start(f32[40,128]{1,0:T(8,128)S(1)} %bitcast_add_fusion.1), channel_id=1, source_target_pairs={{0,8},{4,12},{8,0},{12,4},{16,24},{20,28},{24,16},{28,20},{32,40},... | collective-permute-start | bytes 61448 | tf_op jit(solution)/shard_map/ppermute | solution.py:32
  129.6 4.4 %collective-permute-start.12 = (f32[40,128]{1,0:T(8,128)S(1)}, f32[40,128]{1,0:T(8,128)S(1)}, u32[]{:S(2)}, u32[]{:S(2)}) collective-permute-start(f32[40,128]{1,0:T(8,128)S(1)} %fusion.31), channel_id=1, source_target_pairs={{0,16},{4,20},{8,24},{12,28},{16,0},{20,4},{24,8},{28,12},{32,48},... | collective-permute-start | bytes 61448 | tf_op jit(solution)/shard_map/ppermute | solution.py:32
  145.0 17.5 %collective-permute-start.13 = (bf16[32,5120]{1,0:T(8,128)(2,1)S(1)}, bf16[32,5120]{1,0:T(8,128)(2,1)S(1)}, u32[]{:S(2)}, u32[]{:S(2)}) collective-permute-start(bf16[32,5120]{1,0:T(8,128)(2,1)S(1)} %slice.14), channel_id=1, source_target_pairs={{0,1},{1,2},{2,3},{3,0},{4,5},{5,6},{6,7},{7,4},{8,9},{9,10},{10,1... | collective-permute-start | bytes 983048 | tf_op jit(solution)/shard_map/ppermute | solution.py:36
  154.7 7.9 %collective-permute-start.14 = (bf16[32,5120]{1,0:T(8,128)(2,1)S(1)}, bf16[32,5120]{1,0:T(8,128)(2,1)S(1)}, u32[]{:S(2)}, u32[]{:S(2)}) collective-permute-start(bf16[32,5120]{1,0:T(8,128)(2,1)S(1)} %slice.15), channel_id=1, source_target_pairs={{0,3},{1,0},{2,1},{3,2},{4,7},{5,4},{6,5},{7,6},{8,11},{9,8},{10,9... | collective-permute-start | bytes 983048 | tf_op jit(solution)/shard_map/ppermute | solution.py:36
  154.8 2.6 %collective-permute-start.15 = (f32[40,128]{1,0:T(8,128)S(1)}, f32[40,128]{1,0:T(8,128)S(1)}, u32[]{:S(2)}, u32[]{:S(2)}) collective-permute-start(f32[40,128]{1,0:T(8,128)S(1)} %add.78), channel_id=1, source_target_pairs={{0,64},{4,68},{8,72},{12,76},{16,80},{20,84},{24,88},{28,92},{32,9... | collective-permute-start | bytes 61448 | tf_op jit(solution)/shard_map/ppermute | solution.py:32
  157.4 4.1 %collective-permute-start.16 = (f32[40,128]{1,0:T(8,128)S(1)}, f32[40,128]{1,0:T(8,128)S(1)}, u32[]{:S(2)}, u32[]{:S(2)}) collective-permute-start(f32[40,128]{1,0:T(8,128)S(1)} %add.79), channel_id=1, source_target_pairs={{0,128},{4,132},{8,136},{12,140},{16,144},{20,148},{24,152},{28,15... | collective-permute-start | bytes 61448 | tf_op jit(solution)/shard_map/ppermute | solution.py:32
  169.5 15.5 %collective-permute-start.17 = (bf16[4,4,2,80,640]{4,3,2,1,0:T(8,128)(2,1)S(1)}, bf16[4,4,2,80,640]{4,3,2,1,0:T(8,128)(2,1)S(1)}, u32[]{:S(2)}, u32[]{:S(2)}) collective-permute-start(bf16[4,4,2,80,640]{4,3,2,1,0:T(8,128)(2,1)S(1)} %get-tuple-element.44), channel_id=1, source_target_pairs={{0,4},{4,0},{8,12},{12,8},{16,20},{20,16},{24,28},{28,24},{32,36},... | collective-permute-start | bytes 9830408 | tf_op jit(solution)/shard_map/ppermute | solution.py:32
  187.6 10.8 %copy-start.3 = (f32[5,256,256]{1,2,0:T(8,128)S(1)}, f32[5,256,256]{1,2,0:T(8,128)}, u32[]{:S(2)}) copy-start(f32[5,256,256]{1,2,0:T(8,128)} %get-tuple-element.71) | copy-start | bytes 3932164
  187.6 10.8 %copy-start.7 = (bf16[256,640]{0,1:T(8,128)(2,1)S(1)}, bf16[256,640]{0,1:T(8,128)(2,1)}, u32[]{:S(2)}) copy-start(bf16[256,640]{0,1:T(8,128)(2,1)} %copy.51) | copy-start | bytes 983044
  187.6 26.8 %all-to-all-start.2 = ((bf16[4,4,2,80,640]{4,3,2,1,0:T(8,128)(2,1)}), bf16[4,4,2,80,640]{4,3,2,1,0:T(8,128)(2,1)}, u32[]{:S(2)}, u32[]{:S(2)}) async-start(bf16[4,4,2,80,640]{4,3,2,1,0:T(8,128)(2,1)} %add_convert_fusion), calls=%async_computation.2 | async-start | bytes 6553600 | tf_op jit(solution)/shard_map/all_to_all | solution.py:40
  192.5 4.4 %collective-permute-start.18 = (f32[40,128]{1,0:T(8,128)S(1)}, f32[40,128]{1,0:T(8,128)S(1)}, u32[]{:S(2)}, u32[]{:S(2)}) collective-permute-start(f32[40,128]{1,0:T(8,128)S(1)} %add.80), channel_id=1, source_target_pairs={{0,32},{4,36},{8,40},{12,44},{16,48},{20,52},{24,56},{28,60},{32,0... | collective-permute-start | bytes 61448 | tf_op jit(solution)/shard_map/ppermute | solution.py:32
  196.8 3.9 %collective-permute-start.19 = (f32[40,128]{1,0:T(8,128)S(1)}, f32[40,128]{1,0:T(8,128)S(1)}, u32[]{:S(2)}, u32[]{:S(2)}) collective-permute-start(f32[40,128]{1,0:T(8,128)S(1)} %add.82), channel_id=1, source_target_pairs={{0,1},{1,0},{2,3},{3,2},{4,5},{5,4},{6,7},{7,6},{8,9},{9,8},{10,11... | collective-permute-start | bytes 61448 | tf_op jit(solution)/shard_map/ppermute | solution.py:279
  200.8 6.5 %collective-permute-start.20 = (f32[40,128]{1,0:T(8,128)S(1)}, f32[40,128]{1,0:T(8,128)S(1)}, u32[]{:S(2)}, u32[]{:S(2)}) collective-permute-start(f32[40,128]{1,0:T(8,128)S(1)} %add.83), channel_id=1, source_target_pairs={{0,2},{1,3},{2,0},{3,1},{4,6},{5,7},{6,4},{7,5},{8,10},{9,11},{10,... | collective-permute-start | bytes 61448 | tf_op jit(solution)/shard_map/ppermute | solution.py:279
  218.0 12.3 %all-to-all-start.3 = ((bf16[4,2,80,640]{3,2,1,0:T(8,128)(2,1)}), bf16[4,2,80,640]{3,2,1,0:T(8,128)(2,1)S(1)}, u32[]{:S(2)}, u32[]{:S(2)}) async-start(bf16[4,2,80,640]{3,2,1,0:T(8,128)(2,1)} %reduce_sum.71), calls=%async_computation.3 | async-start | bytes 1638400 | tf_op jit(solution)/shard_map/all_to_all | solution.py:40
  221.5 3.0 %copy-start.5 = (bf16[256,640]{0,1:T(8,128)(2,1)S(1)}, bf16[256,640]{0,1:T(8,128)(2,1)}, u32[]{:S(2)}) copy-start(bf16[256,640]{0,1:T(8,128)(2,1)} %copy.48) | copy-start | bytes 983044
  222.6 3.1 %copy-start.4 = (bf16[256,640]{0,1:T(8,128)(2,1)S(1)}, bf16[256,640]{0,1:T(8,128)(2,1)}, u32[]{:S(2)}) copy-start(bf16[256,640]{0,1:T(8,128)(2,1)} %copy.47) | copy-start | bytes 983044
  230.5 4.8 %collective-permute-start.21 = (bf16[80,640]{1,0:T(8,128)(2,1)S(1)}, bf16[80,640]{1,0:T(8,128)(2,1)S(1)}, u32[]{:S(2)}, u32[]{:S(2)}) collective-permute-start(bf16[80,640]{1,0:T(8,128)(2,1)S(1)} %fusion.16), channel_id=1, source_target_pairs={{0,32},{4,36},{8,40},{12,44},{16,48},{20,52},{24,56},{28,60},{32,0... | collective-permute-start | bytes 307208 | tf_op jit(solution)/shard_map/ppermute | solution.py:32
  (3 other events, 3.1 us)

commit v4 on v3

v4 whole, which is shorter than its diff:
```python
import math

import jax
import jax.numpy as jnp
from jax import lax
from jax.experimental import pallas as pl
from jax.experimental.pallas import tpu as pltpu
from jax.sharding import PartitionSpec as P

HD = 128
BF = jnp.bfloat16
F32 = jnp.float32
VMEM_LIMIT = 40 * 1024 * 1024


def rings(along_y):
    groups = []
    for c in range(2):
        for w in range(2):
            for line in range(4):
                places = [(line, k) if (c == 0) == along_y else (k, line) for k in range(4)]
                groups.append([((x * 2 + w) * 4 + y) * 2 + c for x, y in places])
    return groups


FAR = rings(False)
NEAR = [
    [i ^ flip for i in group for flip in (0, 8)] for group in rings(True) if not group[0] & 8
]
FLIP_C = [(i, i ^ 1) for i in range(64)]


def swap(value, pairs):
    return lax.ppermute(value, "dp", pairs)


def send_mp(value, step):
    return lax.ppermute(value, "mp", [(i, (i + step) % 4) for i in range(4)])


def exchange(blocks, groups):
    return lax.all_to_all(blocks, "dp", 0, 0, axis_index_groups=groups)


def spread(block, copies):
    return jnp.broadcast_to(block[None], (copies, *block.shape))


def attention_probs(query3, key3, doc_ids):
    seq = query3.shape[0]
    scale = 1.0 / math.sqrt(HD)
    scores = jnp.einsum("thd,shd->hts", query3, key3, preferred_element_type=F32) * scale
    pos = lax.iota(jnp.int32, seq)
    allowed = (pos[None, :] <= pos[:, None]) & (doc_ids[None, :] == doc_ids[:, None])
    scores = jnp.where(allowed[None], scores, -1e30)
    top = jnp.max(scores, axis=2, keepdims=True)
    weights = jnp.exp(scores - top)
    return weights / jnp.sum(weights, axis=2, keepdims=True)


def turn_tokens(pos, att_ref, att_s):
    rows = att_ref.shape[0] // 4
    for k in range(4):
        start = pl.multiple_of(((pos[1] + k) % 4) * rows, 16)
        att_s[pl.ds(k * rows, rows), :] = att_ref[pl.ds(start, rows), :]


def place(c, x, y):
    return jnp.where(c == 0, x, y), jnp.where(c == 0, y, x)


def assemble(c, mine, other, w_s):
    piece = mine[0].shape[3]
    for w in range(2):
        for y in range(4):
            i = 2 * (w * 4 + y)
            w_s[pl.ds(pl.multiple_of((i + c) * piece, 16), piece), :] = mine[y][0, 0, w]
            w_s[pl.ds(pl.multiple_of((i + 1 - c) * piece, 16), piece), :] = other[y][0, 0, w]


def weight_specs(piece, width):
    def block(flip, y):
        def at(i, pos):
            return *place(pos[0] ^ flip, i, y), 0, 0, 0

        return pl.BlockSpec((1, 1, 2, piece, width), at)

    return [block(flip, y) for flip in range(2) for y in range(4)]


def branch_kernel(pos, att_ref, *refs):
    p0, p1a, p3b, up, down, att_s, w_s = refs[8:]
    rows = att_ref.shape[0] // 4
    half = rows // 2

    @pl.when(pl.program_id(0) == 0)
    def _():
        turn_tokens(pos, att_ref, att_s)

    assemble(pos[0], refs[:4], refs[4:8], w_s)
    prod = lax.dot_general(
        att_s[...], w_s[...], (((1,), (1,)), ((), ())), preferred_element_type=F32
    ).astype(BF)
    p0[...] = prod[:rows]
    p1a[...] = prod[rows : rows + half]
    p3b[...] = prod[3 * rows + half :]
    up[pl.ds(0, half), :] = prod[2 * rows : 2 * rows + half]
    up[pl.ds(half, half), :] = prod[rows + half : 2 * rows]
    down[pl.ds(0, half), :] = prod[2 * rows + half : 3 * rows]
    down[pl.ds(half, half), :] = prod[3 * rows : 3 * rows + half]


def branch_part(pos, attended, cat, oth):
    piece, width = cat.shape[3:]
    seq = attended.shape[0]
    rows, span = seq // 4, 16 * piece
    total = 4 * span
    heights = (rows, rows // 2, rows // 2, rows, rows)
    return pl.pallas_call(
        branch_kernel,
        grid_spec=pltpu.PrefetchScalarGridSpec(
            num_scalar_prefetch=1,
            grid=(4,),
            in_specs=[pl.BlockSpec((seq, width), lambda i, pos: (0, 0))]
            + weight_specs(piece, width),
            out_specs=[pl.BlockSpec((h, span), lambda i, pos: (0, i)) for h in heights],
            scratch_shapes=[pltpu.VMEM((seq, width), BF), pltpu.VMEM((span, width), BF)],
        ),
        out_shape=[jax.ShapeDtypeStruct((h, total), BF) for h in heights],
        compiler_params=pltpu.CompilerParams(vmem_limit_bytes=VMEM_LIMIT),
        cost_estimate=pl.CostEstimate(
            flops=2 * seq * width * total,
            bytes_accessed=2 * (total * width + seq * total),
            transcendentals=0,
        ),
        name="branch_part",
    )(pos, attended, *[cat] * 4, *[oth] * 4)


def gather_rows(g0, gp, ga, gb, gm, rows_s):
    rows = g0.shape[0]
    half = rows // 2
    rows_s[pl.ds(0, rows), :] = g0[...]
    rows_s[pl.ds(rows, rows), :] = gp[...]
    rows_s[pl.ds(2 * rows, half), :] = ga[...]
    rows_s[pl.ds(2 * rows + half, half), :] = gb[...]
    rows_s[pl.ds(3 * rows, rows), :] = gm[...]


def weight_kernel(pos, g0, gp, ga, gb, gm, att_ref, keep, send, att_s, rows_s):
    piece = keep.shape[3]
    c = pos[0]
    step = pl.program_id(0)

    @pl.when(step == 0)
    def _():
        turn_tokens(pos, att_ref, att_s)

    gather_rows(g0, gp, ga, gb, gm, rows_s)
    prod = lax.dot_general(
        rows_s[...], att_s[...], (((0,), (0,)), ((), ())), preferred_element_type=F32
    ).astype(BF)
    for w in range(2):
        for y in range(4):
            i = 2 * (w * 4 + y)
            even = prod[i * piece : (i + 1) * piece]
            odd = prod[(i + 1) * piece : (i + 2) * piece]
            far, near = place(c, step, y)
            keep[far, near, w] = jnp.where(c == 0, even, odd)
            send[near, far, w] = jnp.where(c == 0, odd, even)


def weight_part(pos, parts, attended, piece):
    seq, width = attended.shape
    span = 16 * piece
    shape = (4, 4, 2, piece, width)
    block = pl.BlockSpec(shape, lambda i: (0, 0, 0, 0, 0))
    return pl.pallas_call(
        weight_kernel,
        grid=(4,),
        in_specs=[pl.BlockSpec(memory_space=pltpu.SMEM)]
        + [pl.BlockSpec((g.shape[0], span), lambda i: (0, i)) for g in parts]
        + [pl.BlockSpec((seq, width), lambda i: (0, 0))],
        out_specs=[block, block],
        out_shape=[jax.ShapeDtypeStruct(shape, BF)] * 2,
        scratch_shapes=[pltpu.VMEM((seq, width), BF), pltpu.VMEM((seq, span), BF)],
        compiler_params=pltpu.CompilerParams(vmem_limit_bytes=VMEM_LIMIT),
        cost_estimate=pl.CostEstimate(
            flops=8 * seq * width * span,
            bytes_accessed=8 * (span * width + seq * span),
            transcendentals=0,
        ),
        name="weight_part",
    )(pos, *parts, attended)


def attended_kernel(pos, g0, gp, ga, gb, gm, *refs):
    out_ref, rows_s, w_s, acc = refs[8:]
    m = pos[1]
    rows = g0.shape[0]
    step = pl.program_id(0)

    @pl.when(step == 0)
    def _():
        acc[...] = jnp.zeros_like(acc)

    gather_rows(g0, gp, ga, gb, gm, rows_s)
    assemble(pos[0], refs[:4], refs[4:8], w_s)
    acc[...] += jnp.dot(rows_s[...], w_s[...], preferred_element_type=F32)

    @pl.when(step == pl.num_programs(0) - 1)
    def _():
        for k in range(4):
            start = pl.multiple_of(((m + k) % 4) * rows, 16)
            out_ref[pl.ds(start, rows), :] = acc[pl.ds(k * rows, rows), :].astype(BF)


def attended_part(pos, parts, cat, oth):
    piece, width = cat.shape[3:]
    seq = 4 * parts[0].shape[0]
    span = 16 * piece
    return pl.pallas_call(
        attended_kernel,
        grid_spec=pltpu.PrefetchScalarGridSpec(
            num_scalar_prefetch=1,
            grid=(4,),
            in_specs=[pl.BlockSpec((g.shape[0], span), lambda i, pos: (0, i)) for g in parts]
            + weight_specs(piece, width),
            out_specs=pl.BlockSpec((seq, width), lambda i, pos: (0, 0)),
            scratch_shapes=[
                pltpu.VMEM((seq, span), BF),
                pltpu.VMEM((span, width), BF),
                pltpu.VMEM((seq, width), F32),
            ],
        ),
        out_shape=jax.ShapeDtypeStruct((seq, width), BF),
        compiler_params=pltpu.CompilerParams(vmem_limit_bytes=VMEM_LIMIT),
        cost_estimate=pl.CostEstimate(
            flops=8 * seq * width * span,
            bytes_accessed=8 * (span * width + seq * span),
            transcendentals=0,
        ),
        name="attended_part",
    )(pos, *parts, *[cat] * 4, *[oth] * 4)


def sum_f32(*parts):
    total = parts[0].astype(F32)
    for part in parts[1:]:
        total = total + part.astype(F32)
    return total


def on_device(query, key, value, residual, cotangent, out_weight, norm_gain, doc_ids):
    seq, width = query.shape
    heads = width // HD
    piece = out_weight.shape[0]
    rows, d_model = residual.shape
    half = rows // 2
    scale = 1.0 / math.sqrt(HD)
    dp = lax.axis_index("dp")
    c = dp % 2
    m = lax.axis_index("mp")
    pos = jnp.stack([c, m]).astype(jnp.int32)

    planes = exchange(spread(out_weight, 8), NEAR).reshape(4, 2, piece, width)
    cat = exchange(spread(planes, 4), FAR)

    query3 = query.reshape(seq, heads, HD)
    key3 = key.reshape(seq, heads, HD)
    value3 = value.reshape(seq, heads, HD)
    probs = attention_probs(query3, key3, doc_ids)
    probs_b = probs.astype(BF)
    attended = jnp.einsum("hts,shd->thd", probs_b, value3, preferred_element_type=F32)
    attended = attended.astype(BF).reshape(seq, width)

    cat, attended = lax.optimization_barrier((cat, attended))
    oth = swap(cat, FLIP_C)
    p0, p1a, p3b, up, down = branch_part(pos, attended, cat, oth)
    up, down = send_mp(up, 1), send_mp(down, -1)
    up_a = send_mp(sum_f32(p1a, up[:half]).astype(BF), 1)
    down_b = send_mp(sum_f32(p3b, down[:half]).astype(BF), -1)
    up = jnp.concatenate([up_a, up[half:]])
    down = jnp.concatenate([down[half:], down_b])
    mixed = sum_f32(residual, p0, up, down)
    cot = cotangent.astype(F32)
    gscaled = cot * norm_gain
    inv = lax.rsqrt(jnp.mean(mixed * mixed, axis=1, keepdims=True) + 1e-05)
    mean_dot = jnp.mean(gscaled * mixed, axis=1, keepdims=True)
    grad_residual = (inv * (gscaled - mixed * inv * inv * mean_dot)).astype(BF)

    tie = lax.optimization_barrier

    def add_from(total, bits):
        for bit in bits:
            total = total + swap(total, [(i, i ^ bit) for i in range(64)])
        return total

    gain = jnp.sum(cot * mixed * inv, axis=0).reshape(d_model // 128, 128)
    gm = send_mp(grad_residual, 1)
    gp = send_mp(grad_residual, -1)
    gm, gp, gain = tie((gm, gp, add_from(gain, (1, 2, 4))))
    ga = send_mp(gm[:half], 1)
    gb = send_mp(gp[half:], -1)
    ga, gb, gain = tie((ga, gb, add_from(gain, (16, 32))))
    parts = (grad_residual, gp, ga, gb, gm)
    keep, send = weight_part(pos, parts, attended, piece)
    both = sum_f32(keep, swap(send, FLIP_C)).astype(BF)
    grad_attended = attended_part(pos, parts, cat, oth)
    part = exchange(both, FAR)
    gain = add_from(gain, (8,))
    for bit in (1, 2):
        gain = gain + lax.ppermute(gain, "mp", [(i, i ^ bit) for i in range(4)])
    part, gain = tie((part, gain))
    part = sum_f32(*part).astype(BF).reshape(8, piece, width)
    grad_weight = sum_f32(*exchange(part, NEAR)) / 64
    grad_gain = lax.dynamic_slice_in_dim(gain.reshape(d_model) / 64, dp * piece, piece, 0)

    grad3 = grad_attended.reshape(seq, heads, HD)
    grad_value = jnp.einsum("hts,thd->shd", probs_b, grad3, preferred_element_type=F32)
    grad_value = grad_value.astype(BF).reshape(seq, width)
    grad_probs = jnp.einsum("thd,shd->hts", grad3, value3, preferred_element_type=F32)
    delta = jnp.sum(probs * grad_probs, axis=2, keepdims=True)
    grad_scores = (probs * (grad_probs - delta)).astype(BF)
    grad_query = jnp.einsum("hts,shd->thd", grad_scores, key3, preferred_element_type=F32) * scale
    grad_key = jnp.einsum("hts,thd->shd", grad_scores, query3, preferred_element_type=F32) * scale
    grad_query = grad_query.astype(BF).reshape(seq, width)
    grad_key = grad_key.astype(BF).reshape(seq, width)
    return (grad_query, grad_key, grad_value, grad_residual, grad_weight, grad_gain)


def solution(mesh):
    placed = (
        P("dp", "mp"),
        P("dp", "mp"),
        P("dp", "mp"),
        P(("dp", "mp"), None),
        P(("dp", "mp"), None),
        P("dp", "mp"),
        P(),
        P("dp"),
    )
    return jax.shard_map(
        on_device,
        mesh=mesh,
        in_specs=placed,
        out_specs=(
            P("dp", "mp"),
            P("dp", "mp"),
            P("dp", "mp"),
            P(("dp", "mp"), None),
            P("dp", "mp"),
            P("dp"),
        ),
        check_vma=False,
    )
```

time: 238 us -> 232 us (0.975); the launches traced: 236 us -> 227 us
  waiting for transfers between devices: 111 us -> 80.4 us
  starting transfers between devices: 63.9 us -> 74 us
  local copies, waits for them, and re-layouts: 15.6 us -> 23.2 us
  blocking collectives: 13 us -> 18.1 us
    ppermute x10 -> x8, starting transfers between devices: 25 us -> 41.8 us  [swap(): return lax.ppermute(value, 'dp', pairs)]
    ppermute x10 -> x8, waiting for transfers between devices: 56.6 us -> 42.8 us  [send_mp(): return lax.ppermute(value, 'mp', [(i, (i + step) % 4) for i in range(4)])]
    ppermute x10 -> x8, starting transfers between devices: 22.6 us -> 14.3 us  [send_mp(): return lax.ppermute(value, 'mp', [(i, (i + step) % 4) for i in range(4)])]
    all_to_all x3, waiting for transfers between devices: 21.6 us -> 14.9 us  [exchange(): return lax.all_to_all(blocks, 'dp', 0, 0, axis_index_groups=groups)]
    ppermute x10 -> x8, waiting for transfers between devices: 27.3 us -> 21.1 us  [swap(): return lax.ppermute(value, 'dp', pairs)]
    unnamed x26 -> x48, local copies, waits for them, and re-layouts: 10.9 us -> 16.6 us
    all_to_all x1, blocking collectives: 13 us -> 18.1 us  [exchange(): return lax.all_to_all(blocks, 'dp', 0, 0, axis_index_groups=groups)]
    ppermute x2, waiting for transfers between devices: 5.91 us -> 1.71 us  [on_device(): gain = gain + lax.ppermute(gain, 'mp', [(i, i ^ bit) for i in range(4)])]
  transfers between devices with their start and end apart: 25 -> 21, of which waited for: 22 -> 15; matrix products, arithmetic and copies ran while one was open for 8% -> 8% of each run, Pallas kernels for 0% -> 3%
where the time goes in v4:
time: 232 us; the launch traced here: 227 us
  waiting for transfers between devices  80.4 us (35%)
  starting transfers between devices  74 us (32%)
  local copies, waits for them, and re-layouts  23.2 us (10%)
  blocking collectives  18.1 us (8%)
  Pallas kernels  15.6 us (7%)
  other arithmetic  8.56 us (4%)
  matrix products  6.56 us (3%)
    ppermute x8, waiting for transfers between devices, send_mp(): return lax.ppermute(value, 'mp', [(i, (i + step) % 4) for i in range(4)])  42.8 us
    ppermute x8, starting transfers between devices, swap(): return lax.ppermute(value, 'dp', pairs)  41.8 us
    ppermute x8, waiting for transfers between devices, swap(): return lax.ppermute(value, 'dp', pairs)  21.1 us
    all_to_all x1, blocking collectives, exchange(): return lax.all_to_all(blocks, 'dp', 0, 0, axis_index_groups=groups)  18.1 us
    unnamed x48, local copies, waits for them, and re-layouts  16.6 us
    all_to_all x3, waiting for transfers between devices, exchange(): return lax.all_to_all(blocks, 'dp', 0, 0, axis_index_groups=groups)  14.9 us
    ppermute x8, starting transfers between devices, send_mp(): return lax.ppermute(value, 'mp', [(i, (i + step) % 4) for i in range(4)])  14.3 us
    all_to_all x3, starting transfers between devices, exchange(): return lax.all_to_all(blocks, 'dp', 0, 0, axis_index_groups=groups)  12.6 us
  transfers between devices with their start and end apart: 21, of which 15 were waited for; matrix products, arithmetic and copies ran while one was open for 8% of the time, Pallas kernels for 3%

profile of v4, /device:TPU:1, one launch (start us, length us, event | category | flops | bytes accessed | tf_op | source)
XLA Modules:
  0.0 227.5 jit_solution(12287402658558290342)
XLA Ops:
  1.6 18.1 %all_to_all.20 = bf16[8,80,640]{2,1,0:T(8,128)(2,1)S(1)} all-to-all(bf16[8,80,640]{2,1,0:T(8,128)(2,1)S(1)} %broadcast_in_dim.20), channel_id=1, replica_groups={{0,32,8,40,16,48,24,56},{64,96,72,104,80,112,88,120},{128,160,136,168,1..., dimensions={0} | all-to-all | bytes 1638400 | tf_op jit(solution)/shard_map/all_to_all | solution.py:42
  21.6 4.3 %all-to-all-start.1 = ((bf16[4,4,2,80,640]{4,3,2,1,0:T(8,128)(2,1)}), bf16[4,4,2,80,640]{4,3,2,1,0:T(8,128)(2,1)S(1)}, u32[]{:S(2)}, u32[]{:S(2)}) async-start(bf16[4,4,2,80,640]{4,3,2,1,0:T(8,128)(2,1)} %broadcast_in_dim.22), calls=%async_computation.1 | async-start | bytes 6553600 | tf_op jit(solution)/shard_map/all_to_all | solution.py:42
  31.6 2.7 %fusion.19 = (f32[5,256]{1,0:T(8,128)S(1)}, f32[5,256,256]{1,2,0:T(8,128)}) fusion(bf16[256,5,128]{0,2,1:T(8,128)(2,1)} %bitcast.39, bf16[256,5,128]{0,2,1:T(8,128)(2,1)} %bitcast.41, pred[256,256]{0,1:T(8,128)(4,1)S(1)} %fusion.15), kind=kOutput, calls=%fused_computation.42 | convolution fusion | flops 85197056 | bytes 2036736 | tf_op jit(solution)/shard_map/sub | solution.py:57
  34.4 2.4 %convolution_convert_fusion = bf16[5,256,128]{1,2,0:T(8,128)(2,1)} fusion(bf16[256,5,128]{0,2,1:T(8,128)(2,1)} %bitcast.45, f32[5,256,256]{1,2,0:T(8,128)} %get-tuple-element.57, f32[5,256]{1,0:T(8,128)S(1)} %get-tuple-element.56), kind=kOutput, calls=%fused_computation.24 | convolution fusion | flops 84705280 | bytes 1971200 | tf_op jit(solution)/shard_map/hts,shd->thd/dot_general | solution.py:274
  36.8 11.1 %all-to-all-done.1.refs_0_.refs_1_.refs_2_.refs_3_ = bf16[4,4,2,80,640]{4,3,2,1,0:T(8,128)(2,1)S(1)} async-done(((bf16[4,4,2,80,640]{4,3,2,1,0:T(8,128)(2,1)}), bf16[4,4,2,80,640]{4,3,2,1,0:T(8,128)(2,1)S(1)}, u32[]{:S(2)}, u32[]{:S(2)}) %all-to-all-start.1) | async-done | bytes 3276832 | tf_op jit(solution)/shard_map/all_to_all | solution.py:42
  47.9 3.4 %collective-permute-start = (bf16[4,4,2,80,640]{4,3,2,1,0:T(8,128)(2,1)S(1)}, bf16[4,4,2,80,640]{4,3,2,1,0:T(8,128)(2,1)}, u32[]{:S(2)}, u32[]{:S(2)}) collective-permute-start(bf16[4,4,2,80,640]{4,3,2,1,0:T(8,128)(2,1)S(1)} %all-to-all-done.1.refs_0_.refs_1_.refs_2_.refs_3_), channel_id=1, source_target_pairs={{0,4},{4,0},{8,12},{12,8},{16,20},{20,16},{24,28},{28,24},{32,36},... | collective-permute-start | bytes 9830408 | tf_op jit(solution)/shard_map/ppermute | solution.py:34
  53.2 3.6 %collective-permute-done.refs_4_.refs_5_.refs_6_.refs_7_ = bf16[4,4,2,80,640]{4,3,2,1,0:T(8,128)(2,1)} collective-permute-done((bf16[4,4,2,80,640]{4,3,2,1,0:T(8,128)(2,1)S(1)}, bf16[4,4,2,80,640]{4,3,2,1,0:T(8,128)(2,1)}, u32[]{:S(2)}, u32[]{:S(2)}) %collective-permute-start) | collective-permute-done | bytes 3276832 | tf_op jit(solution)/shard_map/ppermute | solution.py:34
  57.8 5.9 %branch_part.1 = (bf16[64,5120]{1,0:T(8,128)(2,1)S(1)}, bf16[32,5120]{1,0:T(8,128)(2,1)S(1)}, bf16[32,5120]{1,0:T(8,128)(2,1)S(1)}, bf16[64,5120]{1,0:T(8,128)(2,1)S(1)}, bf16[64,5120]{1,0:T(8,128)(2,1)S(1)}) custom-call(s32[2]{0:T(128)S(1)} %pad_add_fusion.pos, bf16[256,640]{1,0:T(8,128)(2,1)S(1)} %copy-done.7, ...), custom_call_target="tpu_custom_call" | custom-call | flops 1677721600 | bytes 9175040 | tf_op jit(solution)/shard_map/branch_part/pallas_call | solution.py:119
  63.8 3.1 %collective-permute-start.1 = (bf16[64,5120]{1,0:T(8,128)(2,1)S(1)}, bf16[64,5120]{1,0:T(8,128)(2,1)S(1)}, u32[]{:S(2)}, u32[]{:S(2)}) collective-permute-start(bf16[64,5120]{1,0:T(8,128)(2,1)S(1)} %get-tuple-element.27), channel_id=1, source_target_pairs={{0,1},{1,2},{2,3},{3,0},{4,5},{5,6},{6,7},{7,4},{8,9},{9,10},{10,1... | collective-permute-start | bytes 1966088 | tf_op jit(solution)/shard_map/ppermute | solution.py:38
  66.8 2.2 collective-permute-start.3
  69.1 29.0 %collective-permute-done.1 = bf16[64,5120]{1,0:T(8,128)(2,1)S(1)} collective-permute-done((bf16[64,5120]{1,0:T(8,128)(2,1)S(1)}, bf16[64,5120]{1,0:T(8,128)(2,1)S(1)}, u32[]{:S(2)}, u32[]{:S(2)}) %collective-permute-start.1) | collective-permute-done | bytes 655392 | tf_op jit(solution)/shard_map/ppermute | solution.py:38
  99.5 2.5 %collective-permute-start.4 = (bf16[32,5120]{1,0:T(8,128)(2,1)S(1)}, bf16[32,5120]{1,0:T(8,128)(2,1)S(1)}, u32[]{:S(2)}, u32[]{:S(2)}) collective-permute-start(bf16[32,5120]{1,0:T(8,128)(2,1)S(1)} %add_convert_fusion.2), channel_id=1, source_target_pairs={{0,3},{1,0},{2,1},{3,2},{4,7},{5,4},{6,5},{7,6},{8,11},{9,8},{10,9... | collective-permute-start | bytes 983048 | tf_op jit(solution)/shard_map/ppermute | solution.py:38
  102.0 12.5 %collective-permute-done.2 = bf16[32,5120]{1,0:T(8,128)(2,1)S(1)} collective-permute-done((bf16[32,5120]{1,0:T(8,128)(2,1)S(1)}, bf16[32,5120]{1,0:T(8,128)(2,1)S(1)}, u32[]{:S(2)}, u32[]{:S(2)}) %collective-permute-start.2) | collective-permute-done | bytes 327712 | tf_op jit(solution)/shard_map/ppermute | solution.py:38
  116.6 2.6 %collective-permute-start.6 = (bf16[64,5120]{1,0:T(8,128)(2,1)S(1)}, bf16[64,5120]{1,0:T(8,128)(2,1)S(1)}, u32[]{:S(2)}, u32[]{:S(2)}) collective-permute-start(bf16[64,5120]{1,0:T(8,128)(2,1)S(1)} %fusion.8.g0), channel_id=1, source_target_pairs={{0,3},{1,0},{2,1},{3,2},{4,7},{5,4},{6,5},{7,6},{8,11},{9,8},{10,9... | collective-permute-start | bytes 1966088 | tf_op jit(solution)/shard_map/ppermute | solution.py:38
  119.2 12.2 %collective-permute-start.7 = (f32[40,128]{1,0:T(8,128)S(1)}, f32[40,128]{1,0:T(8,128)S(1)}, u32[]{:S(2)}, u32[]{:S(2)}) collective-permute-start(f32[40,128]{1,0:T(8,128)S(1)} %bitcast.51), channel_id=1, source_target_pairs={{0,4},{4,0},{8,12},{12,8},{16,20},{20,16},{24,28},{28,24},{32,36},... | collective-permute-start | bytes 61448 | tf_op jit(solution)/shard_map/ppermute | solution.py:34
  132.2 7.0 %collective-permute-start.8 = (f32[40,128]{1,0:T(8,128)S(1)}, f32[40,128]{1,0:T(8,128)S(1)}, u32[]{:S(2)}, u32[]{:S(2)}) collective-permute-start(f32[40,128]{1,0:T(8,128)S(1)} %bitcast_add_fusion), channel_id=1, source_target_pairs={{0,8},{4,12},{8,0},{12,4},{16,24},{20,28},{24,16},{28,20},{32,40},... | collective-permute-start | bytes 61448 | tf_op jit(solution)/shard_map/ppermute | solution.py:34
  142.3 2.9 %collective-permute-done.9 = f32[40,128]{1,0:T(8,128)S(1)} collective-permute-done((f32[40,128]{1,0:T(8,128)S(1)}, f32[40,128]{1,0:T(8,128)S(1)}, u32[]{:S(2)}, u32[]{:S(2)}) %collective-permute-start.9) | collective-permute-done | bytes 20512 | tf_op jit(solution)/shard_map/ppermute | solution.py:34
  145.3 3.7 %collective-permute-start.10 = (bf16[32,5120]{1,0:T(8,128)(2,1)S(1)}, bf16[32,5120]{1,0:T(8,128)(2,1)S(1)}, u32[]{:S(2)}, u32[]{:S(2)}) collective-permute-start(bf16[32,5120]{1,0:T(8,128)(2,1)S(1)} %slice.22), channel_id=1, source_target_pairs={{0,1},{1,2},{2,3},{3,0},{4,5},{5,6},{6,7},{7,4},{8,9},{9,10},{10,1... | collective-permute-start | bytes 983048 | tf_op jit(solution)/shard_map/ppermute | solution.py:38
  149.1 12.6 %collective-permute-start.12 = (f32[40,128]{1,0:T(8,128)S(1)}, f32[40,128]{1,0:T(8,128)S(1)}, u32[]{:S(2)}, u32[]{:S(2)}) collective-permute-start(f32[40,128]{1,0:T(8,128)S(1)} %add.113), channel_id=1, source_target_pairs={{0,64},{4,68},{8,72},{12,76},{16,80},{20,84},{24,88},{28,92},{32,9... | collective-permute-start | bytes 61448 | tf_op jit(solution)/shard_map/ppermute | solution.py:34
  164.6 2.7 %collective-permute-done.13 = f32[40,128]{1,0:T(8,128)S(1)} collective-permute-done((f32[40,128]{1,0:T(8,128)S(1)}, f32[40,128]{1,0:T(8,128)S(1)}, u32[]{:S(2)}, u32[]{:S(2)}) %collective-permute-start.13) | collective-permute-done | bytes 20512 | tf_op jit(solution)/shard_map/ppermute | solution.py:34
  167.4 3.8 %weight_part.1 = (bf16[4,4,2,80,640]{4,3,2,1,0:T(8,128)(2,1)S(1)}, bf16[4,4,2,80,640]{4,3,2,1,0:T(8,128)(2,1)S(1)}) custom-call(s32[2]{0:T(128)S(1)} %pad_add_fusion.pos, bf16[64,5120]{1,0:T(8,128)(2,1)S(1)} %fusion.8.g0, bf16[64,5120]{1,0:T(8,128)(2,1)S(1)} %collective-permute-done.6.gp, bf16[32,5120]{1,0:T(8,128)(2,1)S(1)} %collective-permute-done.10.ga, ...), custom_call_target="tpu_custom_call" | custom-call | flops 1677721600 | bytes 9175040 | tf_op jit(solution)/shard_map/weight_part/pallas_call | solution.py:178
  171.2 3.5 %collective-permute-start.14 = (bf16[4,4,2,80,640]{4,3,2,1,0:T(8,128)(2,1)S(1)}, bf16[4,4,2,80,640]{4,3,2,1,0:T(8,128)(2,1)S(1)}, u32[]{:S(2)}, u32[]{:S(2)}) collective-permute-start(bf16[4,4,2,80,640]{4,3,2,1,0:T(8,128)(2,1)S(1)} %get-tuple-element.36), channel_id=1, source_target_pairs={{0,4},{4,0},{8,12},{12,8},{16,20},{20,16},{24,28},{28,24},{32,36},... | collective-permute-start | bytes 9830408 | tf_op jit(solution)/shard_map/ppermute | solution.py:34
  174.7 5.5 %collective-permute-done.14 = bf16[4,4,2,80,640]{4,3,2,1,0:T(8,128)(2,1)S(1)} collective-permute-done((bf16[4,4,2,80,640]{4,3,2,1,0:T(8,128)(2,1)S(1)}, bf16[4,4,2,80,640]{4,3,2,1,0:T(8,128)(2,1)S(1)}, u32[]{:S(2)}, u32[]{:S(2)}) %collective-permute-start.14) | collective-permute-done | bytes 3276832 | tf_op jit(solution)/shard_map/ppermute | solution.py:34
  180.2 2.6 %add_convert_fusion = bf16[4,4,2,80,640]{4,3,2,1,0:T(8,128)(2,1)} fusion(bf16[4,4,2,80,640]{4,3,2,1,0:T(8,128)(2,1)S(1)} %collective-permute-done.14, bf16[4,4,2,80,640]{4,3,2,1,0:T(8,128)(2,1)S(1)} %get-tuple-element.35), kind=kLoop, calls=%fused_computation.1 | loop fusion | flops 6553600 | bytes 9830400 | tf_op jit(solution)/shard_map/convert_element_type | solution.py:308
  182.8 4.7 %all-to-all-start.2 = ((bf16[4,4,2,80,640]{4,3,2,1,0:T(8,128)(2,1)}), bf16[4,4,2,80,640]{4,3,2,1,0:T(8,128)(2,1)}, u32[]{:S(2)}, u32[]{:S(2)}) async-start(bf16[4,4,2,80,640]{4,3,2,1,0:T(8,128)(2,1)} %add_convert_fusion), calls=%async_computation.2 | async-start | bytes 6553600 | tf_op jit(solution)/shard_map/all_to_all | solution.py:42
  187.6 2.6 %collective-permute-done.15 = f32[40,128]{1,0:T(8,128)S(1)} collective-permute-done((f32[40,128]{1,0:T(8,128)S(1)}, f32[40,128]{1,0:T(8,128)S(1)}, u32[]{:S(2)}, u32[]{:S(2)}) %collective-permute-start.15) | collective-permute-done | bytes 20512 | tf_op jit(solution)/shard_map/ppermute | solution.py:34
  190.2 2.2 collective-permute-start.16
  194.1 3.1 %collective-permute-start.17 = (f32[40,128]{1,0:T(8,128)S(1)}, f32[40,128]{1,0:T(8,128)S(1)}, u32[]{:S(2)}, u32[]{:S(2)}) collective-permute-start(f32[40,128]{1,0:T(8,128)S(1)} %add.118), channel_id=1, source_target_pairs={{0,2},{1,3},{2,0},{3,1},{4,6},{5,7},{6,4},{7,5},{8,10},{9,11},{10,... | collective-permute-start | bytes 61448 | tf_op jit(solution)/shard_map/ppermute | solution.py:313
  202.4 5.9 %attended_part.1 = bf16[256,640]{1,0:T(8,128)(2,1)S(1)} custom-call(s32[2]{0:T(128)S(1)} %pad_add_fusion.pos, bf16[64,5120]{1,0:T(8,128)(2,1)S(1)} %copy-done.1, bf16[64,5120]{1,0:T(8,128)(2,1)S(1)} %copy-done.3, bf16[32,5120]{1,0:T(8,128)(2,1)S(1)} %copy-done.10, bf16[32,5120]{1,0:T(8,128)(2,1)S(1)} %copy-done.12, bf16[64,5120]{1,0:T(8,128)(2,1)S(1)} %copy-done.5, ...), custom_call_target="tpu_custom_call" | custom-call | flops 1677721600 | bytes 9175040 | tf_op jit(solution)/shard_map/attended_part/pallas_call | solution.py:222
  210.2 3.2 %add_convert_fusion.1 = bf16[1,4,2,80,640]{4,3,2,1,0:T(8,128)(2,1)} fusion(bf16[4,4,2,80,640]{4,3,2,1,0:T(8,128)(2,1)} %all-to-all-done.2), kind=kLoop, calls=%fused_computation.2 | loop fusion | flops 3276800 | bytes 4096000 | tf_op jit(solution)/shard_map/convert.4
  213.4 3.7 %all-to-all-start.3 = ((bf16[8,80,640]{2,1,0:T(8,128)(2,1)}), bf16[8,80,640]{2,1,0:T(8,128)(2,1)S(1)}, u32[]{:S(2)}, u32[]{:S(2)}) async-start(bf16[8,80,640]{2,1,0:T(8,128)(2,1)} %bitcast.16), calls=%async_computation.3 | async-start | bytes 1638400 | tf_op jit(solution)/shard_map/all_to_all | solution.py:42
  222.8 3.8 %all-to-all-done.3 = bf16[8,80,640]{2,1,0:T(8,128)(2,1)S(1)} async-done(((bf16[8,80,640]{2,1,0:T(8,128)(2,1)}), bf16[8,80,640]{2,1,0:T(8,128)(2,1)S(1)}, u32[]{:S(2)}, u32[]{:S(2)}) %all-to-all-start.3) | async-done | bytes 819232 | tf_op jit(solution)/shard_map/all_to_all | solution.py:42
  (99 shorter events, 37.5 us)
Async XLA Ops:
  21.6 26.2 %all-to-all-start.1 = ((bf16[4,4,2,80,640]{4,3,2,1,0:T(8,128)(2,1)}), bf16[4,4,2,80,640]{4,3,2,1,0:T(8,128)(2,1)S(1)}, u32[]{:S(2)}, u32[]{:S(2)}) async-start(bf16[4,4,2,80,640]{4,3,2,1,0:T(8,128)(2,1)} %broadcast_in_dim.22), calls=%async_computation.1 | async-start | bytes 6553600 | tf_op jit(solution)/shard_map/all_to_all | solution.py:42
  25.9 5.6 %copy-start.20 = (s32[256]{0:T(256)S(1)}, s32[256]{0:T(256)}, u32[]{:S(2)}) copy-start(s32[256]{0:T(256)} %param.15) | copy-start | bytes 3076
  47.9 9.0 %collective-permute-start = (bf16[4,4,2,80,640]{4,3,2,1,0:T(8,128)(2,1)S(1)}, bf16[4,4,2,80,640]{4,3,2,1,0:T(8,128)(2,1)}, u32[]{:S(2)}, u32[]{:S(2)}) collective-permute-start(bf16[4,4,2,80,640]{4,3,2,1,0:T(8,128)(2,1)S(1)} %all-to-all-done.1.refs_0_.refs_1_.refs_2_.refs_3_), channel_id=1, source_target_pairs={{0,4},{4,0},{8,12},{12,8},{16,20},{20,16},{24,28},{28,24},{32,36},... | collective-permute-start | bytes 9830408 | tf_op jit(solution)/shard_map/ppermute | solution.py:34
  63.8 34.3 %collective-permute-start.1 = (bf16[64,5120]{1,0:T(8,128)(2,1)S(1)}, bf16[64,5120]{1,0:T(8,128)(2,1)S(1)}, u32[]{:S(2)}, u32[]{:S(2)}) collective-permute-start(bf16[64,5120]{1,0:T(8,128)(2,1)S(1)} %get-tuple-element.27), channel_id=1, source_target_pairs={{0,1},{1,2},{2,3},{3,0},{4,5},{5,6},{6,7},{7,4},{8,9},{9,10},{10,1... | collective-permute-start | bytes 1966088 | tf_op jit(solution)/shard_map/ppermute | solution.py:38
  66.8 32.5 %collective-permute-start.3 = (bf16[64,5120]{1,0:T(8,128)(2,1)S(1)}, bf16[64,5120]{1,0:T(8,128)(2,1)S(1)}, u32[]{:S(2)}, u32[]{:S(2)}) collective-permute-start(bf16[64,5120]{1,0:T(8,128)(2,1)S(1)} %get-tuple-element.28), channel_id=1, source_target_pairs={{0,3},{1,0},{2,1},{3,2},{4,7},{5,4},{6,5},{7,6},{8,11},{9,8},{10,9... | collective-permute-start | bytes 1966088 | tf_op jit(solution)/shard_map/ppermute | solution.py:38
  98.1 16.5 %copy-start.17 = (bf16[64,5120]{1,0:T(8,128)(2,1)S(1)}, bf16[64,5120]{1,0:T(8,128)(2,1)}, u32[]{:S(2)}) copy-start(bf16[64,5120]{1,0:T(8,128)(2,1)} %param.11) | copy-start | bytes 1966084
  98.1 16.4 %collective-permute-start.2 = (bf16[32,5120]{1,0:T(8,128)(2,1)S(1)}, bf16[32,5120]{1,0:T(8,128)(2,1)S(1)}, u32[]{:S(2)}, u32[]{:S(2)}) collective-permute-start(bf16[32,5120]{1,0:T(8,128)(2,1)S(1)} %add_convert_fusion.3), channel_id=1, source_target_pairs={{0,1},{1,2},{2,3},{3,0},{4,5},{5,6},{6,7},{7,4},{8,9},{9,10},{10,1... | collective-permute-start | bytes 983048 | tf_op jit(solution)/shard_map/ppermute | solution.py:38
  99.5 15.2 %collective-permute-start.4 = (bf16[32,5120]{1,0:T(8,128)(2,1)S(1)}, bf16[32,5120]{1,0:T(8,128)(2,1)S(1)}, u32[]{:S(2)}, u32[]{:S(2)}) collective-permute-start(bf16[32,5120]{1,0:T(8,128)(2,1)S(1)} %add_convert_fusion.2), channel_id=1, source_target_pairs={{0,3},{1,0},{2,1},{3,2},{4,7},{5,4},{6,5},{7,6},{8,11},{9,8},{10,9... | collective-permute-start | bytes 983048 | tf_op jit(solution)/shard_map/ppermute | solution.py:38
  116.6 54.5 %copy-start = (bf16[64,5120]{1,0:T(8,128)(2,1)}, bf16[64,5120]{1,0:T(8,128)(2,1)S(1)}, u32[]{:S(2)}) copy-start(bf16[64,5120]{1,0:T(8,128)(2,1)S(1)} %fusion.8.g0) | copy-start | bytes 1966084
  116.6 50.7 %copy-start.8 = (bf16[256,640]{1,0:T(8,128)(2,1)S(1)}, bf16[256,640]{1,0:T(8,128)(2,1)}, u32[]{:S(2)}) copy-start(bf16[256,640]{1,0:T(8,128)(2,1)} %copy.36.att_ref) | copy-start | bytes 983044
  116.6 28.6 %collective-permute-start.6 = (bf16[64,5120]{1,0:T(8,128)(2,1)S(1)}, bf16[64,5120]{1,0:T(8,128)(2,1)S(1)}, u32[]{:S(2)}, u32[]{:S(2)}) collective-permute-start(bf16[64,5120]{1,0:T(8,128)(2,1)S(1)} %fusion.8.g0), channel_id=1, source_target_pairs={{0,3},{1,0},{2,1},{3,2},{4,7},{5,4},{6,5},{7,6},{8,11},{9,8},{10,9... | collective-permute-start | bytes 1966088 | tf_op jit(solution)/shard_map/ppermute | solution.py:38
  119.2 26.0 %collective-permute-start.5 = (bf16[64,5120]{1,0:T(8,128)(2,1)S(1)}, bf16[64,5120]{1,0:T(8,128)(2,1)S(1)}, u32[]{:S(2)}, u32[]{:S(2)}) collective-permute-start(bf16[64,5120]{1,0:T(8,128)(2,1)S(1)} %fusion.8.g0), channel_id=1, source_target_pairs={{0,1},{1,2},{2,3},{3,0},{4,5},{5,6},{6,7},{7,4},{8,9},{9,10},{10,1... | collective-permute-start | bytes 1966088 | tf_op jit(solution)/shard_map/ppermute | solution.py:38
  119.2 13.1 %collective-permute-start.7 = (f32[40,128]{1,0:T(8,128)S(1)}, f32[40,128]{1,0:T(8,128)S(1)}, u32[]{:S(2)}, u32[]{:S(2)}) collective-permute-start(f32[40,128]{1,0:T(8,128)S(1)} %bitcast.51), channel_id=1, source_target_pairs={{0,4},{4,0},{8,12},{12,8},{16,20},{20,16},{24,28},{28,24},{32,36},... | collective-permute-start | bytes 61448 | tf_op jit(solution)/shard_map/ppermute | solution.py:34
  132.2 8.5 %collective-permute-start.8 = (f32[40,128]{1,0:T(8,128)S(1)}, f32[40,128]{1,0:T(8,128)S(1)}, u32[]{:S(2)}, u32[]{:S(2)}) collective-permute-start(f32[40,128]{1,0:T(8,128)S(1)} %bitcast_add_fusion), channel_id=1, source_target_pairs={{0,8},{4,12},{8,0},{12,4},{16,24},{20,28},{24,16},{28,20},{32,40},... | collective-permute-start | bytes 61448 | tf_op jit(solution)/shard_map/ppermute | solution.py:34
  140.7 4.4 %collective-permute-start.9 = (f32[40,128]{1,0:T(8,128)S(1)}, f32[40,128]{1,0:T(8,128)S(1)}, u32[]{:S(2)}, u32[]{:S(2)}) collective-permute-start(f32[40,128]{1,0:T(8,128)S(1)} %fusion.30), channel_id=1, source_target_pairs={{0,16},{4,20},{8,24},{12,28},{16,0},{20,4},{24,8},{28,12},{32,48},... | collective-permute-start | bytes 61448 | tf_op jit(solution)/shard_map/ppermute | solution.py:34
  145.2 26.0 %copy-start.2 = (bf16[64,5120]{1,0:T(8,128)(2,1)}, bf16[64,5120]{1,0:T(8,128)(2,1)S(1)}, u32[]{:S(2)}) copy-start(bf16[64,5120]{1,0:T(8,128)(2,1)S(1)} %collective-permute-done.6.gp) | copy-start | bytes 1966084
  145.2 26.0 %copy-start.4 = (bf16[64,5120]{1,0:T(8,128)(2,1)}, bf16[64,5120]{1,0:T(8,128)(2,1)S(1)}, u32[]{:S(2)}) copy-start(bf16[64,5120]{1,0:T(8,128)(2,1)S(1)} %collective-permute-done.5.gm) | copy-start | bytes 1966084
  145.3 22.0 %collective-permute-start.10 = (bf16[32,5120]{1,0:T(8,128)(2,1)S(1)}, bf16[32,5120]{1,0:T(8,128)(2,1)S(1)}, u32[]{:S(2)}, u32[]{:S(2)}) collective-permute-start(bf16[32,5120]{1,0:T(8,128)(2,1)S(1)} %slice.22), channel_id=1, source_target_pairs={{0,1},{1,2},{2,3},{3,0},{4,5},{5,6},{6,7},{7,4},{8,9},{9,10},{10,1... | collective-permute-start | bytes 983048 | tf_op jit(solution)/shard_map/ppermute | solution.py:38
  149.0 18.3 %collective-permute-start.11 = (bf16[32,5120]{1,0:T(8,128)(2,1)S(1)}, bf16[32,5120]{1,0:T(8,128)(2,1)S(1)}, u32[]{:S(2)}, u32[]{:S(2)}) collective-permute-start(bf16[32,5120]{1,0:T(8,128)(2,1)S(1)} %slice.23), channel_id=1, source_target_pairs={{0,3},{1,0},{2,1},{3,2},{4,7},{5,4},{6,5},{7,6},{8,11},{9,8},{10,9... | collective-permute-start | bytes 983048 | tf_op jit(solution)/shard_map/ppermute | solution.py:38
  149.1 14.1 %collective-permute-start.12 = (f32[40,128]{1,0:T(8,128)S(1)}, f32[40,128]{1,0:T(8,128)S(1)}, u32[]{:S(2)}, u32[]{:S(2)}) collective-permute-start(f32[40,128]{1,0:T(8,128)S(1)} %add.113), channel_id=1, source_target_pairs={{0,64},{4,68},{8,72},{12,76},{16,80},{20,84},{24,88},{28,92},{32,9... | collective-permute-start | bytes 61448 | tf_op jit(solution)/shard_map/ppermute | solution.py:34
  163.2 4.1 %collective-permute-start.13 = (f32[40,128]{1,0:T(8,128)S(1)}, f32[40,128]{1,0:T(8,128)S(1)}, u32[]{:S(2)}, u32[]{:S(2)}) collective-permute-start(f32[40,128]{1,0:T(8,128)S(1)} %add.114), channel_id=1, source_target_pairs={{0,128},{4,132},{8,136},{12,140},{16,144},{20,148},{24,152},{28,15... | collective-permute-start | bytes 61448 | tf_op jit(solution)/shard_map/ppermute | solution.py:34
  167.3 3.9 %copy-start.9 = (bf16[32,5120]{1,0:T(8,128)(2,1)}, bf16[32,5120]{1,0:T(8,128)(2,1)S(1)}, u32[]{:S(2)}) copy-start(bf16[32,5120]{1,0:T(8,128)(2,1)S(1)} %collective-permute-done.10.ga) | copy-start | bytes 983044
  167.4 3.8 %copy-start.11 = (bf16[32,5120]{1,0:T(8,128)(2,1)}, bf16[32,5120]{1,0:T(8,128)(2,1)S(1)}, u32[]{:S(2)}) copy-start(bf16[32,5120]{1,0:T(8,128)(2,1)S(1)} %collective-permute-done.11.gb) | copy-start | bytes 983044
  171.2 9.0 %collective-permute-start.14 = (bf16[4,4,2,80,640]{4,3,2,1,0:T(8,128)(2,1)S(1)}, bf16[4,4,2,80,640]{4,3,2,1,0:T(8,128)(2,1)S(1)}, u32[]{:S(2)}, u32[]{:S(2)}) collective-permute-start(bf16[4,4,2,80,640]{4,3,2,1,0:T(8,128)(2,1)S(1)} %get-tuple-element.36), channel_id=1, source_target_pairs={{0,4},{4,0},{8,12},{12,8},{16,20},{20,16},{24,28},{28,24},{32,36},... | collective-permute-start | bytes 9830408 | tf_op jit(solution)/shard_map/ppermute | solution.py:34
  182.8 27.4 %all-to-all-start.2 = ((bf16[4,4,2,80,640]{4,3,2,1,0:T(8,128)(2,1)}), bf16[4,4,2,80,640]{4,3,2,1,0:T(8,128)(2,1)}, u32[]{:S(2)}, u32[]{:S(2)}) async-start(bf16[4,4,2,80,640]{4,3,2,1,0:T(8,128)(2,1)} %add_convert_fusion), calls=%async_computation.2 | async-start | bytes 6553600 | tf_op jit(solution)/shard_map/all_to_all | solution.py:42
  187.5 2.7 %collective-permute-start.15 = (f32[40,128]{1,0:T(8,128)S(1)}, f32[40,128]{1,0:T(8,128)S(1)}, u32[]{:S(2)}, u32[]{:S(2)}) collective-permute-start(f32[40,128]{1,0:T(8,128)S(1)} %add.115), channel_id=1, source_target_pairs={{0,32},{4,36},{8,40},{12,44},{16,48},{20,52},{24,56},{28,60},{32,0... | collective-permute-start | bytes 61448 | tf_op jit(solution)/shard_map/ppermute | solution.py:34
  190.2 3.9 %collective-permute-start.16 = (f32[40,128]{1,0:T(8,128)S(1)}, f32[40,128]{1,0:T(8,128)S(1)}, u32[]{:S(2)}, u32[]{:S(2)}) collective-permute-start(f32[40,128]{1,0:T(8,128)S(1)} %add.117), channel_id=1, source_target_pairs={{0,1},{1,0},{2,3},{3,2},{4,5},{5,4},{6,7},{7,6},{8,9},{9,8},{10,11... | collective-permute-start | bytes 61448 | tf_op jit(solution)/shard_map/ppermute | solution.py:313
  194.1 16.0 %collective-permute-start.17 = (f32[40,128]{1,0:T(8,128)S(1)}, f32[40,128]{1,0:T(8,128)S(1)}, u32[]{:S(2)}, u32[]{:S(2)}) collective-permute-start(f32[40,128]{1,0:T(8,128)S(1)} %add.118), channel_id=1, source_target_pairs={{0,2},{1,3},{2,0},{3,1},{4,6},{5,7},{6,4},{7,5},{8,10},{9,11},{10,... | collective-permute-start | bytes 61448 | tf_op jit(solution)/shard_map/ppermute | solution.py:313
  213.4 3.7 %copy-start.14 = (f32[5,256,256]{1,2,0:T(8,128)S(1)}, f32[5,256,256]{1,2,0:T(8,128)}, u32[]{:S(2)}) copy-start(f32[5,256,256]{1,2,0:T(8,128)} %get-tuple-element.57) | copy-start | bytes 3932164
  213.4 13.2 %all-to-all-start.3 = ((bf16[8,80,640]{2,1,0:T(8,128)(2,1)}), bf16[8,80,640]{2,1,0:T(8,128)(2,1)S(1)}, u32[]{:S(2)}, u32[]{:S(2)}) async-start(bf16[8,80,640]{2,1,0:T(8,128)(2,1)} %bitcast.16), calls=%async_computation.3 | async-start | bytes 1638400 | tf_op jit(solution)/shard_map/all_to_all | solution.py:42
  217.1 1.3 copy-start.18
  219.8 1.2 copy-start.15
  (10 other events, 10.1 us)

commit v5 on v4

--- a/solution.py
+++ b/solution.py
@@ -174,7 +174,7 @@
     seq, width = attended.shape
     span = 16 * piece
     shape = (4, 4, 2, piece, width)
-    block = pl.BlockSpec(shape, lambda i: (0, 0, 0, 0, 0))
+    block = pl.BlockSpec(memory_space=pltpu.VMEM)
     return pl.pallas_call(
         weight_kernel,
         grid=(4,),
@@ -244,6 +244,29 @@
     )(pos, *parts, *[cat] * 4, *[oth] * 4)
 
 
+def sum_kernel(in_ref, out_ref):
+    total = in_ref[0].astype(F32)
+    for k in range(1, 4):
+        total = total + in_ref[k].astype(F32)
+    out_ref[...] = total.astype(BF)
+
+
+def sum_blocks(blocks):
+    piece, width = blocks.shape[3:]
+    return pl.pallas_call(
+        sum_kernel,
+        grid=(4,),
+        in_specs=[pl.BlockSpec((4, 1, 2, piece, width), lambda i: (0, i, 0, 0, 0))],
+        out_specs=pl.BlockSpec((1, 2, piece, width), lambda i: (i, 0, 0, 0)),
+        out_shape=jax.ShapeDtypeStruct((4, 2, piece, width), BF),
+        compiler_params=pltpu.CompilerParams(vmem_limit_bytes=VMEM_LIMIT),
+        cost_estimate=pl.CostEstimate(
+            flops=32 * piece * width, bytes_accessed=80 * piece * width, transcendentals=0
+        ),
+        name="sum_blocks",
+    )(blocks)
+
+
 def sum_f32(*parts):
     total = parts[0].astype(F32)
     for part in parts[1:]:
@@ -299,20 +322,19 @@
     gain = jnp.sum(cot * mixed * inv, axis=0).reshape(d_model // 128, 128)
     gm = send_mp(grad_residual, 1)
     gp = send_mp(grad_residual, -1)
-    gm, gp, gain = tie((gm, gp, add_from(gain, (1, 2, 4))))
+    gm, gp, gain = tie((gm, gp, add_from(gain, (2, 4, 16, 32))))
     ga = send_mp(gm[:half], 1)
     gb = send_mp(gp[half:], -1)
-    ga, gb, gain = tie((ga, gb, add_from(gain, (16, 32))))
     parts = (grad_residual, gp, ga, gb, gm)
     keep, send = weight_part(pos, parts, attended, piece)
-    both = sum_f32(keep, swap(send, FLIP_C)).astype(BF)
-    grad_attended = attended_part(pos, parts, cat, oth)
+    swapped, grad_attended = tie((swap(send, FLIP_C), attended_part(pos, parts, cat, oth)))
+    both = sum_f32(keep, swapped).astype(BF)
     part = exchange(both, FAR)
-    gain = add_from(gain, (8,))
+    gain = add_from(gain, (1, 8))
     for bit in (1, 2):
         gain = gain + lax.ppermute(gain, "mp", [(i, i ^ bit) for i in range(4)])
     part, gain = tie((part, gain))
-    part = sum_f32(*part).astype(BF).reshape(8, piece, width)
+    part = sum_blocks(part).reshape(8, piece, width)
     grad_weight = sum_f32(*exchange(part, NEAR)) / 64
     grad_gain = lax.dynamic_slice_in_dim(gain.reshape(d_model) / 64, dp * piece, piece, 0)
 

time: 232 us -> 230 us (level); the launches traced: 227 us -> 229 us
  waiting for transfers between devices: 80.4 us -> 111 us
  starting transfers between devices: 74 us -> 51.5 us
  local copies, waits for them, and re-layouts: 23.2 us -> 19.7 us
  other arithmetic: 8.56 us -> 5.19 us
    ppermute x8, starting transfers between devices: 41.8 us -> 7.39 us  [swap(): return lax.ppermute(value, 'dp', pairs)]
    ppermute x8, starting transfers between devices: 14.3 us -> 30.2 us  [send_mp(): return lax.ppermute(value, 'mp', [(i, (i + step) % 4) for i in range(4)])]
    ppermute x8, waiting for transfers between devices: 42.8 us -> 58.1 us  [send_mp(): return lax.ppermute(value, 'mp', [(i, (i + step) % 4) for i in range(4)])]
    all_to_all x3, waiting for transfers between devices: 14.9 us -> 24 us  [exchange(): return lax.all_to_all(blocks, 'dp', 0, 0, axis_index_groups=groups)]
    ppermute x2, waiting for transfers between devices: 1.71 us -> 8.12 us  [on_device(): gain = gain + lax.ppermute(gain, 'mp', [(i, i ^ bit) for i in range(4)])]
    unnamed x48 -> x34, local copies, waits for them, and re-layouts: 16.6 us -> 12.3 us
    another operation x1 -> x0, other arithmetic: 3.2 us -> none
    ppermute x2, starting transfers between devices: 5.29 us -> 2.25 us  [on_device(): gain = gain + lax.ppermute(gain, 'mp', [(i, i ^ bit) for i in range(4)])]
  transfers between devices with their start and end apart: 21 -> 21, of which waited for: 15 -> 20; matrix products, arithmetic and copies ran while one was open for 8% -> 9% of each run, Pallas kernels for 3% -> 3%
where the time goes in v5:
time: 230 us; the launch traced here: 229 us
  waiting for transfers between devices  111 us (48%)
  starting transfers between devices  51.5 us (22%)
  local copies, waits for them, and re-layouts  19.7 us (9%)
  blocking collectives  18.1 us (8%)
  Pallas kernels  16.4 us (7%)
  matrix products  6.59 us (3%)
  other arithmetic  5.19 us (2%)
    ppermute x8, waiting for transfers between devices, send_mp(): return lax.ppermute(value, 'mp', [(i, (i + step) % 4) for i in range(4)])  58.1 us
    ppermute x8, starting transfers between devices, send_mp(): return lax.ppermute(value, 'mp', [(i, (i + step) % 4) for i in range(4)])  30.2 us
    all_to_all x3, waiting for transfers between devices, exchange(): return lax.all_to_all(blocks, 'dp', 0, 0, axis_index_groups=groups)  24 us
    ppermute x8, waiting for transfers between devices, swap(): return lax.ppermute(value, 'dp', pairs)  20.6 us
    all_to_all x1, blocking collectives, exchange(): return lax.all_to_all(blocks, 'dp', 0, 0, axis_index_groups=groups)  18.1 us
    unnamed x34, local copies, waits for them, and re-layouts  12.3 us
    all_to_all x3, starting transfers between devices, exchange(): return lax.all_to_all(blocks, 'dp', 0, 0, axis_index_groups=groups)  11.7 us
    ppermute x2, waiting for transfers between devices, on_device(): gain = gain + lax.ppermute(gain, 'mp', [(i, i ^ bit) for i in range(4)])  8.12 us
  transfers between devices with their start and end apart: 21, of which 20 were waited for; matrix products, arithmetic and copies ran while one was open for 9% of the time, Pallas kernels for 3%

profile of v5, /device:TPU:1, one launch (start us, length us, event | category | flops | bytes accessed | tf_op | source)
XLA Modules:
  0.0 229.1 jit_solution(6893351707658555025)
XLA Ops:
  1.6 18.1 %all_to_all.20 = bf16[8,80,640]{2,1,0:T(8,128)(2,1)S(1)} all-to-all(bf16[8,80,640]{2,1,0:T(8,128)(2,1)S(1)} %broadcast_in_dim.20), channel_id=1, replica_groups={{0,32,8,40,16,48,24,56},{64,96,72,104,80,112,88,120},{128,160,136,168,1..., dimensions={0} | all-to-all | bytes 1638400 | tf_op jit(solution)/shard_map/all_to_all | solution.py:42
  21.6 4.3 %all-to-all-start.1 = ((bf16[4,4,2,80,640]{4,3,2,1,0:T(8,128)(2,1)}), bf16[4,4,2,80,640]{4,3,2,1,0:T(8,128)(2,1)S(1)}, u32[]{:S(2)}, u32[]{:S(2)}) async-start(bf16[4,4,2,80,640]{4,3,2,1,0:T(8,128)(2,1)} %broadcast_in_dim.22), calls=%async_computation.1 | async-start | bytes 6553600 | tf_op jit(solution)/shard_map/all_to_all | solution.py:42
  31.6 2.8 %fusion.19 = (f32[5,256]{1,0:T(8,128)S(1)}, f32[5,256,256]{1,2,0:T(8,128)}) fusion(bf16[256,5,128]{0,2,1:T(8,128)(2,1)} %bitcast.40, bf16[256,5,128]{0,2,1:T(8,128)(2,1)} %bitcast.42, pred[256,256]{0,1:T(8,128)(4,1)S(1)} %fusion.15), kind=kOutput, calls=%fused_computation.41 | convolution fusion | flops 85197056 | bytes 2036736 | tf_op jit(solution)/shard_map/sub | solution.py:57
  34.4 2.4 %convolution_convert_fusion = bf16[5,256,128]{1,2,0:T(8,128)(2,1)} fusion(bf16[256,5,128]{0,2,1:T(8,128)(2,1)} %bitcast.46, f32[5,256,256]{1,2,0:T(8,128)} %get-tuple-element.55, f32[5,256]{1,0:T(8,128)S(1)} %get-tuple-element.54), kind=kOutput, calls=%fused_computation.23 | convolution fusion | flops 84705280 | bytes 1971200 | tf_op jit(solution)/shard_map/hts,shd->thd/dot_general | solution.py:297
  36.8 11.1 %all-to-all-done.1.refs_0_.refs_1_.refs_2_.refs_3_ = bf16[4,4,2,80,640]{4,3,2,1,0:T(8,128)(2,1)S(1)} async-done(((bf16[4,4,2,80,640]{4,3,2,1,0:T(8,128)(2,1)}), bf16[4,4,2,80,640]{4,3,2,1,0:T(8,128)(2,1)S(1)}, u32[]{:S(2)}, u32[]{:S(2)}) %all-to-all-start.1) | async-done | bytes 3276832 | tf_op jit(solution)/shard_map/all_to_all | solution.py:42
  47.9 3.4 %collective-permute-start = (bf16[4,4,2,80,640]{4,3,2,1,0:T(8,128)(2,1)S(1)}, bf16[4,4,2,80,640]{4,3,2,1,0:T(8,128)(2,1)}, u32[]{:S(2)}, u32[]{:S(2)}) collective-permute-start(bf16[4,4,2,80,640]{4,3,2,1,0:T(8,128)(2,1)S(1)} %all-to-all-done.1.refs_0_.refs_1_.refs_2_.refs_3_), channel_id=1, source_target_pairs={{0,4},{4,0},{8,12},{12,8},{16,20},{20,16},{24,28},{28,24},{32,36},... | collective-permute-start | bytes 9830408 | tf_op jit(solution)/shard_map/ppermute | solution.py:34
  53.2 3.6 %collective-permute-done.refs_4_.refs_5_.refs_6_.refs_7_ = bf16[4,4,2,80,640]{4,3,2,1,0:T(8,128)(2,1)} collective-permute-done((bf16[4,4,2,80,640]{4,3,2,1,0:T(8,128)(2,1)S(1)}, bf16[4,4,2,80,640]{4,3,2,1,0:T(8,128)(2,1)}, u32[]{:S(2)}, u32[]{:S(2)}) %collective-permute-start) | collective-permute-done | bytes 3276832 | tf_op jit(solution)/shard_map/ppermute | solution.py:34
  57.8 5.9 %branch_part.1 = (bf16[64,5120]{1,0:T(8,128)(2,1)S(1)}, bf16[32,5120]{1,0:T(8,128)(2,1)S(1)}, bf16[32,5120]{1,0:T(8,128)(2,1)S(1)}, bf16[64,5120]{1,0:T(8,128)(2,1)S(1)}, bf16[64,5120]{1,0:T(8,128)(2,1)S(1)}) custom-call(s32[2]{0:T(128)S(1)} %pad_add_fusion.pos, bf16[256,640]{1,0:T(8,128)(2,1)S(1)} %copy-done.3, ...), custom_call_target="tpu_custom_call" | custom-call | flops 1677721600 | bytes 9175040 | tf_op jit(solution)/shard_map/branch_part/pallas_call | solution.py:119
  63.8 3.1 %collective-permute-start.1 = (bf16[64,5120]{1,0:T(8,128)(2,1)S(1)}, bf16[64,5120]{1,0:T(8,128)(2,1)S(1)}, u32[]{:S(2)}, u32[]{:S(2)}) collective-permute-start(bf16[64,5120]{1,0:T(8,128)(2,1)S(1)} %get-tuple-element.26), channel_id=1, source_target_pairs={{0,1},{1,2},{2,3},{3,0},{4,5},{5,6},{6,7},{7,4},{8,9},{9,10},{10,1... | collective-permute-start | bytes 1966088 | tf_op jit(solution)/shard_map/ppermute | solution.py:38
  69.1 29.0 %collective-permute-done.1 = bf16[64,5120]{1,0:T(8,128)(2,1)S(1)} collective-permute-done((bf16[64,5120]{1,0:T(8,128)(2,1)S(1)}, bf16[64,5120]{1,0:T(8,128)(2,1)S(1)}, u32[]{:S(2)}, u32[]{:S(2)}) %collective-permute-start.1) | collective-permute-done | bytes 655392 | tf_op jit(solution)/shard_map/ppermute | solution.py:38
  99.4 2.5 %collective-permute-start.4 = (bf16[32,5120]{1,0:T(8,128)(2,1)S(1)}, bf16[32,5120]{1,0:T(8,128)(2,1)S(1)}, u32[]{:S(2)}, u32[]{:S(2)}) collective-permute-start(bf16[32,5120]{1,0:T(8,128)(2,1)S(1)} %add_convert_fusion.1), channel_id=1, source_target_pairs={{0,3},{1,0},{2,1},{3,2},{4,7},{5,4},{6,5},{7,6},{8,11},{9,8},{10,9... | collective-permute-start | bytes 983048 | tf_op jit(solution)/shard_map/ppermute | solution.py:38
  102.0 12.5 %collective-permute-done.2 = bf16[32,5120]{1,0:T(8,128)(2,1)S(1)} collective-permute-done((bf16[32,5120]{1,0:T(8,128)(2,1)S(1)}, bf16[32,5120]{1,0:T(8,128)(2,1)S(1)}, u32[]{:S(2)}, u32[]{:S(2)}) %collective-permute-start.2) | collective-permute-done | bytes 327712 | tf_op jit(solution)/shard_map/ppermute | solution.py:38
  114.5 3.1 %collective-permute-done.4 = bf16[32,5120]{1,0:T(8,128)(2,1)S(1)} collective-permute-done((bf16[32,5120]{1,0:T(8,128)(2,1)S(1)}, bf16[32,5120]{1,0:T(8,128)(2,1)S(1)}, u32[]{:S(2)}, u32[]{:S(2)}) %collective-permute-start.4) | collective-permute-done | bytes 327712 | tf_op jit(solution)/shard_map/ppermute | solution.py:38
  120.2 15.7 %collective-permute-start.5 = (bf16[64,5120]{1,0:T(8,128)(2,1)S(1)}, bf16[64,5120]{1,0:T(8,128)(2,1)S(1)}, u32[]{:S(2)}, u32[]{:S(2)}) collective-permute-start(bf16[64,5120]{1,0:T(8,128)(2,1)S(1)} %fusion.8.g0), channel_id=1, source_target_pairs={{0,1},{1,2},{2,3},{3,0},{4,5},{5,6},{6,7},{7,4},{8,9},{9,10},{10,1... | collective-permute-start | bytes 1966088 | tf_op jit(solution)/shard_map/ppermute | solution.py:38
  139.3 3.6 %collective-permute-done.8 = f32[40,128]{1,0:T(8,128)S(1)} collective-permute-done((f32[40,128]{1,0:T(8,128)S(1)}, f32[40,128]{1,0:T(8,128)S(1)}, u32[]{:S(2)}, u32[]{:S(2)}) %collective-permute-start.8) | collective-permute-done | bytes 20512 | tf_op jit(solution)/shard_map/ppermute | solution.py:34
  143.0 2.9 %collective-permute-done.9 = f32[40,128]{1,0:T(8,128)S(1)} collective-permute-done((f32[40,128]{1,0:T(8,128)S(1)}, f32[40,128]{1,0:T(8,128)S(1)}, u32[]{:S(2)}, u32[]{:S(2)}) %collective-permute-start.9) | collective-permute-done | bytes 20512 | tf_op jit(solution)/shard_map/ppermute | solution.py:34
  146.2 4.1 %collective-permute-done.10 = f32[40,128]{1,0:T(8,128)S(1)} collective-permute-done((f32[40,128]{1,0:T(8,128)S(1)}, f32[40,128]{1,0:T(8,128)S(1)}, u32[]{:S(2)}, u32[]{:S(2)}) %collective-permute-start.10) | collective-permute-done | bytes 20512 | tf_op jit(solution)/shard_map/ppermute | solution.py:34
  150.3 2.6 %collective-permute-done.6.gp = bf16[64,5120]{1,0:T(8,128)(2,1)S(1)} collective-permute-done((bf16[64,5120]{1,0:T(8,128)(2,1)S(1)}, bf16[64,5120]{1,0:T(8,128)(2,1)S(1)}, u32[]{:S(2)}, u32[]{:S(2)}) %collective-permute-start.6) | collective-permute-done | bytes 655392 | tf_op jit(solution)/shard_map/ppermute | solution.py:38
  154.1 6.0 %collective-permute-start.11 = (bf16[32,5120]{1,0:T(8,128)(2,1)S(1)}, bf16[32,5120]{1,0:T(8,128)(2,1)S(1)}, u32[]{:S(2)}, u32[]{:S(2)}) collective-permute-start(bf16[32,5120]{1,0:T(8,128)(2,1)S(1)} %slice.22), channel_id=1, source_target_pairs={{0,1},{1,2},{2,3},{3,0},{4,5},{5,6},{6,7},{7,4},{8,9},{9,10},{10,1... | collective-permute-start | bytes 983048 | tf_op jit(solution)/shard_map/ppermute | solution.py:38
  160.1 5.9 %collective-permute-done.11.ga = bf16[32,5120]{1,0:T(8,128)(2,1)S(1)} collective-permute-done((bf16[32,5120]{1,0:T(8,128)(2,1)S(1)}, bf16[32,5120]{1,0:T(8,128)(2,1)S(1)}, u32[]{:S(2)}, u32[]{:S(2)}) %collective-permute-start.11) | collective-permute-done | bytes 327712 | tf_op jit(solution)/shard_map/ppermute | solution.py:38
  166.0 2.8 %collective-permute-done.12.gb = bf16[32,5120]{1,0:T(8,128)(2,1)S(1)} collective-permute-done((bf16[32,5120]{1,0:T(8,128)(2,1)S(1)}, bf16[32,5120]{1,0:T(8,128)(2,1)S(1)}, u32[]{:S(2)}, u32[]{:S(2)}) %collective-permute-start.12) | collective-permute-done | bytes 327712 | tf_op jit(solution)/shard_map/ppermute | solution.py:38
  168.8 3.8 %weight_part.1 = (bf16[4,4,2,80,640]{4,3,2,1,0:T(8,128)(2,1)S(1)}, bf16[4,4,2,80,640]{4,3,2,1,0:T(8,128)(2,1)S(1)}) custom-call(s32[2]{0:T(128)S(1)} %pad_add_fusion.pos, bf16[64,5120]{1,0:T(8,128)(2,1)S(1)} %fusion.8.g0, bf16[64,5120]{1,0:T(8,128)(2,1)S(1)} %collective-permute-done.6.gp, bf16[32,5120]{1,0:T(8,128)(2,1)S(1)} %collective-permute-done.11.ga, ...), custom_call_target="tpu_custom_call" | custom-call | flops 1677721600 | bytes 9175040 | tf_op jit(solution)/shard_map/weight_part/pallas_call | solution.py:178
  172.6 2.4 %collective-permute-start.13 = (bf16[4,4,2,80,640]{4,3,2,1,0:T(8,128)(2,1)S(1)}, bf16[4,4,2,80,640]{4,3,2,1,0:T(8,128)(2,1)S(1)}, u32[]{:S(2)}, u32[]{:S(2)}) collective-permute-start(bf16[4,4,2,80,640]{4,3,2,1,0:T(8,128)(2,1)S(1)} %get-tuple-element.31), channel_id=1, source_target_pairs={{0,4},{4,0},{8,12},{12,8},{16,20},{20,16},{24,28},{28,24},{32,36},... | collective-permute-start | bytes 9830408 | tf_op jit(solution)/shard_map/ppermute | solution.py:34
  174.9 5.9 %attended_part.1 = bf16[256,640]{1,0:T(8,128)(2,1)S(1)} custom-call(s32[2]{0:T(128)S(1)} %pad_add_fusion.pos, bf16[64,5120]{1,0:T(8,128)(2,1)S(1)} %fusion.8.g0, bf16[64,5120]{1,0:T(8,128)(2,1)S(1)} %collective-permute-done.6.gp, bf16[32,5120]{1,0:T(8,128)(2,1)S(1)} %collective-permute-done.11.ga, bf16[32,5120]{1,0:T(8,128)(2,1)S(1)} %collective-permute-done.12.gb, ...), custom_call_target="tpu_custom_call" | custom-call | flops 1677721600 | bytes 9175040 | tf_op jit(solution)/shard_map/attended_part/pallas_call | solution.py:222
  181.6 2.5 %add_convert_fusion = bf16[4,4,2,80,640]{4,3,2,1,0:T(8,128)(2,1)} fusion(bf16[4,4,2,80,640]{4,3,2,1,0:T(8,128)(2,1)S(1)} %collective-permute-done.13, bf16[4,4,2,80,640]{4,3,2,1,0:T(8,128)(2,1)S(1)} %get-tuple-element.33), kind=kLoop, calls=%fused_computation.1 | loop fusion | flops 6553600 | bytes 9830400 | tf_op jit(solution)/shard_map/convert_element_type | solution.py:331
  184.1 3.7 %all-to-all-start.2 = ((bf16[4,4,2,80,640]{4,3,2,1,0:T(8,128)(2,1)}), bf16[4,4,2,80,640]{4,3,2,1,0:T(8,128)(2,1)S(1)}, u32[]{:S(2)}, u32[]{:S(2)}) async-start(bf16[4,4,2,80,640]{4,3,2,1,0:T(8,128)(2,1)} %add_convert_fusion), calls=%async_computation.2 | async-start | bytes 6553600 | tf_op jit(solution)/shard_map/all_to_all | solution.py:42
  189.1 2.9 %collective-permute-done.15 = f32[40,128]{1,0:T(8,128)S(1)} collective-permute-done((f32[40,128]{1,0:T(8,128)S(1)}, f32[40,128]{1,0:T(8,128)S(1)}, u32[]{:S(2)}, u32[]{:S(2)}) %collective-permute-start.15) | collective-permute-done | bytes 20512 | tf_op jit(solution)/shard_map/ppermute | solution.py:34
  193.3 2.5 %collective-permute-done.16 = f32[40,128]{1,0:T(8,128)S(1)} collective-permute-done((f32[40,128]{1,0:T(8,128)S(1)}, f32[40,128]{1,0:T(8,128)S(1)}, u32[]{:S(2)}, u32[]{:S(2)}) %collective-permute-start.16) | collective-permute-done | bytes 20512 | tf_op jit(solution)/shard_map/ppermute | solution.py:335
  196.8 5.6 %collective-permute-done.17 = f32[40,128]{1,0:T(8,128)S(1)} collective-permute-done((f32[40,128]{1,0:T(8,128)S(1)}, f32[40,128]{1,0:T(8,128)S(1)}, u32[]{:S(2)}, u32[]{:S(2)}) %collective-permute-start.17) | collective-permute-done | bytes 20512 | tf_op jit(solution)/shard_map/ppermute | solution.py:335
  204.2 5.5 %all-to-all-done.2.in_ref = bf16[4,4,2,80,640]{4,3,2,1,0:T(8,128)(2,1)S(1)} async-done(((bf16[4,4,2,80,640]{4,3,2,1,0:T(8,128)(2,1)}), bf16[4,4,2,80,640]{4,3,2,1,0:T(8,128)(2,1)S(1)}, u32[]{:S(2)}, u32[]{:S(2)}) %all-to-all-start.2) | async-done | bytes 3276832 | tf_op jit(solution)/shard_map/all_to_all | solution.py:42
  211.4 3.7 %all-to-all-start.3 = ((bf16[8,80,640]{2,1,0:T(8,128)(2,1)}), bf16[8,80,640]{2,1,0:T(8,128)(2,1)S(1)}, u32[]{:S(2)}, u32[]{:S(2)}) async-start(bf16[8,80,640]{2,1,0:T(8,128)(2,1)} %bitcast.38), calls=%async_computation.3 | async-start | bytes 1638400 | tf_op jit(solution)/shard_map/all_to_all | solution.py:42
  220.8 7.5 %all-to-all-done.3 = bf16[8,80,640]{2,1,0:T(8,128)(2,1)S(1)} async-done(((bf16[8,80,640]{2,1,0:T(8,128)(2,1)}), bf16[8,80,640]{2,1,0:T(8,128)(2,1)S(1)}, u32[]{:S(2)}, u32[]{:S(2)}) %all-to-all-start.3) | async-done | bytes 819232 | tf_op jit(solution)/shard_map/all_to_all | solution.py:42
  (85 shorter events, 37.1 us)
Async XLA Ops:
  21.6 26.2 %all-to-all-start.1 = ((bf16[4,4,2,80,640]{4,3,2,1,0:T(8,128)(2,1)}), bf16[4,4,2,80,640]{4,3,2,1,0:T(8,128)(2,1)S(1)}, u32[]{:S(2)}, u32[]{:S(2)}) async-start(bf16[4,4,2,80,640]{4,3,2,1,0:T(8,128)(2,1)} %broadcast_in_dim.22), calls=%async_computation.1 | async-start | bytes 6553600 | tf_op jit(solution)/shard_map/all_to_all | solution.py:42
  25.9 5.6 %copy-start.13 = (s32[256]{0:T(256)S(1)}, s32[256]{0:T(256)}, u32[]{:S(2)}) copy-start(s32[256]{0:T(256)} %param.15) | copy-start | bytes 3076
  47.9 9.0 %collective-permute-start = (bf16[4,4,2,80,640]{4,3,2,1,0:T(8,128)(2,1)S(1)}, bf16[4,4,2,80,640]{4,3,2,1,0:T(8,128)(2,1)}, u32[]{:S(2)}, u32[]{:S(2)}) collective-permute-start(bf16[4,4,2,80,640]{4,3,2,1,0:T(8,128)(2,1)S(1)} %all-to-all-done.1.refs_0_.refs_1_.refs_2_.refs_3_), channel_id=1, source_target_pairs={{0,4},{4,0},{8,12},{12,8},{16,20},{20,16},{24,28},{28,24},{32,36},... | collective-permute-start | bytes 9830408 | tf_op jit(solution)/shard_map/ppermute | solution.py:34
  63.8 34.3 %collective-permute-start.1 = (bf16[64,5120]{1,0:T(8,128)(2,1)S(1)}, bf16[64,5120]{1,0:T(8,128)(2,1)S(1)}, u32[]{:S(2)}, u32[]{:S(2)}) collective-permute-start(bf16[64,5120]{1,0:T(8,128)(2,1)S(1)} %get-tuple-element.26), channel_id=1, source_target_pairs={{0,1},{1,2},{2,3},{3,0},{4,5},{5,6},{6,7},{7,4},{8,9},{9,10},{10,1... | collective-permute-start | bytes 1966088 | tf_op jit(solution)/shard_map/ppermute | solution.py:38
  66.8 32.5 %collective-permute-start.3 = (bf16[64,5120]{1,0:T(8,128)(2,1)S(1)}, bf16[64,5120]{1,0:T(8,128)(2,1)S(1)}, u32[]{:S(2)}, u32[]{:S(2)}) collective-permute-start(bf16[64,5120]{1,0:T(8,128)(2,1)S(1)} %get-tuple-element.27), channel_id=1, source_target_pairs={{0,3},{1,0},{2,1},{3,2},{4,7},{5,4},{6,5},{7,6},{8,11},{9,8},{10,9... | collective-permute-start | bytes 1966088 | tf_op jit(solution)/shard_map/ppermute | solution.py:38
  98.1 19.5 %copy-start.9 = (bf16[64,5120]{1,0:T(8,128)(2,1)S(1)}, bf16[64,5120]{1,0:T(8,128)(2,1)}, u32[]{:S(2)}) copy-start(bf16[64,5120]{1,0:T(8,128)(2,1)} %param.11) | copy-start | bytes 1966084
  98.1 16.4 %collective-permute-start.2 = (bf16[32,5120]{1,0:T(8,128)(2,1)S(1)}, bf16[32,5120]{1,0:T(8,128)(2,1)S(1)}, u32[]{:S(2)}, u32[]{:S(2)}) collective-permute-start(bf16[32,5120]{1,0:T(8,128)(2,1)S(1)} %add_convert_fusion.2), channel_id=1, source_target_pairs={{0,1},{1,2},{2,3},{3,0},{4,5},{5,6},{6,7},{7,4},{8,9},{9,10},{10,1... | collective-permute-start | bytes 983048 | tf_op jit(solution)/shard_map/ppermute | solution.py:38
  99.4 18.1 %collective-permute-start.4 = (bf16[32,5120]{1,0:T(8,128)(2,1)S(1)}, bf16[32,5120]{1,0:T(8,128)(2,1)S(1)}, u32[]{:S(2)}, u32[]{:S(2)}) collective-permute-start(bf16[32,5120]{1,0:T(8,128)(2,1)S(1)} %add_convert_fusion.1), channel_id=1, source_target_pairs={{0,3},{1,0},{2,1},{3,2},{4,7},{5,4},{6,5},{7,6},{8,11},{9,8},{10,9... | collective-permute-start | bytes 983048 | tf_op jit(solution)/shard_map/ppermute | solution.py:38
  117.6 1.1 copy-start.5
  117.6 1.1 copy-start.12
  119.5 55.4 %copy-start.1 = (bf16[64,5120]{1,0:T(8,128)(2,1)}, bf16[64,5120]{1,0:T(8,128)(2,1)S(1)}, u32[]{:S(2)}) copy-start(bf16[64,5120]{1,0:T(8,128)(2,1)S(1)} %fusion.8.g0) | copy-start | bytes 1966084
  119.5 49.2 %copy-start.4 = (bf16[256,640]{1,0:T(8,128)(2,1)S(1)}, bf16[256,640]{1,0:T(8,128)(2,1)}, u32[]{:S(2)}) copy-start(bf16[256,640]{1,0:T(8,128)(2,1)} %copy.36.att_ref) | copy-start | bytes 983044
  119.6 33.4 %collective-permute-start.6 = (bf16[64,5120]{1,0:T(8,128)(2,1)S(1)}, bf16[64,5120]{1,0:T(8,128)(2,1)S(1)}, u32[]{:S(2)}, u32[]{:S(2)}) collective-permute-start(bf16[64,5120]{1,0:T(8,128)(2,1)S(1)} %fusion.8.g0), channel_id=1, source_target_pairs={{0,3},{1,0},{2,1},{3,2},{4,7},{5,4},{6,5},{7,6},{8,11},{9,8},{10,9... | collective-permute-start | bytes 1966088 | tf_op jit(solution)/shard_map/ppermute | solution.py:38
  120.2 33.8 %collective-permute-start.5 = (bf16[64,5120]{1,0:T(8,128)(2,1)S(1)}, bf16[64,5120]{1,0:T(8,128)(2,1)S(1)}, u32[]{:S(2)}, u32[]{:S(2)}) collective-permute-start(bf16[64,5120]{1,0:T(8,128)(2,1)S(1)} %fusion.8.g0), channel_id=1, source_target_pairs={{0,1},{1,2},{2,3},{3,0},{4,5},{5,6},{6,7},{7,4},{8,9},{9,10},{10,1... | collective-permute-start | bytes 1966088 | tf_op jit(solution)/shard_map/ppermute | solution.py:38
  135.9 2.6 %collective-permute-start.7 = (f32[40,128]{1,0:T(8,128)S(1)}, f32[40,128]{1,0:T(8,128)S(1)}, u32[]{:S(2)}, u32[]{:S(2)}) collective-permute-start(f32[40,128]{1,0:T(8,128)S(1)} %bitcast.52), channel_id=1, source_target_pairs={{0,8},{4,12},{8,0},{12,4},{16,24},{20,28},{24,16},{28,20},{32,40},... | collective-permute-start | bytes 61448 | tf_op jit(solution)/shard_map/ppermute | solution.py:34
  138.5 4.4 %collective-permute-start.8 = (f32[40,128]{1,0:T(8,128)S(1)}, f32[40,128]{1,0:T(8,128)S(1)}, u32[]{:S(2)}, u32[]{:S(2)}) collective-permute-start(f32[40,128]{1,0:T(8,128)S(1)} %bitcast_add_fusion), channel_id=1, source_target_pairs={{0,16},{4,20},{8,24},{12,28},{16,0},{20,4},{24,8},{28,12},{32,48},... | collective-permute-start | bytes 61448 | tf_op jit(solution)/shard_map/ppermute | solution.py:34
  143.0 2.9 %collective-permute-start.9 = (f32[40,128]{1,0:T(8,128)S(1)}, f32[40,128]{1,0:T(8,128)S(1)}, u32[]{:S(2)}, u32[]{:S(2)}) collective-permute-start(f32[40,128]{1,0:T(8,128)S(1)} %fusion.30), channel_id=1, source_target_pairs={{0,64},{4,68},{8,72},{12,76},{16,80},{20,84},{24,88},{28,92},{32,9... | collective-permute-start | bytes 61448 | tf_op jit(solution)/shard_map/ppermute | solution.py:34
  145.9 4.4 %collective-permute-start.10 = (f32[40,128]{1,0:T(8,128)S(1)}, f32[40,128]{1,0:T(8,128)S(1)}, u32[]{:S(2)}, u32[]{:S(2)}) collective-permute-start(f32[40,128]{1,0:T(8,128)S(1)} %add.96), channel_id=1, source_target_pairs={{0,128},{4,132},{8,136},{12,140},{16,144},{20,148},{24,152},{28,15... | collective-permute-start | bytes 61448 | tf_op jit(solution)/shard_map/ppermute | solution.py:34
  154.1 11.9 %collective-permute-start.11 = (bf16[32,5120]{1,0:T(8,128)(2,1)S(1)}, bf16[32,5120]{1,0:T(8,128)(2,1)S(1)}, u32[]{:S(2)}, u32[]{:S(2)}) collective-permute-start(bf16[32,5120]{1,0:T(8,128)(2,1)S(1)} %slice.22), channel_id=1, source_target_pairs={{0,1},{1,2},{2,3},{3,0},{4,5},{5,6},{6,7},{7,4},{8,9},{9,10},{10,1... | collective-permute-start | bytes 983048 | tf_op jit(solution)/shard_map/ppermute | solution.py:38
  160.1 8.7 %collective-permute-start.12 = (bf16[32,5120]{1,0:T(8,128)(2,1)S(1)}, bf16[32,5120]{1,0:T(8,128)(2,1)S(1)}, u32[]{:S(2)}, u32[]{:S(2)}) collective-permute-start(bf16[32,5120]{1,0:T(8,128)(2,1)S(1)} %slice.23), channel_id=1, source_target_pairs={{0,3},{1,0},{2,1},{3,2},{4,7},{5,4},{6,5},{7,6},{8,11},{9,8},{10,9... | collective-permute-start | bytes 983048 | tf_op jit(solution)/shard_map/ppermute | solution.py:38
  172.6 9.0 %collective-permute-start.13 = (bf16[4,4,2,80,640]{4,3,2,1,0:T(8,128)(2,1)S(1)}, bf16[4,4,2,80,640]{4,3,2,1,0:T(8,128)(2,1)S(1)}, u32[]{:S(2)}, u32[]{:S(2)}) collective-permute-start(bf16[4,4,2,80,640]{4,3,2,1,0:T(8,128)(2,1)S(1)} %get-tuple-element.31), channel_id=1, source_target_pairs={{0,4},{4,0},{8,12},{12,8},{16,20},{20,16},{24,28},{28,24},{32,36},... | collective-permute-start | bytes 9830408 | tf_op jit(solution)/shard_map/ppermute | solution.py:34
  184.1 25.7 %all-to-all-start.2 = ((bf16[4,4,2,80,640]{4,3,2,1,0:T(8,128)(2,1)}), bf16[4,4,2,80,640]{4,3,2,1,0:T(8,128)(2,1)S(1)}, u32[]{:S(2)}, u32[]{:S(2)}) async-start(bf16[4,4,2,80,640]{4,3,2,1,0:T(8,128)(2,1)} %add_convert_fusion), calls=%async_computation.2 | async-start | bytes 6553600 | tf_op jit(solution)/shard_map/all_to_all | solution.py:42
  187.8 1.3 collective-permute-start.14
  189.1 2.9 %collective-permute-start.15 = (f32[40,128]{1,0:T(8,128)S(1)}, f32[40,128]{1,0:T(8,128)S(1)}, u32[]{:S(2)}, u32[]{:S(2)}) collective-permute-start(f32[40,128]{1,0:T(8,128)S(1)} %add.99), channel_id=1, source_target_pairs={{0,32},{4,36},{8,40},{12,44},{16,48},{20,52},{24,56},{28,60},{32,0... | collective-permute-start | bytes 61448 | tf_op jit(solution)/shard_map/ppermute | solution.py:34
  192.0 3.8 %collective-permute-start.16 = (f32[40,128]{1,0:T(8,128)S(1)}, f32[40,128]{1,0:T(8,128)S(1)}, u32[]{:S(2)}, u32[]{:S(2)}) collective-permute-start(f32[40,128]{1,0:T(8,128)S(1)} %add.100), channel_id=1, source_target_pairs={{0,1},{1,0},{2,3},{3,2},{4,5},{5,4},{6,7},{7,6},{8,9},{9,8},{10,11... | collective-permute-start | bytes 61448 | tf_op jit(solution)/shard_map/ppermute | solution.py:335
  195.8 6.5 %collective-permute-start.17 = (f32[40,128]{1,0:T(8,128)S(1)}, f32[40,128]{1,0:T(8,128)S(1)}, u32[]{:S(2)}, u32[]{:S(2)}) collective-permute-start(f32[40,128]{1,0:T(8,128)S(1)} %add.101), channel_id=1, source_target_pairs={{0,2},{1,3},{2,0},{3,1},{4,6},{5,7},{6,4},{7,5},{8,10},{9,11},{10,... | collective-permute-start | bytes 61448 | tf_op jit(solution)/shard_map/ppermute | solution.py:335
  211.4 3.7 %copy-start.6 = (f32[5,256,256]{1,2,0:T(8,128)S(1)}, f32[5,256,256]{1,2,0:T(8,128)}, u32[]{:S(2)}) copy-start(f32[5,256,256]{1,2,0:T(8,128)} %get-tuple-element.55) | copy-start | bytes 3932164
  211.4 3.7 %copy-start.11 = (bf16[256,640]{0,1:T(8,128)(2,1)S(1)}, bf16[256,640]{0,1:T(8,128)(2,1)}, u32[]{:S(2)}) copy-start(bf16[256,640]{0,1:T(8,128)(2,1)} %copy.38) | copy-start | bytes 983044
  211.4 16.9 %all-to-all-start.3 = ((bf16[8,80,640]{2,1,0:T(8,128)(2,1)}), bf16[8,80,640]{2,1,0:T(8,128)(2,1)S(1)}, u32[]{:S(2)}, u32[]{:S(2)}) async-start(bf16[8,80,640]{2,1,0:T(8,128)(2,1)} %bitcast.38), calls=%async_computation.3 | async-start | bytes 1638400 | tf_op jit(solution)/shard_map/all_to_all | solution.py:42
  215.1 1.3 copy-start.10
  216.8 1.0 copy-start.8
  217.8 1.2 copy-start.7
  (3 other events, 2.6 us)

commit v6 on v5

--- a/solution.py
+++ b/solution.py
@@ -89,7 +89,7 @@
 
 
 def branch_kernel(pos, att_ref, *refs):
-    p0, p1a, p3b, up, down, att_s, w_s = refs[8:]
+    p0, p1a, p1b, p2a, p2b, p3a, p3b, att_s, w_s = refs[8:]
     rows = att_ref.shape[0] // 4
     half = rows // 2
 
@@ -103,11 +103,11 @@
     ).astype(BF)
     p0[...] = prod[:rows]
     p1a[...] = prod[rows : rows + half]
+    p1b[...] = prod[rows + half : 2 * rows]
+    p2a[...] = prod[2 * rows : 2 * rows + half]
+    p2b[...] = prod[2 * rows + half : 3 * rows]
+    p3a[...] = prod[3 * rows : 3 * rows + half]
     p3b[...] = prod[3 * rows + half :]
-    up[pl.ds(0, half), :] = prod[2 * rows : 2 * rows + half]
-    up[pl.ds(half, half), :] = prod[rows + half : 2 * rows]
-    down[pl.ds(0, half), :] = prod[2 * rows + half : 3 * rows]
-    down[pl.ds(half, half), :] = prod[3 * rows : 3 * rows + half]
 
 
 def branch_part(pos, attended, cat, oth):
@@ -115,7 +115,7 @@
     seq = attended.shape[0]
     rows, span = seq // 4, 16 * piece
     total = 4 * span
-    heights = (rows, rows // 2, rows // 2, rows, rows)
+    heights = (rows,) + (rows // 2,) * 6
     return pl.pallas_call(
         branch_kernel,
         grid_spec=pltpu.PrefetchScalarGridSpec(
@@ -299,12 +299,13 @@
 
     cat, attended = lax.optimization_barrier((cat, attended))
     oth = swap(cat, FLIP_C)
-    p0, p1a, p3b, up, down = branch_part(pos, attended, cat, oth)
-    up, down = send_mp(up, 1), send_mp(down, -1)
-    up_a = send_mp(sum_f32(p1a, up[:half]).astype(BF), 1)
-    down_b = send_mp(sum_f32(p3b, down[:half]).astype(BF), -1)
-    up = jnp.concatenate([up_a, up[half:]])
-    down = jnp.concatenate([down[half:], down_b])
+    p0, p1a, p1b, p2a, p2b, p3a, p3b = branch_part(pos, attended, cat, oth)
+    ra, rb = send_mp(p2a, 1), send_mp(p2b, -1)
+    up_b, down_a = send_mp(p1b, 1), send_mp(p3a, -1)
+    up_a = send_mp(sum_f32(p1a, ra).astype(BF), 1)
+    down_b = send_mp(sum_f32(p3b, rb).astype(BF), -1)
+    up = jnp.concatenate([up_a, up_b])
+    down = jnp.concatenate([down_a, down_b])
     mixed = sum_f32(residual, p0, up, down)
     cot = cotangent.astype(F32)
     gscaled = cot * norm_gain

time: 230 us -> 228 us (level)
  waiting for transfers between devices: 111 us -> 104 us
  starting transfers between devices: 51.5 us -> 56 us
    ppermute x8 -> x10, starting transfers between devices: 30.2 us -> 18.5 us  [send_mp(): return lax.ppermute(value, 'mp', [(i, (i + step) % 4) for i in range(4)])]
    ppermute x8, starting transfers between devices: 7.39 us -> 17.1 us  [swap(): return lax.ppermute(value, 'dp', pairs)]
    all_to_all x3, waiting for transfers between devices: 24 us -> 18.8 us  [exchange(): return lax.all_to_all(blocks, 'dp', 0, 0, axis_index_groups=groups)]
    all_to_all x3, starting transfers between devices: 11.7 us -> 16.5 us  [exchange(): return lax.all_to_all(blocks, 'dp', 0, 0, axis_index_groups=groups)]
    ppermute x8 -> x10, waiting for transfers between devices: 58.1 us -> 60.8 us  [send_mp(): return lax.ppermute(value, 'mp', [(i, (i + step) % 4) for i in range(4)])]
    ppermute x8, waiting for transfers between devices: 20.6 us -> 17.9 us  [swap(): return lax.ppermute(value, 'dp', pairs)]
  transfers between devices with their start and end apart: 21 -> 23, of which waited for: 20 -> 18; matrix products, arithmetic and copies ran while one was open for 9% -> 9% of each run, Pallas kernels for 3% -> 3%
where the time goes in v6:
time: 228 us; the launch traced here: 227 us
  waiting for transfers between devices  104 us (46%)
  starting transfers between devices  56 us (25%)
  local copies, waits for them, and re-layouts  19.6 us (9%)
  blocking collectives  18.1 us (8%)
  Pallas kernels  16.4 us (7%)
  matrix products  6.57 us (3%)
  other arithmetic  5.19 us (2%)
    ppermute x10, waiting for transfers between devices, send_mp(): return lax.ppermute(value, 'mp', [(i, (i + step) % 4) for i in range(4)])  60.8 us
    all_to_all x3, waiting for transfers between devices, exchange(): return lax.all_to_all(blocks, 'dp', 0, 0, axis_index_groups=groups)  18.8 us
    ppermute x10, starting transfers between devices, send_mp(): return lax.ppermute(value, 'mp', [(i, (i + step) % 4) for i in range(4)])  18.5 us
    all_to_all x1, blocking collectives, exchange(): return lax.all_to_all(blocks, 'dp', 0, 0, axis_index_groups=groups)  18.1 us
    ppermute x8, waiting for transfers between devices, swap(): return lax.ppermute(value, 'dp', pairs)  17.9 us
    ppermute x8, starting transfers between devices, swap(): return lax.ppermute(value, 'dp', pairs)  17.1 us
    all_to_all x3, starting transfers between devices, exchange(): return lax.all_to_all(blocks, 'dp', 0, 0, axis_index_groups=groups)  16.5 us
    unnamed x34, local copies, waits for them, and re-layouts  12.3 us
  transfers between devices with their start and end apart: 23, of which 18 were waited for; matrix products, arithmetic and copies ran while one was open for 9% of the time, Pallas kernels for 3%

profile of v6, /device:TPU:1, one launch (start us, length us, event | category | flops | bytes accessed | tf_op | source)
XLA Modules:
  0.0 227.0 jit_solution(3859735515796400502)
XLA Ops:
  1.6 18.1 %all_to_all.20 = bf16[8,80,640]{2,1,0:T(8,128)(2,1)S(1)} all-to-all(bf16[8,80,640]{2,1,0:T(8,128)(2,1)S(1)} %broadcast_in_dim.20), channel_id=1, replica_groups={{0,32,8,40,16,48,24,56},{64,96,72,104,80,112,88,120},{128,160,136,168,1..., dimensions={0} | all-to-all | bytes 1638400 | tf_op jit(solution)/shard_map/all_to_all | solution.py:42
  19.7 2.0 broadcast_in_dim.22
  21.6 4.3 %all-to-all-start.1 = ((bf16[4,4,2,80,640]{4,3,2,1,0:T(8,128)(2,1)}), bf16[4,4,2,80,640]{4,3,2,1,0:T(8,128)(2,1)S(1)}, u32[]{:S(2)}, u32[]{:S(2)}) async-start(bf16[4,4,2,80,640]{4,3,2,1,0:T(8,128)(2,1)} %broadcast_in_dim.22), calls=%async_computation.1 | async-start | bytes 6553600 | tf_op jit(solution)/shard_map/all_to_all | solution.py:42
  31.6 2.7 %fusion.19 = (f32[5,256]{1,0:T(8,128)S(1)}, f32[5,256,256]{1,2,0:T(8,128)}) fusion(bf16[256,5,128]{0,2,1:T(8,128)(2,1)} %bitcast.40, bf16[256,5,128]{0,2,1:T(8,128)(2,1)} %bitcast.42, pred[256,256]{0,1:T(8,128)(4,1)S(1)} %fusion.15), kind=kOutput, calls=%fused_computation.41 | convolution fusion | flops 85197056 | bytes 2036736 | tf_op jit(solution)/shard_map/sub | solution.py:57
  34.4 2.4 %convolution_convert_fusion = bf16[5,256,128]{1,2,0:T(8,128)(2,1)} fusion(bf16[256,5,128]{0,2,1:T(8,128)(2,1)} %bitcast.46, f32[5,256,256]{1,2,0:T(8,128)} %get-tuple-element.59, f32[5,256]{1,0:T(8,128)S(1)} %get-tuple-element.58), kind=kOutput, calls=%fused_computation.23 | convolution fusion | flops 84705280 | bytes 1971200 | tf_op jit(solution)/shard_map/hts,shd->thd/dot_general | solution.py:297
  36.8 11.1 %all-to-all-done.1.refs_0_.refs_1_.refs_2_.refs_3_ = bf16[4,4,2,80,640]{4,3,2,1,0:T(8,128)(2,1)S(1)} async-done(((bf16[4,4,2,80,640]{4,3,2,1,0:T(8,128)(2,1)}), bf16[4,4,2,80,640]{4,3,2,1,0:T(8,128)(2,1)S(1)}, u32[]{:S(2)}, u32[]{:S(2)}) %all-to-all-start.1) | async-done | bytes 3276832 | tf_op jit(solution)/shard_map/all_to_all | solution.py:42
  47.9 3.4 %collective-permute-start = (bf16[4,4,2,80,640]{4,3,2,1,0:T(8,128)(2,1)S(1)}, bf16[4,4,2,80,640]{4,3,2,1,0:T(8,128)(2,1)}, u32[]{:S(2)}, u32[]{:S(2)}) collective-permute-start(bf16[4,4,2,80,640]{4,3,2,1,0:T(8,128)(2,1)S(1)} %all-to-all-done.1.refs_0_.refs_1_.refs_2_.refs_3_), channel_id=1, source_target_pairs={{0,4},{4,0},{8,12},{12,8},{16,20},{20,16},{24,28},{28,24},{32,36},... | collective-permute-start | bytes 9830408 | tf_op jit(solution)/shard_map/ppermute | solution.py:34
  53.2 3.6 %collective-permute-done.refs_4_.refs_5_.refs_6_.refs_7_ = bf16[4,4,2,80,640]{4,3,2,1,0:T(8,128)(2,1)} collective-permute-done((bf16[4,4,2,80,640]{4,3,2,1,0:T(8,128)(2,1)S(1)}, bf16[4,4,2,80,640]{4,3,2,1,0:T(8,128)(2,1)}, u32[]{:S(2)}, u32[]{:S(2)}) %collective-permute-start) | collective-permute-done | bytes 3276832 | tf_op jit(solution)/shard_map/ppermute | solution.py:34
  57.8 6.0 %branch_part.1 = (bf16[64,5120]{1,0:T(8,128)(2,1)S(1)}, bf16[32,5120]{1,0:T(8,128)(2,1)S(1)}, bf16[32,5120]{1,0:T(8,128)(2,1)S(1)}, bf16[32,5120]{1,0:T(8,128)(2...) custom-call(s32[2]{0:T(128)S(1)} %pad_add_fusion.pos, ...), custom_call_target="tpu_custom_call" | custom-call | flops 1677721600 | bytes 9175040 | tf_op jit(solution)/shard_map/branch_part/pallas_call | solution.py:119
  63.8 3.1 %collective-permute-start.1 = (bf16[32,5120]{1,0:T(8,128)(2,1)S(1)}, bf16[32,5120]{1,0:T(8,128)(2,1)S(1)}, u32[]{:S(2)}, u32[]{:S(2)}) collective-permute-start(bf16[32,5120]{1,0:T(8,128)(2,1)S(1)} %get-tuple-element.28), channel_id=1, source_target_pairs={{0,1},{1,2},{2,3},{3,0},{4,5},{5,6},{6,7},{7,4},{8,9},{9,10},{10,1... | collective-permute-start | bytes 983048 | tf_op jit(solution)/shard_map/ppermute | solution.py:38
  66.9 3.3 %collective-permute-start.3 = (bf16[32,5120]{1,0:T(8,128)(2,1)S(1)}, bf16[32,5120]{1,0:T(8,128)(2,1)S(1)}, u32[]{:S(2)}, u32[]{:S(2)}) collective-permute-start(bf16[32,5120]{1,0:T(8,128)(2,1)S(1)} %get-tuple-element.29), channel_id=1, source_target_pairs={{0,1},{1,2},{2,3},{3,0},{4,5},{5,6},{6,7},{7,4},{8,9},{9,10},{10,1... | collective-permute-start | bytes 983048 | tf_op jit(solution)/shard_map/ppermute | solution.py:38
  71.5 12.1 %collective-permute-done.1 = bf16[32,5120]{1,0:T(8,128)(2,1)S(1)} collective-permute-done((bf16[32,5120]{1,0:T(8,128)(2,1)S(1)}, bf16[32,5120]{1,0:T(8,128)(2,1)S(1)}, u32[]{:S(2)}, u32[]{:S(2)}) %collective-permute-start.1) | collective-permute-done | bytes 327712 | tf_op jit(solution)/shard_map/ppermute | solution.py:38
  83.7 2.0 collective-permute-start.2
  85.6 16.2 %collective-permute-done.5 = bf16[32,5120]{1,0:T(8,128)(2,1)S(1)} collective-permute-done((bf16[32,5120]{1,0:T(8,128)(2,1)S(1)}, bf16[32,5120]{1,0:T(8,128)(2,1)S(1)}, u32[]{:S(2)}, u32[]{:S(2)}) %collective-permute-start.5) | collective-permute-done | bytes 327712 | tf_op jit(solution)/shard_map/ppermute | solution.py:38
  103.5 8.7 %collective-permute-done.2 = bf16[32,5120]{1,0:T(8,128)(2,1)S(1)} collective-permute-done((bf16[32,5120]{1,0:T(8,128)(2,1)S(1)}, bf16[32,5120]{1,0:T(8,128)(2,1)S(1)}, u32[]{:S(2)}, u32[]{:S(2)}) %collective-permute-start.2) | collective-permute-done | bytes 327712 | tf_op jit(solution)/shard_map/ppermute | solution.py:38
  115.9 3.6 %collective-permute-start.8 = (bf16[64,5120]{1,0:T(8,128)(2,1)S(1)}, bf16[64,5120]{1,0:T(8,128)(2,1)S(1)}, u32[]{:S(2)}, u32[]{:S(2)}) collective-permute-start(bf16[64,5120]{1,0:T(8,128)(2,1)S(1)} %fusion.8.g0), channel_id=1, source_target_pairs={{0,3},{1,0},{2,1},{3,2},{4,7},{5,4},{6,5},{7,6},{8,11},{9,8},{10,9... | collective-permute-start | bytes 1966088 | tf_op jit(solution)/shard_map/ppermute | solution.py:38
  120.0 2.2 collective-permute-done.9
  123.5 3.2 %collective-permute-done.10 = f32[40,128]{1,0:T(8,128)S(1)} collective-permute-done((f32[40,128]{1,0:T(8,128)S(1)}, f32[40,128]{1,0:T(8,128)S(1)}, u32[]{:S(2)}, u32[]{:S(2)}) %collective-permute-start.10) | collective-permute-done | bytes 20512 | tf_op jit(solution)/shard_map/ppermute | solution.py:34
  127.0 2.6 %collective-permute-done.11 = f32[40,128]{1,0:T(8,128)S(1)} collective-permute-done((f32[40,128]{1,0:T(8,128)S(1)}, f32[40,128]{1,0:T(8,128)S(1)}, u32[]{:S(2)}, u32[]{:S(2)}) %collective-permute-start.11) | collective-permute-done | bytes 20512 | tf_op jit(solution)/shard_map/ppermute | solution.py:34
  130.2 3.7 %collective-permute-done.12 = f32[40,128]{1,0:T(8,128)S(1)} collective-permute-done((f32[40,128]{1,0:T(8,128)S(1)}, f32[40,128]{1,0:T(8,128)S(1)}, u32[]{:S(2)}, u32[]{:S(2)}) %collective-permute-start.12) | collective-permute-done | bytes 20512 | tf_op jit(solution)/shard_map/ppermute | solution.py:34
  134.0 12.7 %collective-permute-done.8.gp = bf16[64,5120]{1,0:T(8,128)(2,1)S(1)} collective-permute-done((bf16[64,5120]{1,0:T(8,128)(2,1)S(1)}, bf16[64,5120]{1,0:T(8,128)(2,1)S(1)}, u32[]{:S(2)}, u32[]{:S(2)}) %collective-permute-start.8) | collective-permute-done | bytes 655392 | tf_op jit(solution)/shard_map/ppermute | solution.py:38
  146.7 2.9 %collective-permute-start.13 = (bf16[32,5120]{1,0:T(8,128)(2,1)S(1)}, bf16[32,5120]{1,0:T(8,128)(2,1)S(1)}, u32[]{:S(2)}, u32[]{:S(2)}) collective-permute-start(bf16[32,5120]{1,0:T(8,128)(2,1)S(1)} %slice.6), channel_id=1, source_target_pairs={{0,1},{1,2},{2,3},{3,0},{4,5},{5,6},{6,7},{7,4},{8,9},{9,10},{10,1... | collective-permute-start | bytes 983048 | tf_op jit(solution)/shard_map/ppermute | solution.py:38
  150.4 8.9 %collective-permute-done.13.ga = bf16[32,5120]{1,0:T(8,128)(2,1)S(1)} collective-permute-done((bf16[32,5120]{1,0:T(8,128)(2,1)S(1)}, bf16[32,5120]{1,0:T(8,128)(2,1)S(1)}, u32[]{:S(2)}, u32[]{:S(2)}) %collective-permute-start.13) | collective-permute-done | bytes 327712 | tf_op jit(solution)/shard_map/ppermute | solution.py:38
  159.8 3.8 %weight_part.1 = (bf16[4,4,2,80,640]{4,3,2,1,0:T(8,128)(2,1)S(1)}, bf16[4,4,2,80,640]{4,3,2,1,0:T(8,128)(2,1)S(1)}) custom-call(s32[2]{0:T(128)S(1)} %pad_add_fusion.pos, bf16[64,5120]{1,0:T(8,128)(2,1)S(1)} %fusion.8.g0, bf16[64,5120]{1,0:T(8,128)(2,1)S(1)} %collective-permute-done.8.gp, bf16[32,5120]{1,0:T(8,128)(2,1)S(1)} %collective-permute-done.13.ga, ...), custom_call_target="tpu_custom_call" | custom-call | flops 1677721600 | bytes 9175040 | tf_op jit(solution)/shard_map/weight_part/pallas_call | solution.py:178
  165.3 5.9 %attended_part.1 = bf16[256,640]{1,0:T(8,128)(2,1)S(1)} custom-call(s32[2]{0:T(128)S(1)} %pad_add_fusion.pos, bf16[64,5120]{1,0:T(8,128)(2,1)S(1)} %fusion.8.g0, bf16[64,5120]{1,0:T(8,128)(2,1)S(1)} %collective-permute-done.8.gp, bf16[32,5120]{1,0:T(8,128)(2,1)S(1)} %collective-permute-done.13.ga, bf16[32,5120]{1,0:T(8,128)(2,1)S(1)} %collective-permute-done.14.gb, ...), custom_call_target="tpu_custom_call" | custom-call | flops 1677721600 | bytes 9175040 | tf_op jit(solution)/shard_map/attended_part/pallas_call | solution.py:222
  172.0 2.5 %add_convert_fusion = bf16[4,4,2,80,640]{4,3,2,1,0:T(8,128)(2,1)} fusion(bf16[4,4,2,80,640]{4,3,2,1,0:T(8,128)(2,1)S(1)} %collective-permute-done.15, bf16[4,4,2,80,640]{4,3,2,1,0:T(8,128)(2,1)S(1)} %get-tuple-element.37), kind=kLoop, calls=%fused_computation.1 | loop fusion | flops 6553600 | bytes 9830400 | tf_op jit(solution)/shard_map/convert_element_type | solution.py:332
  174.5 3.7 %all-to-all-start.2 = ((bf16[4,4,2,80,640]{4,3,2,1,0:T(8,128)(2,1)}), bf16[4,4,2,80,640]{4,3,2,1,0:T(8,128)(2,1)S(1)}, u32[]{:S(2)}, u32[]{:S(2)}) async-start(bf16[4,4,2,80,640]{4,3,2,1,0:T(8,128)(2,1)} %add_convert_fusion), calls=%async_computation.2 | async-start | bytes 6553600 | tf_op jit(solution)/shard_map/all_to_all | solution.py:42
  179.5 9.0 %collective-permute-start.17 = (f32[40,128]{1,0:T(8,128)S(1)}, f32[40,128]{1,0:T(8,128)S(1)}, u32[]{:S(2)}, u32[]{:S(2)}) collective-permute-start(f32[40,128]{1,0:T(8,128)S(1)} %add.99), channel_id=1, source_target_pairs={{0,32},{4,36},{8,40},{12,44},{16,48},{20,52},{24,56},{28,60},{32,0... | collective-permute-start | bytes 61448 | tf_op jit(solution)/shard_map/ppermute | solution.py:34
  190.0 2.7 %collective-permute-start.18 = (f32[40,128]{1,0:T(8,128)S(1)}, f32[40,128]{1,0:T(8,128)S(1)}, u32[]{:S(2)}, u32[]{:S(2)}) collective-permute-start(f32[40,128]{1,0:T(8,128)S(1)} %add.100), channel_id=1, source_target_pairs={{0,1},{1,0},{2,3},{3,2},{4,5},{5,4},{6,7},{7,6},{8,9},{9,8},{10,11... | collective-permute-start | bytes 61448 | tf_op jit(solution)/shard_map/ppermute | solution.py:336
  195.4 5.3 %collective-permute-done.19 = f32[40,128]{1,0:T(8,128)S(1)} collective-permute-done((f32[40,128]{1,0:T(8,128)S(1)}, f32[40,128]{1,0:T(8,128)S(1)}, u32[]{:S(2)}, u32[]{:S(2)}) %collective-permute-start.19) | collective-permute-done | bytes 20512 | tf_op jit(solution)/shard_map/ppermute | solution.py:336
  204.2 8.5 %all-to-all-start.3 = ((bf16[8,80,640]{2,1,0:T(8,128)(2,1)}), bf16[8,80,640]{2,1,0:T(8,128)(2,1)S(1)}, u32[]{:S(2)}, u32[]{:S(2)}) async-start(bf16[8,80,640]{2,1,0:T(8,128)(2,1)} %bitcast.38), calls=%async_computation.3 | async-start | bytes 1638400 | tf_op jit(solution)/shard_map/all_to_all | solution.py:42
  218.4 7.8 %all-to-all-done.3 = bf16[8,80,640]{2,1,0:T(8,128)(2,1)S(1)} async-done(((bf16[8,80,640]{2,1,0:T(8,128)(2,1)}), bf16[8,80,640]{2,1,0:T(8,128)(2,1)S(1)}, u32[]{:S(2)}, u32[]{:S(2)}) %all-to-all-start.3) | async-done | bytes 819232 | tf_op jit(solution)/shard_map/all_to_all | solution.py:42
  (87 shorter events, 38.6 us)
Async XLA Ops:
  21.6 26.2 %all-to-all-start.1 = ((bf16[4,4,2,80,640]{4,3,2,1,0:T(8,128)(2,1)}), bf16[4,4,2,80,640]{4,3,2,1,0:T(8,128)(2,1)S(1)}, u32[]{:S(2)}, u32[]{:S(2)}) async-start(bf16[4,4,2,80,640]{4,3,2,1,0:T(8,128)(2,1)} %broadcast_in_dim.22), calls=%async_computation.1 | async-start | bytes 6553600 | tf_op jit(solution)/shard_map/all_to_all | solution.py:42
  25.9 5.6 %copy-start.13 = (s32[256]{0:T(256)S(1)}, s32[256]{0:T(256)}, u32[]{:S(2)}) copy-start(s32[256]{0:T(256)} %param.15) | copy-start | bytes 3076
  47.9 9.0 %collective-permute-start = (bf16[4,4,2,80,640]{4,3,2,1,0:T(8,128)(2,1)S(1)}, bf16[4,4,2,80,640]{4,3,2,1,0:T(8,128)(2,1)}, u32[]{:S(2)}, u32[]{:S(2)}) collective-permute-start(bf16[4,4,2,80,640]{4,3,2,1,0:T(8,128)(2,1)S(1)} %all-to-all-done.1.refs_0_.refs_1_.refs_2_.refs_3_), channel_id=1, source_target_pairs={{0,4},{4,0},{8,12},{12,8},{16,20},{20,16},{24,28},{28,24},{32,36},... | collective-permute-start | bytes 9830408 | tf_op jit(solution)/shard_map/ppermute | solution.py:34
  63.8 50.2 %copy-start.9 = (bf16[64,5120]{1,0:T(8,128)(2,1)S(1)}, bf16[64,5120]{1,0:T(8,128)(2,1)}, u32[]{:S(2)}) copy-start(bf16[64,5120]{1,0:T(8,128)(2,1)} %param.11) | copy-start | bytes 1966084
  63.8 19.8 %collective-permute-start.1 = (bf16[32,5120]{1,0:T(8,128)(2,1)S(1)}, bf16[32,5120]{1,0:T(8,128)(2,1)S(1)}, u32[]{:S(2)}, u32[]{:S(2)}) collective-permute-start(bf16[32,5120]{1,0:T(8,128)(2,1)S(1)} %get-tuple-element.28), channel_id=1, source_target_pairs={{0,1},{1,2},{2,3},{3,0},{4,5},{5,6},{6,7},{7,4},{8,9},{9,10},{10,1... | collective-permute-start | bytes 983048 | tf_op jit(solution)/shard_map/ppermute | solution.py:38
  66.9 36.6 %collective-permute-start.3 = (bf16[32,5120]{1,0:T(8,128)(2,1)S(1)}, bf16[32,5120]{1,0:T(8,128)(2,1)S(1)}, u32[]{:S(2)}, u32[]{:S(2)}) collective-permute-start(bf16[32,5120]{1,0:T(8,128)(2,1)S(1)} %get-tuple-element.29), channel_id=1, source_target_pairs={{0,1},{1,2},{2,3},{3,0},{4,5},{5,6},{6,7},{7,4},{8,9},{9,10},{10,1... | collective-permute-start | bytes 983048 | tf_op jit(solution)/shard_map/ppermute | solution.py:38
  70.2 33.4 %collective-permute-start.4 = (bf16[32,5120]{1,0:T(8,128)(2,1)S(1)}, bf16[32,5120]{1,0:T(8,128)(2,1)S(1)}, u32[]{:S(2)}, u32[]{:S(2)}) collective-permute-start(bf16[32,5120]{1,0:T(8,128)(2,1)S(1)} %get-tuple-element.30), channel_id=1, source_target_pairs={{0,3},{1,0},{2,1},{3,2},{4,7},{5,4},{6,5},{7,6},{8,11},{9,8},{10,9... | collective-permute-start | bytes 983048 | tf_op jit(solution)/shard_map/ppermute | solution.py:38
  70.5 31.4 %collective-permute-start.5 = (bf16[32,5120]{1,0:T(8,128)(2,1)S(1)}, bf16[32,5120]{1,0:T(8,128)(2,1)S(1)}, u32[]{:S(2)}, u32[]{:S(2)}) collective-permute-start(bf16[32,5120]{1,0:T(8,128)(2,1)S(1)} %get-tuple-element.32), channel_id=1, source_target_pairs={{0,3},{1,0},{2,1},{3,2},{4,7},{5,4},{6,5},{7,6},{8,11},{9,8},{10,9... | collective-permute-start | bytes 983048 | tf_op jit(solution)/shard_map/ppermute | solution.py:38
  83.7 28.5 %collective-permute-start.2 = (bf16[32,5120]{1,0:T(8,128)(2,1)S(1)}, bf16[32,5120]{1,0:T(8,128)(2,1)S(1)}, u32[]{:S(2)}, u32[]{:S(2)}) collective-permute-start(bf16[32,5120]{1,0:T(8,128)(2,1)S(1)} %add_convert_fusion.2), channel_id=1, source_target_pairs={{0,1},{1,2},{2,3},{3,0},{4,5},{5,6},{6,7},{7,4},{8,9},{9,10},{10,1... | collective-permute-start | bytes 983048 | tf_op jit(solution)/shard_map/ppermute | solution.py:38
  101.9 12.1 %collective-permute-start.6 = (bf16[32,5120]{1,0:T(8,128)(2,1)S(1)}, bf16[32,5120]{1,0:T(8,128)(2,1)S(1)}, u32[]{:S(2)}, u32[]{:S(2)}) collective-permute-start(bf16[32,5120]{1,0:T(8,128)(2,1)S(1)} %add_convert_fusion.1), channel_id=1, source_target_pairs={{0,3},{1,0},{2,1},{3,2},{4,7},{5,4},{6,5},{7,6},{8,11},{9,8},{10,9... | collective-permute-start | bytes 983048 | tf_op jit(solution)/shard_map/ppermute | solution.py:38
  114.0 1.1 copy-start.12
  115.9 49.4 %copy-start.1 = (bf16[64,5120]{1,0:T(8,128)(2,1)}, bf16[64,5120]{1,0:T(8,128)(2,1)S(1)}, u32[]{:S(2)}) copy-start(bf16[64,5120]{1,0:T(8,128)(2,1)S(1)} %fusion.8.g0) | copy-start | bytes 1966084
  115.9 43.9 %copy-start.4 = (bf16[256,640]{1,0:T(8,128)(2,1)S(1)}, bf16[256,640]{1,0:T(8,128)(2,1)}, u32[]{:S(2)}) copy-start(bf16[256,640]{1,0:T(8,128)(2,1)} %copy.36.att_ref) | copy-start | bytes 983044
  115.9 30.7 %collective-permute-start.8 = (bf16[64,5120]{1,0:T(8,128)(2,1)S(1)}, bf16[64,5120]{1,0:T(8,128)(2,1)S(1)}, u32[]{:S(2)}, u32[]{:S(2)}) collective-permute-start(bf16[64,5120]{1,0:T(8,128)(2,1)S(1)} %fusion.8.g0), channel_id=1, source_target_pairs={{0,3},{1,0},{2,1},{3,2},{4,7},{5,4},{6,5},{7,6},{8,11},{9,8},{10,9... | collective-permute-start | bytes 1966088 | tf_op jit(solution)/shard_map/ppermute | solution.py:38
  119.5 27.1 %collective-permute-start.7 = (bf16[64,5120]{1,0:T(8,128)(2,1)S(1)}, bf16[64,5120]{1,0:T(8,128)(2,1)S(1)}, u32[]{:S(2)}, u32[]{:S(2)}) collective-permute-start(bf16[64,5120]{1,0:T(8,128)(2,1)S(1)} %fusion.8.g0), channel_id=1, source_target_pairs={{0,1},{1,2},{2,3},{3,0},{4,5},{5,6},{6,7},{7,4},{8,9},{9,10},{10,1... | collective-permute-start | bytes 1966088 | tf_op jit(solution)/shard_map/ppermute | solution.py:38
  119.5 2.6 %collective-permute-start.9 = (f32[40,128]{1,0:T(8,128)S(1)}, f32[40,128]{1,0:T(8,128)S(1)}, u32[]{:S(2)}, u32[]{:S(2)}) collective-permute-start(f32[40,128]{1,0:T(8,128)S(1)} %bitcast.52), channel_id=1, source_target_pairs={{0,8},{4,12},{8,0},{12,4},{16,24},{20,28},{24,16},{28,20},{32,40},... | collective-permute-start | bytes 61448 | tf_op jit(solution)/shard_map/ppermute | solution.py:34
  122.2 4.4 %collective-permute-start.10 = (f32[40,128]{1,0:T(8,128)S(1)}, f32[40,128]{1,0:T(8,128)S(1)}, u32[]{:S(2)}, u32[]{:S(2)}) collective-permute-start(f32[40,128]{1,0:T(8,128)S(1)} %bitcast_add_fusion), channel_id=1, source_target_pairs={{0,16},{4,20},{8,24},{12,28},{16,0},{20,4},{24,8},{28,12},{32,48},... | collective-permute-start | bytes 61448 | tf_op jit(solution)/shard_map/ppermute | solution.py:34
  126.6 2.9 %collective-permute-start.11 = (f32[40,128]{1,0:T(8,128)S(1)}, f32[40,128]{1,0:T(8,128)S(1)}, u32[]{:S(2)}, u32[]{:S(2)}) collective-permute-start(f32[40,128]{1,0:T(8,128)S(1)} %fusion.30), channel_id=1, source_target_pairs={{0,64},{4,68},{8,72},{12,76},{16,80},{20,84},{24,88},{28,92},{32,9... | collective-permute-start | bytes 61448 | tf_op jit(solution)/shard_map/ppermute | solution.py:34
  129.6 4.4 %collective-permute-start.12 = (f32[40,128]{1,0:T(8,128)S(1)}, f32[40,128]{1,0:T(8,128)S(1)}, u32[]{:S(2)}, u32[]{:S(2)}) collective-permute-start(f32[40,128]{1,0:T(8,128)S(1)} %add.96), channel_id=1, source_target_pairs={{0,128},{4,132},{8,136},{12,140},{16,144},{20,148},{24,152},{28,15... | collective-permute-start | bytes 61448 | tf_op jit(solution)/shard_map/ppermute | solution.py:34
  146.7 12.6 %collective-permute-start.13 = (bf16[32,5120]{1,0:T(8,128)(2,1)S(1)}, bf16[32,5120]{1,0:T(8,128)(2,1)S(1)}, u32[]{:S(2)}, u32[]{:S(2)}) collective-permute-start(bf16[32,5120]{1,0:T(8,128)(2,1)S(1)} %slice.6), channel_id=1, source_target_pairs={{0,1},{1,2},{2,3},{3,0},{4,5},{5,6},{6,7},{7,4},{8,9},{9,10},{10,1... | collective-permute-start | bytes 983048 | tf_op jit(solution)/shard_map/ppermute | solution.py:38
  149.6 10.2 %collective-permute-start.14 = (bf16[32,5120]{1,0:T(8,128)(2,1)S(1)}, bf16[32,5120]{1,0:T(8,128)(2,1)S(1)}, u32[]{:S(2)}, u32[]{:S(2)}) collective-permute-start(bf16[32,5120]{1,0:T(8,128)(2,1)S(1)} %slice.7), channel_id=1, source_target_pairs={{0,3},{1,0},{2,1},{3,2},{4,7},{5,4},{6,5},{7,6},{8,11},{9,8},{10,9... | collective-permute-start | bytes 983048 | tf_op jit(solution)/shard_map/ppermute | solution.py:38
  163.6 8.4 %collective-permute-start.15 = (bf16[4,4,2,80,640]{4,3,2,1,0:T(8,128)(2,1)S(1)}, bf16[4,4,2,80,640]{4,3,2,1,0:T(8,128)(2,1)S(1)}, u32[]{:S(2)}, u32[]{:S(2)}) collective-permute-start(bf16[4,4,2,80,640]{4,3,2,1,0:T(8,128)(2,1)S(1)} %get-tuple-element.35), channel_id=1, source_target_pairs={{0,4},{4,0},{8,12},{12,8},{16,20},{20,16},{24,28},{28,24},{32,36},... | collective-permute-start | bytes 9830408 | tf_op jit(solution)/shard_map/ppermute | solution.py:34
  174.5 28.1 %all-to-all-start.2 = ((bf16[4,4,2,80,640]{4,3,2,1,0:T(8,128)(2,1)}), bf16[4,4,2,80,640]{4,3,2,1,0:T(8,128)(2,1)S(1)}, u32[]{:S(2)}, u32[]{:S(2)}) async-start(bf16[4,4,2,80,640]{4,3,2,1,0:T(8,128)(2,1)} %add_convert_fusion), calls=%async_computation.2 | async-start | bytes 6553600 | tf_op jit(solution)/shard_map/all_to_all | solution.py:42
  178.2 1.3 collective-permute-start.16
  179.5 10.5 %collective-permute-start.17 = (f32[40,128]{1,0:T(8,128)S(1)}, f32[40,128]{1,0:T(8,128)S(1)}, u32[]{:S(2)}, u32[]{:S(2)}) collective-permute-start(f32[40,128]{1,0:T(8,128)S(1)} %add.99), channel_id=1, source_target_pairs={{0,32},{4,36},{8,40},{12,44},{16,48},{20,52},{24,56},{28,60},{32,0... | collective-permute-start | bytes 61448 | tf_op jit(solution)/shard_map/ppermute | solution.py:34
  190.0 4.1 %collective-permute-start.18 = (f32[40,128]{1,0:T(8,128)S(1)}, f32[40,128]{1,0:T(8,128)S(1)}, u32[]{:S(2)}, u32[]{:S(2)}) collective-permute-start(f32[40,128]{1,0:T(8,128)S(1)} %add.100), channel_id=1, source_target_pairs={{0,1},{1,0},{2,3},{3,2},{4,5},{5,4},{6,7},{7,6},{8,9},{9,8},{10,11... | collective-permute-start | bytes 61448 | tf_op jit(solution)/shard_map/ppermute | solution.py:336
  194.1 6.5 %collective-permute-start.19 = (f32[40,128]{1,0:T(8,128)S(1)}, f32[40,128]{1,0:T(8,128)S(1)}, u32[]{:S(2)}, u32[]{:S(2)}) collective-permute-start(f32[40,128]{1,0:T(8,128)S(1)} %add.101), channel_id=1, source_target_pairs={{0,2},{1,3},{2,0},{3,1},{4,6},{5,7},{6,4},{7,5},{8,10},{9,11},{10,... | collective-permute-start | bytes 61448 | tf_op jit(solution)/shard_map/ppermute | solution.py:336
  204.2 8.5 %copy-start.6 = (f32[5,256,256]{1,2,0:T(8,128)S(1)}, f32[5,256,256]{1,2,0:T(8,128)}, u32[]{:S(2)}) copy-start(f32[5,256,256]{1,2,0:T(8,128)} %get-tuple-element.59) | copy-start | bytes 3932164
  204.2 8.5 %copy-start.11 = (bf16[256,640]{0,1:T(8,128)(2,1)S(1)}, bf16[256,640]{0,1:T(8,128)(2,1)}, u32[]{:S(2)}) copy-start(bf16[256,640]{0,1:T(8,128)(2,1)} %copy.38) | copy-start | bytes 983044
  204.2 22.0 %all-to-all-start.3 = ((bf16[8,80,640]{2,1,0:T(8,128)(2,1)}), bf16[8,80,640]{2,1,0:T(8,128)(2,1)S(1)}, u32[]{:S(2)}, u32[]{:S(2)}) async-start(bf16[8,80,640]{2,1,0:T(8,128)(2,1)} %bitcast.38), calls=%async_computation.3 | async-start | bytes 1638400 | tf_op jit(solution)/shard_map/all_to_all | solution.py:42
  212.7 1.3 copy-start.10
  215.4 1.2 copy-start.7
  (5 other events, 4.7 us)

commit v7 on v6

--- a/solution.py
+++ b/solution.py
@@ -137,17 +137,15 @@
     )(pos, attended, *[cat] * 4, *[oth] * 4)
 
 
-def gather_rows(g0, gp, ga, gb, gm, rows_s):
-    rows = g0.shape[0]
-    half = rows // 2
-    rows_s[pl.ds(0, rows), :] = g0[...]
-    rows_s[pl.ds(rows, rows), :] = gp[...]
-    rows_s[pl.ds(2 * rows, half), :] = ga[...]
-    rows_s[pl.ds(2 * rows + half, half), :] = gb[...]
-    rows_s[pl.ds(3 * rows, rows), :] = gm[...]
-
-
-def weight_kernel(pos, g0, gp, ga, gb, gm, att_ref, keep, send, att_s, rows_s):
+def gather_rows(parts, rows_s):
+    start = 0
+    for part in parts:
+        rows_s[pl.ds(start, part.shape[0]), :] = part[...]
+        start += part.shape[0]
+
+
+def weight_kernel(pos, *refs):
+    parts, (att_ref, keep, send, att_s, rows_s) = refs[:7], refs[7:]
     piece = keep.shape[3]
     c = pos[0]
     step = pl.program_id(0)
@@ -156,7 +154,7 @@
     def _():
         turn_tokens(pos, att_ref, att_s)
 
-    gather_rows(g0, gp, ga, gb, gm, rows_s)
+    gather_rows(parts, rows_s)
     prod = lax.dot_general(
         rows_s[...], att_s[...], (((0,), (0,)), ((), ())), preferred_element_type=F32
     ).astype(BF)
@@ -194,17 +192,18 @@
     )(pos, *parts, attended)
 
 
-def attended_kernel(pos, g0, gp, ga, gb, gm, *refs):
+def attended_kernel(pos, *refs):
+    parts, refs = refs[:7], refs[7:]
     out_ref, rows_s, w_s, acc = refs[8:]
     m = pos[1]
-    rows = g0.shape[0]
+    rows = parts[0].shape[0]
     step = pl.program_id(0)
 
     @pl.when(step == 0)
     def _():
         acc[...] = jnp.zeros_like(acc)
 
-    gather_rows(g0, gp, ga, gb, gm, rows_s)
+    gather_rows(parts, rows_s)
     assemble(pos[0], refs[:4], refs[4:8], w_s)
     acc[...] += jnp.dot(rows_s[...], w_s[...], preferred_element_type=F32)
 
@@ -321,12 +320,13 @@
         return total
 
     gain = jnp.sum(cot * mixed * inv, axis=0).reshape(d_model // 128, 128)
-    gm = send_mp(grad_residual, 1)
-    gp = send_mp(grad_residual, -1)
-    gm, gp, gain = tie((gm, gp, add_from(gain, (2, 4, 16, 32))))
-    ga = send_mp(gm[:half], 1)
-    gb = send_mp(gp[half:], -1)
-    parts = (grad_residual, gp, ga, gb, gm)
+    low, high = grad_residual[:half], grad_residual[half:]
+    gma, gpb = send_mp(low, 1), send_mp(high, -1)
+    gmb, gpa = send_mp(high, 1), send_mp(low, -1)
+    gma, gpb, gain = tie((gma, gpb, add_from(gain, (2, 4))))
+    ga, gb = send_mp(gma, 1), send_mp(gpb, -1)
+    gmb, gpa, gain = tie((gmb, gpa, add_from(gain, (16, 32))))
+    parts = (grad_residual, gpa, gpb, ga, gb, gma, gmb)
     keep, send = weight_part(pos, parts, attended, piece)
     swapped, grad_attended = tie((swap(send, FLIP_C), attended_part(pos, parts, cat, oth)))
     both = sum_f32(keep, swapped).astype(BF)

time: 228 us -> 224 us (0.982)
  waiting for transfers between devices: 104 us -> 95.8 us
  starting transfers between devices: 56 us -> 60.9 us
    ppermute x8, waiting for transfers between devices: 17.9 us -> 13 us  [swap(): return lax.ppermute(value, 'dp', pairs)]
    all_to_all x3, starting transfers between devices: 16.5 us -> 19.4 us  [exchange(): return lax.all_to_all(blocks, 'dp', 0, 0, axis_index_groups=groups)]
    ppermute x10 -> x12, waiting for transfers between devices: 60.8 us -> 58.5 us  [send_mp(): return lax.ppermute(value, 'mp', [(i, (i + step) % 4) for i in range(4)])]
    ppermute x10 -> x12, starting transfers between devices: 18.5 us -> 19.6 us  [send_mp(): return lax.ppermute(value, 'mp', [(i, (i + step) % 4) for i in range(4)])]
  transfers between devices with their start and end apart: 23 -> 25, of which waited for: 18 -> 19; matrix products, arithmetic and copies ran while one was open for 9% -> 9% of each run, Pallas kernels for 3% -> 3%
where the time goes in v7:
time: 224 us; the launch traced here: 223 us
  waiting for transfers between devices  95.8 us (43%)
  starting transfers between devices  60.9 us (27%)
  local copies, waits for them, and re-layouts  19.6 us (9%)
  blocking collectives  18.1 us (8%)
  Pallas kernels  16.5 us (7%)
  matrix products  6.59 us (3%)
  other arithmetic  5.19 us (2%)
    ppermute x12, waiting for transfers between devices, send_mp(): return lax.ppermute(value, 'mp', [(i, (i + step) % 4) for i in range(4)])  58.5 us
    ppermute x12, starting transfers between devices, send_mp(): return lax.ppermute(value, 'mp', [(i, (i + step) % 4) for i in range(4)])  19.6 us
    all_to_all x3, starting transfers between devices, exchange(): return lax.all_to_all(blocks, 'dp', 0, 0, axis_index_groups=groups)  19.4 us
    all_to_all x3, waiting for transfers between devices, exchange(): return lax.all_to_all(blocks, 'dp', 0, 0, axis_index_groups=groups)  18.1 us
    all_to_all x1, blocking collectives, exchange(): return lax.all_to_all(blocks, 'dp', 0, 0, axis_index_groups=groups)  18.1 us
    ppermute x8, starting transfers between devices, swap(): return lax.ppermute(value, 'dp', pairs)  17.1 us
    ppermute x8, waiting for transfers between devices, swap(): return lax.ppermute(value, 'dp', pairs)  13 us
    unnamed x34, local copies, waits for them, and re-layouts  12.3 us
  transfers between devices with their start and end apart: 25, of which 19 were waited for; matrix products, arithmetic and copies ran while one was open for 9% of the time, Pallas kernels for 3%

profile of v7, /device:TPU:1, one launch (start us, length us, event | category | flops | bytes accessed | tf_op | source)
XLA Modules:
  0.0 223.4 jit_solution(10927424135662872941)
XLA Ops:
  1.6 18.1 %all_to_all.20 = bf16[8,80,640]{2,1,0:T(8,128)(2,1)S(1)} all-to-all(bf16[8,80,640]{2,1,0:T(8,128)(2,1)S(1)} %broadcast_in_dim.20), channel_id=1, replica_groups={{0,32,8,40,16,48,24,56},{64,96,72,104,80,112,88,120},{128,160,136,168,1..., dimensions={0} | all-to-all | bytes 1638400 | tf_op jit(solution)/shard_map/all_to_all | solution.py:42
  21.6 4.3 %all-to-all-start.1 = ((bf16[4,4,2,80,640]{4,3,2,1,0:T(8,128)(2,1)}), bf16[4,4,2,80,640]{4,3,2,1,0:T(8,128)(2,1)S(1)}, u32[]{:S(2)}, u32[]{:S(2)}) async-start(bf16[4,4,2,80,640]{4,3,2,1,0:T(8,128)(2,1)} %broadcast_in_dim.22), calls=%async_computation.1 | async-start | bytes 6553600 | tf_op jit(solution)/shard_map/all_to_all | solution.py:42
  31.6 2.8 %fusion.20 = (f32[5,256]{1,0:T(8,128)S(1)}, f32[5,256,256]{1,2,0:T(8,128)}) fusion(bf16[256,5,128]{0,2,1:T(8,128)(2,1)} %bitcast.40, bf16[256,5,128]{0,2,1:T(8,128)(2,1)} %bitcast.42, pred[256,256]{0,1:T(8,128)(4,1)S(1)} %fusion.15), kind=kOutput, calls=%fused_computation.42 | convolution fusion | flops 85197056 | bytes 2036736 | tf_op jit(solution)/shard_map/sub | solution.py:57
  34.4 2.4 %convolution_convert_fusion = bf16[5,256,128]{1,2,0:T(8,128)(2,1)} fusion(bf16[256,5,128]{0,2,1:T(8,128)(2,1)} %bitcast.46, f32[5,256,256]{1,2,0:T(8,128)} %get-tuple-element.67, f32[5,256]{1,0:T(8,128)S(1)} %get-tuple-element.66), kind=kOutput, calls=%fused_computation.23 | convolution fusion | flops 84705280 | bytes 1971200 | tf_op jit(solution)/shard_map/hts,shd->thd/dot_general | solution.py:296
  36.8 11.1 %all-to-all-done.1.refs_0_.refs_1_.refs_2_.refs_3_.refs_7_.refs_8_.refs_9_.refs_10_ = bf16[4,4,2,80,640]{4,3,2,1,0:T(8,128)(2,1)S(1)} async-done(((bf16[4,4,2,80,640]{4,3,2,1,0:T(8,128)(2,1)}), bf16[4,4,2,80,640]{4,3,2,1,0:T(8,128)(2,1)S(1)}, u32[]{:S(2)}, u32[]{:S(2)}) %all-to-all-start.1) | async-done | bytes 3276832 | tf_op jit(solution)/shard_map/all_to_all | solution.py:42
  47.9 3.4 %collective-permute-start = (bf16[4,4,2,80,640]{4,3,2,1,0:T(8,128)(2,1)S(1)}, bf16[4,4,2,80,640]{4,3,2,1,0:T(8,128)(2,1)}, u32[]{:S(2)}, u32[]{:S(2)}) collective-permute-start(bf16[4,4,2,80,640]{4,3,2,1,0:T(8,128)(2,1)S(1)} %all-to-all-done.1.refs_0_.refs_1_.refs_2_.refs_3_.refs_7_.refs_8_.refs_9_.refs_10_), channel_id=1, source_target_pairs={{0,4},{4,0},{8,12},{12,8},{16,20},{20,16},{24,28},{28,24},{32,36},... | collective-permute-start | bytes 9830408 | tf_op jit(solution)/shard_map/ppermute | solution.py:34
  53.2 3.6 %collective-permute-done.refs_4_.refs_5_.refs_6_.refs_7_.refs_11_.refs_12_.refs_13_.refs_14_ = bf16[4,4,2,80,640]{4,3,2,1,0:T(8,128)(2,1)} collective-permute-done((bf16[4,4,2,80,640]{4,3,2,1,0:T(8,128)(2,1)S(1)}, bf16[4,4,2,80,640]{4,3,2,1,0:T(8,128)(2,1)}, u32[]{:S(2)}, u32[]{:S(2)}) %collective-permute-start) | collective-permute-done | bytes 3276832 | tf_op jit(solution)/shard_map/ppermute | solution.py:34
  57.8 6.0 %branch_part.1 = (bf16[64,5120]{1,0:T(8,128)(2,1)S(1)}, bf16[32,5120]{1,0:T(8,128)(2,1)S(1)}, bf16[32,5120]{1,0:T(8,128)(2,1)S(1)}, bf16[32,5120]{1,0:T(8,128)(2...) custom-call(s32[2]{0:T(128)S(1)} %pad_add_fusion.pos, ...), custom_call_target="tpu_custom_call" | custom-call | flops 1677721600 | bytes 9175040 | tf_op jit(solution)/shard_map/branch_part/pallas_call | solution.py:119
  63.8 3.1 %collective-permute-start.1 = (bf16[32,5120]{1,0:T(8,128)(2,1)S(1)}, bf16[32,5120]{1,0:T(8,128)(2,1)S(1)}, u32[]{:S(2)}, u32[]{:S(2)}) collective-permute-start(bf16[32,5120]{1,0:T(8,128)(2,1)S(1)} %get-tuple-element.31), channel_id=1, source_target_pairs={{0,1},{1,2},{2,3},{3,0},{4,5},{5,6},{6,7},{7,4},{8,9},{9,10},{10,1... | collective-permute-start | bytes 983048 | tf_op jit(solution)/shard_map/ppermute | solution.py:38
  66.9 3.3 %collective-permute-start.3 = (bf16[32,5120]{1,0:T(8,128)(2,1)S(1)}, bf16[32,5120]{1,0:T(8,128)(2,1)S(1)}, u32[]{:S(2)}, u32[]{:S(2)}) collective-permute-start(bf16[32,5120]{1,0:T(8,128)(2,1)S(1)} %get-tuple-element.32), channel_id=1, source_target_pairs={{0,1},{1,2},{2,3},{3,0},{4,5},{5,6},{6,7},{7,4},{8,9},{9,10},{10,1... | collective-permute-start | bytes 983048 | tf_op jit(solution)/shard_map/ppermute | solution.py:38
  71.5 12.2 %collective-permute-done.1 = bf16[32,5120]{1,0:T(8,128)(2,1)S(1)} collective-permute-done((bf16[32,5120]{1,0:T(8,128)(2,1)S(1)}, bf16[32,5120]{1,0:T(8,128)(2,1)S(1)}, u32[]{:S(2)}, u32[]{:S(2)}) %collective-permute-start.1) | collective-permute-done | bytes 327712 | tf_op jit(solution)/shard_map/ppermute | solution.py:38
  83.7 2.0 collective-permute-start.2
  85.7 16.2 %collective-permute-done.5 = bf16[32,5120]{1,0:T(8,128)(2,1)S(1)} collective-permute-done((bf16[32,5120]{1,0:T(8,128)(2,1)S(1)}, bf16[32,5120]{1,0:T(8,128)(2,1)S(1)}, u32[]{:S(2)}, u32[]{:S(2)}) %collective-permute-start.5) | collective-permute-done | bytes 327712 | tf_op jit(solution)/shard_map/ppermute | solution.py:38
  103.5 8.7 %collective-permute-done.2 = bf16[32,5120]{1,0:T(8,128)(2,1)S(1)} collective-permute-done((bf16[32,5120]{1,0:T(8,128)(2,1)S(1)}, bf16[32,5120]{1,0:T(8,128)(2,1)S(1)}, u32[]{:S(2)}, u32[]{:S(2)}) %collective-permute-start.2) | collective-permute-done | bytes 327712 | tf_op jit(solution)/shard_map/ppermute | solution.py:38
  117.2 2.9 %collective-permute-start.10 = (bf16[32,5120]{1,0:T(8,128)(2,1)S(1)}, bf16[32,5120]{1,0:T(8,128)(2,1)S(1)}, u32[]{:S(2)}, u32[]{:S(2)}) collective-permute-start(bf16[32,5120]{1,0:T(8,128)(2,1)S(1)} %get-tuple-element.65), channel_id=1, source_target_pairs={{0,3},{1,0},{2,1},{3,2},{4,7},{5,4},{6,5},{7,6},{8,11},{9,8},{10,9... | collective-permute-start | bytes 983048 | tf_op jit(solution)/shard_map/ppermute | solution.py:38
  122.0 2.3 %collective-permute-start.8 = (bf16[32,5120]{1,0:T(8,128)(2,1)S(1)}, bf16[32,5120]{1,0:T(8,128)(2,1)S(1)}, u32[]{:S(2)}, u32[]{:S(2)}) collective-permute-start(bf16[32,5120]{1,0:T(8,128)(2,1)S(1)} %get-tuple-element.64), channel_id=1, source_target_pairs={{0,3},{1,0},{2,1},{3,2},{4,7},{5,4},{6,5},{7,6},{8,11},{9,8},{10,9... | collective-permute-start | bytes 983048 | tf_op jit(solution)/shard_map/ppermute | solution.py:38
  124.9 2.1 collective-permute-done.9.refs_5_
  127.0 6.0 %collective-permute-done.10.refs_2_ = bf16[32,5120]{1,0:T(8,128)(2,1)S(1)} collective-permute-done((bf16[32,5120]{1,0:T(8,128)(2,1)S(1)}, bf16[32,5120]{1,0:T(8,128)(2,1)S(1)}, u32[]{:S(2)}, u32[]{:S(2)}) %collective-permute-start.10) | collective-permute-done | bytes 327712 | tf_op jit(solution)/shard_map/ppermute | solution.py:38
  133.1 2.4 %collective-permute-start.15 = (bf16[32,5120]{1,0:T(8,128)(2,1)S(1)}, bf16[32,5120]{1,0:T(8,128)(2,1)S(1)}, u32[]{:S(2)}, u32[]{:S(2)}) collective-permute-start(bf16[32,5120]{1,0:T(8,128)(2,1)S(1)} %collective-permute-done.9.refs_5_), channel_id=1, source_target_pairs={{0,1},{1,2},{2,3},{3,0},{4,5},{5,6},{6,7},{7,4},{8,9},{9,10},{10,1... | collective-permute-start | bytes 983048 | tf_op jit(solution)/shard_map/ppermute | solution.py:38
  135.7 2.6 %collective-permute-done.13 = f32[40,128]{1,0:T(8,128)S(1)} collective-permute-done((f32[40,128]{1,0:T(8,128)S(1)}, f32[40,128]{1,0:T(8,128)S(1)}, u32[]{:S(2)}, u32[]{:S(2)}) %collective-permute-start.13) | collective-permute-done | bytes 20512 | tf_op jit(solution)/shard_map/ppermute | solution.py:34
  139.0 3.5 %collective-permute-done.14 = f32[40,128]{1,0:T(8,128)S(1)} collective-permute-done((f32[40,128]{1,0:T(8,128)S(1)}, f32[40,128]{1,0:T(8,128)S(1)}, u32[]{:S(2)}, u32[]{:S(2)}) %collective-permute-start.14) | collective-permute-done | bytes 20512 | tf_op jit(solution)/shard_map/ppermute | solution.py:34
  143.0 9.9 %collective-permute-done.16.refs_4_ = bf16[32,5120]{1,0:T(8,128)(2,1)S(1)} collective-permute-done((bf16[32,5120]{1,0:T(8,128)(2,1)S(1)}, bf16[32,5120]{1,0:T(8,128)(2,1)S(1)}, u32[]{:S(2)}, u32[]{:S(2)}) %collective-permute-start.16) | collective-permute-done | bytes 327712 | tf_op jit(solution)/shard_map/ppermute | solution.py:38
  153.9 3.8 %weight_part.1 = (bf16[4,4,2,80,640]{4,3,2,1,0:T(8,128)(2,1)S(1)}, bf16[4,4,2,80,640]{4,3,2,1,0:T(8,128)(2,1)S(1)}) custom-call(s32[2]{0:T(128)S(1)} %pad_add_fusion.pos, bf16[64,5120]{1,0:T(8,128)(2,1)S(1)} %fusion.8.refs_0_, bf16[32,5120]{1,0:T(8,128)(2,1)S(1)} %collective-permute-done.8.refs_1_, bf16[32,5120]{1,0:T(8,128)(2,1)S(1)} %collective-permute-done.10.refs_2_, ...), custom_call_target="tpu_custom_call" | custom-call | flops 1677721600 | bytes 9175040 | tf_op jit(solution)/shard_map/weight_part/pallas_call | solution.py:176
  157.7 2.3 %collective-permute-start.17 = (bf16[4,4,2,80,640]{4,3,2,1,0:T(8,128)(2,1)S(1)}, bf16[4,4,2,80,640]{4,3,2,1,0:T(8,128)(2,1)S(1)}, u32[]{:S(2)}, u32[]{:S(2)}) collective-permute-start(bf16[4,4,2,80,640]{4,3,2,1,0:T(8,128)(2,1)S(1)} %get-tuple-element.41), channel_id=1, source_target_pairs={{0,4},{4,0},{8,12},{12,8},{16,20},{20,16},{24,28},{28,24},{32,36},... | collective-permute-start | bytes 9830408 | tf_op jit(solution)/shard_map/ppermute | solution.py:34
  160.1 5.9 %attended_part.1 = bf16[256,640]{1,0:T(8,128)(2,1)S(1)} custom-call(s32[2]{0:T(128)S(1)} %pad_add_fusion.pos, bf16[64,5120]{1,0:T(8,128)(2,1)S(1)} %fusion.8.refs_0_, bf16[32,5120]{1,0:T(8,128)(2,1)S(1)} %collective-permute-done.8.refs_1_, bf16[32,5120]{1,0:T(8,128)(2,1)S(1)} %collective-permute-done.10.refs_2_, ...), custom_call_target="tpu_custom_call" | custom-call | flops 1677721600 | bytes 9175040 | tf_op jit(solution)/shard_map/attended_part/pallas_call | solution.py:221
  166.8 2.5 %add_convert_fusion = bf16[4,4,2,80,640]{4,3,2,1,0:T(8,128)(2,1)} fusion(bf16[4,4,2,80,640]{4,3,2,1,0:T(8,128)(2,1)S(1)} %collective-permute-done.17, bf16[4,4,2,80,640]{4,3,2,1,0:T(8,128)(2,1)S(1)} %get-tuple-element.43), kind=kLoop, calls=%fused_computation.1 | loop fusion | flops 6553600 | bytes 9830400 | tf_op jit(solution)/shard_map/convert_element_type | solution.py:332
  169.2 6.7 %all-to-all-start.2 = ((bf16[4,4,2,80,640]{4,3,2,1,0:T(8,128)(2,1)}), bf16[4,4,2,80,640]{4,3,2,1,0:T(8,128)(2,1)S(1)}, u32[]{:S(2)}, u32[]{:S(2)}) async-start(bf16[4,4,2,80,640]{4,3,2,1,0:T(8,128)(2,1)} %add_convert_fusion), calls=%async_computation.2 | async-start | bytes 6553600 | tf_op jit(solution)/shard_map/all_to_all | solution.py:42
  177.1 8.3 %collective-permute-start.19 = (f32[40,128]{1,0:T(8,128)S(1)}, f32[40,128]{1,0:T(8,128)S(1)}, u32[]{:S(2)}, u32[]{:S(2)}) collective-permute-start(f32[40,128]{1,0:T(8,128)S(1)} %add.99), channel_id=1, source_target_pairs={{0,32},{4,36},{8,40},{12,44},{16,48},{20,52},{24,56},{28,60},{32,0... | collective-permute-start | bytes 61448 | tf_op jit(solution)/shard_map/ppermute | solution.py:34
  186.8 2.9 %collective-permute-start.20 = (f32[40,128]{1,0:T(8,128)S(1)}, f32[40,128]{1,0:T(8,128)S(1)}, u32[]{:S(2)}, u32[]{:S(2)}) collective-permute-start(f32[40,128]{1,0:T(8,128)S(1)} %add.100), channel_id=1, source_target_pairs={{0,1},{1,0},{2,3},{3,2},{4,5},{5,4},{6,7},{7,6},{8,9},{9,8},{10,11... | collective-permute-start | bytes 61448 | tf_op jit(solution)/shard_map/ppermute | solution.py:336
  193.1 4.7 %collective-permute-done.21 = f32[40,128]{1,0:T(8,128)S(1)} collective-permute-done((f32[40,128]{1,0:T(8,128)S(1)}, f32[40,128]{1,0:T(8,128)S(1)}, u32[]{:S(2)}, u32[]{:S(2)}) %collective-permute-start.21) | collective-permute-done | bytes 20512 | tf_op jit(solution)/shard_map/ppermute | solution.py:336
  201.4 8.4 %all-to-all-start.3 = ((bf16[8,80,640]{2,1,0:T(8,128)(2,1)}), bf16[8,80,640]{2,1,0:T(8,128)(2,1)S(1)}, u32[]{:S(2)}, u32[]{:S(2)}) async-start(bf16[8,80,640]{2,1,0:T(8,128)(2,1)} %bitcast.38), calls=%async_computation.3 | async-start | bytes 1638400 | tf_op jit(solution)/shard_map/all_to_all | solution.py:42
  215.5 7.1 %all-to-all-done.3 = bf16[8,80,640]{2,1,0:T(8,128)(2,1)S(1)} async-done(((bf16[8,80,640]{2,1,0:T(8,128)(2,1)}), bf16[8,80,640]{2,1,0:T(8,128)(2,1)S(1)}, u32[]{:S(2)}, u32[]{:S(2)}) %all-to-all-start.3) | async-done | bytes 819232 | tf_op jit(solution)/shard_map/all_to_all | solution.py:42
  (90 shorter events, 41.1 us)
Async XLA Ops:
  21.6 26.2 %all-to-all-start.1 = ((bf16[4,4,2,80,640]{4,3,2,1,0:T(8,128)(2,1)}), bf16[4,4,2,80,640]{4,3,2,1,0:T(8,128)(2,1)S(1)}, u32[]{:S(2)}, u32[]{:S(2)}) async-start(bf16[4,4,2,80,640]{4,3,2,1,0:T(8,128)(2,1)} %broadcast_in_dim.22), calls=%async_computation.1 | async-start | bytes 6553600 | tf_op jit(solution)/shard_map/all_to_all | solution.py:42
  25.9 5.6 %copy-start.13 = (s32[256]{0:T(256)S(1)}, s32[256]{0:T(256)}, u32[]{:S(2)}) copy-start(s32[256]{0:T(256)} %param.15) | copy-start | bytes 3076
  47.9 9.0 %collective-permute-start = (bf16[4,4,2,80,640]{4,3,2,1,0:T(8,128)(2,1)S(1)}, bf16[4,4,2,80,640]{4,3,2,1,0:T(8,128)(2,1)}, u32[]{:S(2)}, u32[]{:S(2)}) collective-permute-start(bf16[4,4,2,80,640]{4,3,2,1,0:T(8,128)(2,1)S(1)} %all-to-all-done.1.refs_0_.refs_1_.refs_2_.refs_3_.refs_7_.refs_8_.refs_9_.refs_10_), channel_id=1, source_target_pairs={{0,4},{4,0},{8,12},{12,8},{16,20},{20,16},{24,28},{28,24},{32,36},... | collective-permute-start | bytes 9830408 | tf_op jit(solution)/shard_map/ppermute | solution.py:34
  63.8 50.3 %copy-start.9 = (bf16[64,5120]{1,0:T(8,128)(2,1)S(1)}, bf16[64,5120]{1,0:T(8,128)(2,1)}, u32[]{:S(2)}) copy-start(bf16[64,5120]{1,0:T(8,128)(2,1)} %param.11) | copy-start | bytes 1966084
  63.8 19.8 %collective-permute-start.1 = (bf16[32,5120]{1,0:T(8,128)(2,1)S(1)}, bf16[32,5120]{1,0:T(8,128)(2,1)S(1)}, u32[]{:S(2)}, u32[]{:S(2)}) collective-permute-start(bf16[32,5120]{1,0:T(8,128)(2,1)S(1)} %get-tuple-element.31), channel_id=1, source_target_pairs={{0,1},{1,2},{2,3},{3,0},{4,5},{5,6},{6,7},{7,4},{8,9},{9,10},{10,1... | collective-permute-start | bytes 983048 | tf_op jit(solution)/shard_map/ppermute | solution.py:38
  66.9 36.6 %collective-permute-start.3 = (bf16[32,5120]{1,0:T(8,128)(2,1)S(1)}, bf16[32,5120]{1,0:T(8,128)(2,1)S(1)}, u32[]{:S(2)}, u32[]{:S(2)}) collective-permute-start(bf16[32,5120]{1,0:T(8,128)(2,1)S(1)} %get-tuple-element.32), channel_id=1, source_target_pairs={{0,1},{1,2},{2,3},{3,0},{4,5},{5,6},{6,7},{7,4},{8,9},{9,10},{10,1... | collective-permute-start | bytes 983048 | tf_op jit(solution)/shard_map/ppermute | solution.py:38
  70.2 33.3 %collective-permute-start.4 = (bf16[32,5120]{1,0:T(8,128)(2,1)S(1)}, bf16[32,5120]{1,0:T(8,128)(2,1)S(1)}, u32[]{:S(2)}, u32[]{:S(2)}) collective-permute-start(bf16[32,5120]{1,0:T(8,128)(2,1)S(1)} %get-tuple-element.33), channel_id=1, source_target_pairs={{0,3},{1,0},{2,1},{3,2},{4,7},{5,4},{6,5},{7,6},{8,11},{9,8},{10,9... | collective-permute-start | bytes 983048 | tf_op jit(solution)/shard_map/ppermute | solution.py:38
  70.4 31.4 %collective-permute-start.5 = (bf16[32,5120]{1,0:T(8,128)(2,1)S(1)}, bf16[32,5120]{1,0:T(8,128)(2,1)S(1)}, u32[]{:S(2)}, u32[]{:S(2)}) collective-permute-start(bf16[32,5120]{1,0:T(8,128)(2,1)S(1)} %get-tuple-element.35), channel_id=1, source_target_pairs={{0,3},{1,0},{2,1},{3,2},{4,7},{5,4},{6,5},{7,6},{8,11},{9,8},{10,9... | collective-permute-start | bytes 983048 | tf_op jit(solution)/shard_map/ppermute | solution.py:38
  83.7 28.5 %collective-permute-start.2 = (bf16[32,5120]{1,0:T(8,128)(2,1)S(1)}, bf16[32,5120]{1,0:T(8,128)(2,1)S(1)}, u32[]{:S(2)}, u32[]{:S(2)}) collective-permute-start(bf16[32,5120]{1,0:T(8,128)(2,1)S(1)} %add_convert_fusion.2), channel_id=1, source_target_pairs={{0,1},{1,2},{2,3},{3,0},{4,5},{5,6},{6,7},{7,4},{8,9},{9,10},{10,1... | collective-permute-start | bytes 983048 | tf_op jit(solution)/shard_map/ppermute | solution.py:38
  101.9 12.1 %collective-permute-start.6 = (bf16[32,5120]{1,0:T(8,128)(2,1)S(1)}, bf16[32,5120]{1,0:T(8,128)(2,1)S(1)}, u32[]{:S(2)}, u32[]{:S(2)}) collective-permute-start(bf16[32,5120]{1,0:T(8,128)(2,1)S(1)} %add_convert_fusion.1), channel_id=1, source_target_pairs={{0,3},{1,0},{2,1},{3,2},{4,7},{5,4},{6,5},{7,6},{8,11},{9,8},{10,9... | collective-permute-start | bytes 983048 | tf_op jit(solution)/shard_map/ppermute | solution.py:38
  116.0 44.1 %copy-start = (bf16[64,5120]{1,0:T(8,128)(2,1)}, bf16[64,5120]{1,0:T(8,128)(2,1)S(1)}, u32[]{:S(2)}) copy-start(bf16[64,5120]{1,0:T(8,128)(2,1)S(1)} %fusion.8.refs_0_) | copy-start | bytes 1966084
  116.0 37.9 %copy-start.4 = (bf16[256,640]{1,0:T(8,128)(2,1)S(1)}, bf16[256,640]{1,0:T(8,128)(2,1)}, u32[]{:S(2)}) copy-start(bf16[256,640]{1,0:T(8,128)(2,1)} %copy.36.att_ref.refs_7_) | copy-start | bytes 983044
  116.0 4.1 %collective-permute-start.11 = (f32[40,128]{1,0:T(8,128)S(1)}, f32[40,128]{1,0:T(8,128)S(1)}, u32[]{:S(2)}, u32[]{:S(2)}) collective-permute-start(f32[40,128]{1,0:T(8,128)S(1)} %bitcast.52), channel_id=1, source_target_pairs={{0,8},{4,12},{8,0},{12,4},{16,24},{20,28},{24,16},{28,20},{32,40},... | collective-permute-start | bytes 61448 | tf_op jit(solution)/shard_map/ppermute | solution.py:34
  116.5 10.5 %collective-permute-start.9 = (bf16[32,5120]{1,0:T(8,128)(2,1)S(1)}, bf16[32,5120]{1,0:T(8,128)(2,1)S(1)}, u32[]{:S(2)}, u32[]{:S(2)}) collective-permute-start(bf16[32,5120]{1,0:T(8,128)(2,1)S(1)} %get-tuple-element.64), channel_id=1, source_target_pairs={{0,1},{1,2},{2,3},{3,0},{4,5},{5,6},{6,7},{7,4},{8,9},{9,10},{10,1... | collective-permute-start | bytes 983048 | tf_op jit(solution)/shard_map/ppermute | solution.py:38
  117.2 15.8 %collective-permute-start.10 = (bf16[32,5120]{1,0:T(8,128)(2,1)S(1)}, bf16[32,5120]{1,0:T(8,128)(2,1)S(1)}, u32[]{:S(2)}, u32[]{:S(2)}) collective-permute-start(bf16[32,5120]{1,0:T(8,128)(2,1)S(1)} %get-tuple-element.65), channel_id=1, source_target_pairs={{0,3},{1,0},{2,1},{3,2},{4,7},{5,4},{6,5},{7,6},{8,11},{9,8},{10,9... | collective-permute-start | bytes 983048 | tf_op jit(solution)/shard_map/ppermute | solution.py:38
  120.2 4.7 %collective-permute-start.12 = (f32[40,128]{1,0:T(8,128)S(1)}, f32[40,128]{1,0:T(8,128)S(1)}, u32[]{:S(2)}, u32[]{:S(2)}) collective-permute-start(f32[40,128]{1,0:T(8,128)S(1)} %bitcast_add_fusion), channel_id=1, source_target_pairs={{0,16},{4,20},{8,24},{12,28},{16,0},{20,4},{24,8},{28,12},{32,48},... | collective-permute-start | bytes 61448 | tf_op jit(solution)/shard_map/ppermute | solution.py:34
  122.0 21.0 %collective-permute-start.8 = (bf16[32,5120]{1,0:T(8,128)(2,1)S(1)}, bf16[32,5120]{1,0:T(8,128)(2,1)S(1)}, u32[]{:S(2)}, u32[]{:S(2)}) collective-permute-start(bf16[32,5120]{1,0:T(8,128)(2,1)S(1)} %get-tuple-element.64), channel_id=1, source_target_pairs={{0,3},{1,0},{2,1},{3,2},{4,7},{5,4},{6,5},{7,6},{8,11},{9,8},{10,9... | collective-permute-start | bytes 983048 | tf_op jit(solution)/shard_map/ppermute | solution.py:38
  124.3 18.8 %collective-permute-start.7 = (bf16[32,5120]{1,0:T(8,128)(2,1)S(1)}, bf16[32,5120]{1,0:T(8,128)(2,1)S(1)}, u32[]{:S(2)}, u32[]{:S(2)}) collective-permute-start(bf16[32,5120]{1,0:T(8,128)(2,1)S(1)} %get-tuple-element.65), channel_id=1, source_target_pairs={{0,1},{1,2},{2,3},{3,0},{4,5},{5,6},{6,7},{7,4},{8,9},{9,10},{10,1... | collective-permute-start | bytes 983048 | tf_op jit(solution)/shard_map/ppermute | solution.py:38
  133.1 19.9 %collective-permute-start.16 = (bf16[32,5120]{1,0:T(8,128)(2,1)S(1)}, bf16[32,5120]{1,0:T(8,128)(2,1)S(1)}, u32[]{:S(2)}, u32[]{:S(2)}) collective-permute-start(bf16[32,5120]{1,0:T(8,128)(2,1)S(1)} %collective-permute-done.10.refs_2_), channel_id=1, source_target_pairs={{0,3},{1,0},{2,1},{3,2},{4,7},{5,4},{6,5},{7,6},{8,11},{9,8},{10,9... | collective-permute-start | bytes 983048 | tf_op jit(solution)/shard_map/ppermute | solution.py:38
  133.1 20.9 %collective-permute-start.15 = (bf16[32,5120]{1,0:T(8,128)(2,1)S(1)}, bf16[32,5120]{1,0:T(8,128)(2,1)S(1)}, u32[]{:S(2)}, u32[]{:S(2)}) collective-permute-start(bf16[32,5120]{1,0:T(8,128)(2,1)S(1)} %collective-permute-done.9.refs_5_), channel_id=1, source_target_pairs={{0,1},{1,2},{2,3},{3,0},{4,5},{5,6},{6,7},{7,4},{8,9},{9,10},{10,1... | collective-permute-start | bytes 983048 | tf_op jit(solution)/shard_map/ppermute | solution.py:38
  135.4 2.9 %collective-permute-start.13 = (f32[40,128]{1,0:T(8,128)S(1)}, f32[40,128]{1,0:T(8,128)S(1)}, u32[]{:S(2)}, u32[]{:S(2)}) collective-permute-start(f32[40,128]{1,0:T(8,128)S(1)} %fusion.31), channel_id=1, source_target_pairs={{0,64},{4,68},{8,72},{12,76},{16,80},{20,84},{24,88},{28,92},{32,9... | collective-permute-start | bytes 61448 | tf_op jit(solution)/shard_map/ppermute | solution.py:34
  138.4 4.1 %collective-permute-start.14 = (f32[40,128]{1,0:T(8,128)S(1)}, f32[40,128]{1,0:T(8,128)S(1)}, u32[]{:S(2)}, u32[]{:S(2)}) collective-permute-start(f32[40,128]{1,0:T(8,128)S(1)} %add.96), channel_id=1, source_target_pairs={{0,128},{4,132},{8,136},{12,140},{16,144},{20,148},{24,152},{28,15... | collective-permute-start | bytes 61448 | tf_op jit(solution)/shard_map/ppermute | solution.py:34
  157.7 9.0 %collective-permute-start.17 = (bf16[4,4,2,80,640]{4,3,2,1,0:T(8,128)(2,1)S(1)}, bf16[4,4,2,80,640]{4,3,2,1,0:T(8,128)(2,1)S(1)}, u32[]{:S(2)}, u32[]{:S(2)}) collective-permute-start(bf16[4,4,2,80,640]{4,3,2,1,0:T(8,128)(2,1)S(1)} %get-tuple-element.41), channel_id=1, source_target_pairs={{0,4},{4,0},{8,12},{12,8},{16,20},{20,16},{24,28},{28,24},{32,36},... | collective-permute-start | bytes 9830408 | tf_op jit(solution)/shard_map/ppermute | solution.py:34
  169.2 30.4 %all-to-all-start.2 = ((bf16[4,4,2,80,640]{4,3,2,1,0:T(8,128)(2,1)}), bf16[4,4,2,80,640]{4,3,2,1,0:T(8,128)(2,1)S(1)}, u32[]{:S(2)}, u32[]{:S(2)}) async-start(bf16[4,4,2,80,640]{4,3,2,1,0:T(8,128)(2,1)} %add_convert_fusion), calls=%async_computation.2 | async-start | bytes 6553600 | tf_op jit(solution)/shard_map/all_to_all | solution.py:42
  175.9 1.2 collective-permute-start.18
  177.1 9.7 %collective-permute-start.19 = (f32[40,128]{1,0:T(8,128)S(1)}, f32[40,128]{1,0:T(8,128)S(1)}, u32[]{:S(2)}, u32[]{:S(2)}) collective-permute-start(f32[40,128]{1,0:T(8,128)S(1)} %add.99), channel_id=1, source_target_pairs={{0,32},{4,36},{8,40},{12,44},{16,48},{20,52},{24,56},{28,60},{32,0... | collective-permute-start | bytes 61448 | tf_op jit(solution)/shard_map/ppermute | solution.py:34
  186.8 4.4 %collective-permute-start.20 = (f32[40,128]{1,0:T(8,128)S(1)}, f32[40,128]{1,0:T(8,128)S(1)}, u32[]{:S(2)}, u32[]{:S(2)}) collective-permute-start(f32[40,128]{1,0:T(8,128)S(1)} %add.100), channel_id=1, source_target_pairs={{0,1},{1,0},{2,3},{3,2},{4,5},{5,4},{6,7},{7,6},{8,9},{9,8},{10,11... | collective-permute-start | bytes 61448 | tf_op jit(solution)/shard_map/ppermute | solution.py:336
  191.2 6.5 %collective-permute-start.21 = (f32[40,128]{1,0:T(8,128)S(1)}, f32[40,128]{1,0:T(8,128)S(1)}, u32[]{:S(2)}, u32[]{:S(2)}) collective-permute-start(f32[40,128]{1,0:T(8,128)S(1)} %add.101), channel_id=1, source_target_pairs={{0,2},{1,3},{2,0},{3,1},{4,6},{5,7},{6,4},{7,5},{8,10},{9,11},{10,... | collective-permute-start | bytes 61448 | tf_op jit(solution)/shard_map/ppermute | solution.py:336
  201.4 8.4 %copy-start.6 = (f32[5,256,256]{1,2,0:T(8,128)S(1)}, f32[5,256,256]{1,2,0:T(8,128)}, u32[]{:S(2)}) copy-start(f32[5,256,256]{1,2,0:T(8,128)} %get-tuple-element.67) | copy-start | bytes 3932164
  201.4 8.4 %copy-start.11 = (bf16[256,640]{0,1:T(8,128)(2,1)S(1)}, bf16[256,640]{0,1:T(8,128)(2,1)}, u32[]{:S(2)}) copy-start(bf16[256,640]{0,1:T(8,128)(2,1)} %copy.38) | copy-start | bytes 983044
  201.4 21.3 %all-to-all-start.3 = ((bf16[8,80,640]{2,1,0:T(8,128)(2,1)}), bf16[8,80,640]{2,1,0:T(8,128)(2,1)S(1)}, u32[]{:S(2)}, u32[]{:S(2)}) async-start(bf16[8,80,640]{2,1,0:T(8,128)(2,1)} %bitcast.38), calls=%async_computation.3 | async-start | bytes 1638400 | tf_op jit(solution)/shard_map/all_to_all | solution.py:42
  209.8 1.3 copy-start.10
  (7 other events, 6.9 us)
